TPU v7x, 32 devices: a whole 2x2x4 slice. The times are simulated.
32 devices in a mesh: pipe: 2 (over y), dp: 8 (over z, x), tensor: 2 (over core).
Axes of the slice: x: 2, y: 2, z: 4, core: 2. Of those that a mesh axis runs over, the one named last changes fastest.
Arguments:
- inputs: bfloat16 [2, 1536, 768], P(None, ('dp', 'tensor')), may hold values from -6 to 6
- lengths: int32 [2, 8, 3], P(None, 'dp'), may hold values from 1 to 144, 192 in all within a row
- ln1_gain: bfloat16 [2, 768], P('pipe', 'dp'), may hold values from 0.25 to 1.75
- ln1_shift: bfloat16 [2, 768], P('pipe', 'dp'), may hold values from -1.5 to 1.5
- ln2_gain: bfloat16 [2, 768], P('pipe', 'dp'), may hold values from 0.25 to 1.75
- ln2_shift: bfloat16 [2, 768], P('pipe', 'dp'), may hold values from -1.5 to 1.5
- qkv_weight: bfloat16 [2, 768, 2304], P('pipe', 'dp', 'tensor'), may hold values from -0.21875 to 0.21875
- qkv_bias: bfloat16 [2, 2304], P('pipe', 'tensor'), may hold values from -2.5 to 2.5
- out_weight: bfloat16 [2, 768, 768], P('pipe', 'tensor', 'dp'), may hold values from -1 to 1
- fc_weight: bfloat16 [2, 768, 3072], P('pipe', 'dp', 'tensor'), may hold values from -0.21875 to 0.21875
- fc_bias: bfloat16 [2, 3072], P('pipe', 'tensor'), may hold values from -2.5 to 2.5
- proj_weight: bfloat16 [2, 3072, 768], P('pipe', 'tensor', 'dp'), may hold values from -0.109375 to 0.109375
- branch_bias: bfloat16 [2, 768], P('pipe', 'dp'), may hold values from -1.5 to 1.5
- cotangent: bfloat16 [2, 1536, 768], P(None, ('dp', 'tensor')), may hold values from -6 to 6
Outputs:
- activations: bfloat16 [2, 2, 1536, 768], P('pipe', None, ('dp', 'tensor'))
- input_grads: bfloat16 [2, 2, 1536, 768], P('pipe', None, ('dp', 'tensor'))
- ln1_gain_grad: float32 [2, 768], P('pipe', 'dp')
- ln1_shift_grad: float32 [2, 768], P('pipe', 'dp')
- ln2_gain_grad: float32 [2, 768], P('pipe', 'dp')
- ln2_shift_grad: float32 [2, 768], P('pipe', 'dp')
- qkv_weight_grad: float32 [2, 768, 2304], P('pipe', 'dp', 'tensor')
- qkv_bias_grad: float32 [2, 2304], P('pipe', 'tensor')
- out_weight_grad: float32 [2, 768, 768], P('pipe', 'tensor', 'dp')
- fc_weight_grad: float32 [2, 768, 3072], P('pipe', 'dp', 'tensor')
- fc_bias_grad: float32 [2, 3072], P('pipe', 'tensor')
- proj_weight_grad: float32 [2, 3072, 768], P('pipe', 'tensor', 'dp')
- branch_bias_grad: float32 [2, 768], P('pipe', 'dp')
Inputs may be any that keep to these rules, and one draw needn't show every extreme that they name: Each row holds, in order, the lengths of the 3 sequences that fill one group's 192 rows of a micro-batch; they sum to 192, and the longest of each row is exactly 144.
All inputs are finite; a program needn't handle non-finite values.
Results may differ from a plain program's by a relative error of at most 0.017.
Values may be sent and summed in bfloat16 or wider, within the bound.
No kernel may reach another device: no remote copies, remote signals or barrier semaphores. Data moves between devices by JAX's collectives and lax.ppermute only.
A program may use at most 128 MiB of HBM per device.

v0:
```python
import math

import jax
import jax.numpy as jnp
from jax import lax
from jax.sharding import PartitionSpec as P

HEAD = 64
ROT = 16


EPSILON = 1e-05
NEG_BIG = -1e30


def shifted(block, axis, distance):
    devices = range(lax.axis_size(axis))
    route = [(i - distance, i) for i in devices if i - distance in devices]
    return lax.ppermute(block, axis, route)


def layer_norm(values, gain, offset):
    average = jnp.mean(values, axis=-1, keepdims=True)
    centred = values - average
    spread = jnp.mean(centred * centred, axis=-1, keepdims=True)
    return centred * lax.rsqrt(spread + EPSILON) * gain + offset


def both_norms(values, gain_one, shift_one, gain_two, shift_two):
    return (layer_norm(values, gain_one, shift_one), layer_norm(values, gain_two, shift_two))


def exact_gelu(values):
    return jax.nn.gelu(values, approximate=False)


def sequence_layout(seq_lengths, row_count, seq_count):
    seq_ends = jnp.cumsum(seq_lengths)
    places = jnp.arange(row_count, dtype=jnp.int32)
    segment = jnp.sum((places[:, None] >= seq_ends[None, :]).astype(jnp.int32), axis=1)
    seq_starts = seq_ends - seq_lengths
    picked = segment[:, None] == jnp.arange(seq_count, dtype=jnp.int32)[None, :]
    first_row = jnp.sum(jnp.where(picked, seq_starts[None, :], 0), axis=1)
    return (segment, places - first_row)


def rotary_tables(positions, rot_dims):
    half_dims = rot_dims // 2
    counter = jnp.arange(half_dims, dtype=jnp.float32)
    inverse = jnp.exp(counter * (-2.0 * math.log(10000.0) / rot_dims))
    angles = positions.astype(jnp.float32)[..., None] * inverse
    angles = jnp.concatenate([angles, angles], axis=-1)
    return (jnp.cos(angles), jnp.sin(angles))


def apply_rotary(heads, cosine, sine):
    rot_dims = cosine.shape[-1]
    half_dims = rot_dims // 2
    front = heads[..., :rot_dims]
    turned = jnp.concatenate([-front[..., half_dims:], front[..., :half_dims]], axis=-1)
    front = front * cosine[..., None, :] + turned * sine[..., None, :]
    return jnp.concatenate([front, heads[..., rot_dims:]], axis=-1)


def rotate_back(grads, cosine, sine):

    def turn(heads):
        return apply_rotary(heads, cosine, sine)

    return jax.vjp(turn, grads)[1](grads)[0]


def attention_mask(segment):
    row_ids = jnp.arange(segment.shape[0], dtype=jnp.int32)
    return (segment[:, None] == segment[None, :]) & (row_ids[:, None] >= row_ids[None, :])


def score_block(queries, key_rows, allowed):
    scores = jnp.einsum("qhd,khd->hqk", queries, key_rows, preferred_element_type=jnp.float32)
    scores = scores * (1.0 / math.sqrt(queries.shape[-1]))
    return jnp.where(allowed[None], scores, NEG_BIG)


def times_transposed(left, right):
    return lax.dot_general(
        left, right, (((1,), (1,)), ((), ())), preferred_element_type=jnp.float32
    )


def contract_rows(left, right):
    return lax.dot_general(
        left, right, (((0,), (0,)), ((), ())), preferred_element_type=jnp.float32
    )


def choose(leading, when_first, otherwise):

    def pick(first_item, other_item):
        return jnp.where(leading, first_item, other_item)

    return jax.tree.map(pick, when_first, otherwise)


def unpack(fetched, qkv_bias, fc_bias):
    vectors, qkv_matrix, out_matrix, fc_matrix, proj_matrix = fetched
    return (
        vectors,
        qkv_matrix[0],
        out_matrix[0],
        fc_matrix[0],
        proj_matrix[0],
        qkv_bias[0],
        fc_bias[0],
    )


def layer_forward(hidden_own, segment, cosine, sine, weights):
    vectors, qkv_matrix, out_matrix, fc_matrix, proj_matrix, qkv_offset, fc_offset = weights
    gathered = lax.all_gather(hidden_own, "tensor", axis=0, tiled=True)
    widened = gathered.astype(jnp.float32)
    vector_f = vectors.astype(jnp.float32)
    first = layer_norm(widened, vector_f[0], vector_f[1]).astype(jnp.bfloat16)
    second = layer_norm(widened, vector_f[2], vector_f[3]).astype(jnp.bfloat16)
    packed = jnp.dot(first, qkv_matrix, preferred_element_type=jnp.float32) + qkv_offset.astype(
        jnp.float32
    )
    row_count = packed.shape[0]
    packed = packed.reshape(row_count, -1, 3, HEAD)
    queries = apply_rotary(packed[:, :, 0], cosine, sine).astype(jnp.bfloat16)
    key_rows = apply_rotary(packed[:, :, 1], cosine, sine).astype(jnp.bfloat16)
    value_rows = packed[:, :, 2].astype(jnp.bfloat16)
    allowed = attention_mask(segment)
    scores = score_block(queries, key_rows, allowed)
    row_peak = jnp.max(scores, axis=-1, keepdims=True)
    expons = jnp.exp(scores - row_peak)
    totals = jnp.sum(expons, axis=-1, keepdims=True)
    attn_weights = (expons / totals).astype(jnp.bfloat16)
    log_total = row_peak + jnp.log(totals)
    mixed = jnp.einsum("hqk,khd->qhd", attn_weights, value_rows, preferred_element_type=jnp.float32)
    mixed = mixed.reshape(row_count, -1).astype(jnp.bfloat16)
    pre_act = jnp.dot(second, fc_matrix, preferred_element_type=jnp.float32) + fc_offset.astype(
        jnp.float32
    )
    hidden_act = exact_gelu(pre_act).astype(jnp.bfloat16)
    branches = jnp.dot(mixed, out_matrix, preferred_element_type=jnp.float32)
    branches = branches + jnp.dot(hidden_act, proj_matrix, preferred_element_type=jnp.float32)
    summed = lax.psum_scatter(branches, "tensor", scatter_dimension=0, tiled=True)
    result = hidden_own.astype(jnp.float32) + summed + vector_f[4]
    kept_values = (
        gathered,
        first,
        second,
        queries,
        key_rows,
        value_rows,
        log_total,
        mixed,
        pre_act,
    )
    return (result, kept_values)


def layer_backward(grad_own, kept_values, segment, cosine, sine, weights):
    vectors, qkv_matrix, out_matrix, fc_matrix, proj_matrix, qkv_offset, fc_offset = weights
    gathered, first, second, queries, key_rows, value_rows, log_total, mixed, pre_act = kept_values
    grad_wide = lax.all_gather(grad_own, "tensor", axis=0, tiled=True)
    row_count = grad_wide.shape[0]
    hidden_act = exact_gelu(pre_act).astype(jnp.bfloat16)
    out_grad = contract_rows(mixed, grad_wide)
    proj_grad = contract_rows(hidden_act, grad_wide)
    d_mixed = times_transposed(grad_wide, out_matrix).astype(jnp.bfloat16)
    d_act = times_transposed(grad_wide, proj_matrix)
    d_pre = jax.vjp(exact_gelu, pre_act)[1](d_act)[0].astype(jnp.bfloat16)
    fc_grad = contract_rows(second, d_pre)
    fc_bias_grad = jnp.sum(d_pre.astype(jnp.float32), axis=0)
    d_second = times_transposed(d_pre, fc_matrix)
    heads_local = queries.shape[1]
    d_heads = d_mixed.reshape(row_count, heads_local, -1)
    allowed = attention_mask(segment)
    scores = score_block(queries, key_rows, allowed)
    attn_full = jnp.where(allowed[None], jnp.exp(scores - log_total), 0.0)
    attn_weights = attn_full.astype(jnp.bfloat16)
    d_values = jnp.einsum("hqk,qhd->khd", attn_weights, d_heads, preferred_element_type=jnp.float32)
    d_attn = jnp.einsum("qhd,khd->hqk", d_heads, value_rows, preferred_element_type=jnp.float32)
    row_dot = jnp.sum(attn_full * d_attn, axis=-1, keepdims=True)
    d_scores = (attn_full * (d_attn - row_dot)).astype(jnp.bfloat16)
    scaling = 1.0 / math.sqrt(queries.shape[-1])
    d_queries = (
        jnp.einsum("hqk,khd->qhd", d_scores, key_rows, preferred_element_type=jnp.float32) * scaling
    )
    d_keys = (
        jnp.einsum("hqk,qhd->khd", d_scores, queries, preferred_element_type=jnp.float32) * scaling
    )
    d_packed = jnp.stack(
        [rotate_back(d_queries, cosine, sine), rotate_back(d_keys, cosine, sine), d_values], axis=2
    )
    d_packed = d_packed.reshape(row_count, -1).astype(jnp.bfloat16)
    qkv_grad = contract_rows(first, d_packed)
    qkv_bias_grad = jnp.sum(d_packed.astype(jnp.float32), axis=0)
    d_first = times_transposed(d_packed, qkv_matrix)
    vector_f = vectors.astype(jnp.float32)
    pullback = jax.vjp(
        both_norms, gathered.astype(jnp.float32), vector_f[0], vector_f[1], vector_f[2], vector_f[3]
    )[1]
    d_wide, gain_grad_one, shift_grad_one, gain_grad_two, shift_grad_two = pullback(
        (d_first, d_second)
    )
    d_rows = lax.psum_scatter(
        d_wide.astype(jnp.bfloat16), "tensor", scatter_dimension=0, tiled=True
    ).astype(jnp.float32)
    d_hidden = grad_own.astype(jnp.float32) + d_rows
    vector_grads = jnp.stack(
        [
            gain_grad_one,
            shift_grad_one,
            gain_grad_two,
            shift_grad_two,
            jnp.sum(grad_own.astype(jnp.float32), axis=0),
        ]
    )
    return (
        d_hidden,
        (vector_grads, qkv_grad, out_grad, fc_grad, proj_grad, qkv_bias_grad, fc_bias_grad),
    )


def local(
    inputs,
    lengths,
    ln1_gain,
    ln1_shift,
    ln2_gain,
    ln2_shift,
    qkv_weight,
    qkv_bias,
    out_weight,
    fc_weight,
    fc_bias,
    proj_weight,
    branch_bias,
    cotangent,
):
    micro_count = inputs.shape[0]
    group_rows = inputs.shape[1] * lax.axis_size("tensor")
    seq_count = lengths.shape[2]
    layouts = []
    for index in range(micro_count):
        segment, positions = sequence_layout(lengths[index, 0], group_rows, seq_count)
        cosine, sine = rotary_tables(positions, ROT)
        layouts.append((segment, cosine, sine))
    section_id = lax.axis_index("pipe")
    leading = section_id == 0
    vectors = jnp.concatenate([ln1_gain, ln1_shift, ln2_gain, ln2_shift, branch_bias], axis=0)
    fetched = (
        lax.all_gather(vectors, "dp", axis=1, tiled=True),
        lax.all_gather(qkv_weight, "dp", axis=1, tiled=True),
        lax.all_gather(out_weight, "dp", axis=2, tiled=True),
        lax.all_gather(fc_weight, "dp", axis=1, tiled=True),
        lax.all_gather(proj_weight, "dp", axis=2, tiled=True),
    )
    weights = unpack(fetched, qkv_bias, fc_bias)
    received = jnp.zeros_like(inputs[0])
    results = []
    stored = []
    for moment in range(micro_count + 1):
        layout = choose(leading, layouts[min(moment, micro_count - 1)], layouts[max(moment - 1, 0)])
        section_input = jnp.where(leading, inputs[min(moment, micro_count - 1)], received)
        result, kept_values = layer_forward(section_input, layout[0], layout[1], layout[2], weights)
        low_result = result.astype(jnp.bfloat16)
        results.append(low_result)
        stored.append((layout, kept_values))
        if moment < micro_count:
            received = shifted(low_result, "pipe", 1)
    refetched = (
        lax.all_gather(vectors, "dp", axis=1, tiled=True),
        lax.all_gather(qkv_weight, "dp", axis=1, tiled=True),
        lax.all_gather(out_weight, "dp", axis=2, tiled=True),
        lax.all_gather(fc_weight, "dp", axis=1, tiled=True),
        lax.all_gather(proj_weight, "dp", axis=2, tiled=True),
    )
    back_weights = unpack(refetched, qkv_bias, fc_bias)
    totals = None
    received = jnp.zeros_like(cotangent[0])
    back_rows = []
    for moment in range(micro_count + 1):
        live = jnp.where(leading, moment >= 1, moment < micro_count).astype(jnp.float32)
        layout, kept_values = choose(
            leading, stored[max(moment - 1, 0)], stored[min(moment + 1, micro_count)]
        )
        grad_own = jnp.where(leading, received, cotangent[min(moment, micro_count - 1)])
        d_hidden, step_grads = layer_backward(
            grad_own, kept_values, layout[0], layout[1], layout[2], back_weights
        )
        step_grads = tuple((item * live for item in step_grads))
        if totals is None:
            totals = step_grads
        else:
            totals = tuple((older + newer for older, newer in zip(totals, step_grads)))
        low_grad = d_hidden.astype(jnp.bfloat16)
        back_rows.append(low_grad)
        if moment < micro_count:
            received = shifted(low_grad, "pipe", -1)
    reduced = (
        lax.psum_scatter(
            totals[0].astype(jnp.bfloat16), "dp", scatter_dimension=1, tiled=True
        ).astype(jnp.float32),
        lax.psum_scatter(
            totals[1].astype(jnp.bfloat16), "dp", scatter_dimension=0, tiled=True
        ).astype(jnp.float32),
        lax.psum_scatter(
            totals[2].astype(jnp.bfloat16), "dp", scatter_dimension=1, tiled=True
        ).astype(jnp.float32),
        lax.psum_scatter(
            totals[3].astype(jnp.bfloat16), "dp", scatter_dimension=0, tiled=True
        ).astype(jnp.float32),
        lax.psum_scatter(
            totals[4].astype(jnp.bfloat16), "dp", scatter_dimension=1, tiled=True
        ).astype(jnp.float32),
    )
    vector_grads = lax.psum(reduced[0], "tensor")
    bias_grads = lax.psum((totals[5], totals[6]), "dp")
    activations = jnp.stack(
        [choose(leading, results[index], results[index + 1]) for index in range(micro_count)]
    )[None]
    input_grads = jnp.stack(
        [choose(leading, back_rows[index + 1], back_rows[index]) for index in range(micro_count)]
    )[None]
    return (
        activations,
        input_grads,
        vector_grads[0][None],
        vector_grads[1][None],
        vector_grads[2][None],
        vector_grads[3][None],
        reduced[1][None],
        bias_grads[0][None],
        reduced[2][None],
        reduced[3][None],
        bias_grads[1][None],
        reduced[4][None],
        vector_grads[4][None],
    )


def solution(mesh):
    placed = (
        P(None, ("dp", "tensor"), None),
        P(None, "dp", None),
        P("pipe", "dp"),
        P("pipe", "dp"),
        P("pipe", "dp"),
        P("pipe", "dp"),
        P("pipe", "dp", "tensor"),
        P("pipe", "tensor"),
        P("pipe", "tensor", "dp"),
        P("pipe", "dp", "tensor"),
        P("pipe", "tensor"),
        P("pipe", "tensor", "dp"),
        P("pipe", "dp"),
        P(None, ("dp", "tensor"), None),
    )
    return jax.shard_map(
        local,
        mesh=mesh,
        in_specs=placed,
        out_specs=(
            P("pipe", None, ("dp", "tensor"), None),
            P("pipe", None, ("dp", "tensor"), None),
            P("pipe", "dp"),
            P("pipe", "dp"),
            P("pipe", "dp"),
            P("pipe", "dp"),
            P("pipe", "dp", "tensor"),
            P("pipe", "tensor"),
            P("pipe", "tensor", "dp"),
            P("pipe", "dp", "tensor"),
            P("pipe", "tensor"),
            P("pipe", "tensor", "dp"),
            P("pipe", "dp"),
        ),
        check_vma=False,
    )
```

profile of v0, /device:TPU:0, one launch (start us, length us, event | category | flops | bytes accessed | tf_op | source)
XLA Modules:
  0.0 697.2 jit_solution(2812464461734134929)
XLA Ops:
  13.9 27.9 %all-gather.2 = bf16[8,96,5]{1,2,0:T(8,128)(2,1)S(1)} all-gather(bf16[1,96,5]{1,2,0:T(8,128)(2,1)S(1)} %bitcast.362), channel_id=1, replica_groups=mesh['pipe'=2,'dp'=8,'tensor'=2] {'dp'}, dimensions={0}, use_global_device_ids=true | all-gather | bytes 8640 | tf_op jit(solution)/shard_map/all_gather | solution.py:255
  42.5 2.0 all-gather
  46.2 32.0 %all_gather.41 = bf16[1,384,768]{1,2,0:T(8,128)(2,1)S(1)} all-gather(bf16[1,384,96]{1,2,0:T(8,128)(2,1)S(1)} %copy-done.93), channel_id=1, replica_groups=mesh['pipe'=2,'dp'=8,'tensor'=2] {'dp'}, dimensions={2}, use_global_device_ids=true | all-gather | bytes 663552 | tf_op jit(solution)/shard_map/all_gather | solution.py:257
  78.2 2.1 convolution_add_fusion.3
  83.5 32.2 %all-gather.9.cloned.1.call-done = bf16[1,768,1536]{2,1,0:T(8,128)(2,1)} async-done(((bf16[1,96,1536]{2,1,0:T(8,128)(2,1)}), bf16[1,768,1536]{2,1,0:T(8,128)(2,1)}) %all-gather.9.cloned.1.call-update) | async-done | bytes 2359312 | tf_op jit(solution)/shard_map/all_gather | solution.py:258
  115.7 2.4 convolution_add_fusion.6
  118.1 50.4 %all-gather.11.cloned.1.call-done = bf16[1,1536,768]{1,2,0:T(8,128)(2,1)} async-done(((bf16[1,1536,96]{1,2,0:T(8,128)(2,1)}), bf16[1,1536,768]{1,2,0:T(8,128)(2,1)}) %all-gather.11.cloned.1.call-update) | async-done | bytes 2359312 | tf_op jit(solution)/shard_map/all_gather | solution.py:259
  168.5 5.6 fusion.49
  174.9 2.0 all-gather.1
  179.3 1.6 reduce-scatter.14.cloned.1.call-done
  181.9 3.6 collective-permute-start
  185.6 1.5 fusion.330
  187.1 2.0 collective-permute-done
  189.8 2.2 all_gather.44
  192.4 1.6 convolution_add_fusion.2
  194.1 2.6 copy.186
  199.4 1.5 convolution_convert_fusion.1
  203.9 4.0 fusion.52
  211.0 6.7 convert_reduce_fusion.2
  218.0 1.8 select_bitcast_fusion.1
  219.8 4.2 collective-permute-start.1
  223.9 2.5 fusion.328
  227.4 2.4 all_gather.45
  229.9 1.8 convert_reduce_fusion.6
  232.3 1.6 convolution_add_fusion.1
  233.8 2.6 copy.191
  246.0 1.6 fusion.491
  249.9 2.8 broadcast_select_fusion.5
  256.3 1.7 convolution_add_fusion.4
  258.0 1.6 reduce-scatter.20.cloned.1.call-done
  260.6 1.3 collective-permute-start.2
  263.2 5.3 collective-permute-done.2
  268.4 1.6 convert_reduce_fusion.14
  270.6 2.4 all_gather.47
  274.8 1.7 copy.201
  276.5 1.7 fusion.326
  284.4 4.0 convert_reduce_fusion.1
  288.4 1.6 fusion.493
  292.3 6.1 fusion.55
  298.4 1.3 stack.103
  300.4 1.8 select_bitcast_fusion
  311.1 1.3 stack.105
  312.4 1.6 convert_reduce_fusion.13
  314.1 2.2 all_gather.48
  319.1 1.6 fusion.324
  326.7 4.0 convert_reduce_fusion
  331.5 1.3 copy-done.185
  335.6 2.2 add_convert_fusion.5
  340.8 1.7 convolution_multiply_fusion.1
  343.6 2.3 fusion.1
  349.1 2.5 add_convert_fusion.1
  353.2 3.4 fusion.190
  356.7 3.4 fusion.191
  360.1 4.8 add_convert_fusion
  367.8 37.4 %all-reduce.24 = (f32[1,1152]{1,0:T(1,128)}, f32[1,1536]{1,0:T(1,128)}) all-reduce(f32[1,1152]{1,0:T(1,128)S(1)} %broadcast_in_dim.283, f32[1,1536]{1,0:T(1,128)S(1)} %broadcast_in_dim.288), channel_id=1, replica_groups=mesh['pipe'=2,'dp'=8,'tensor'=2] {'dp'}, use_global_device_ids=true, to_apply=%region_66.67 | all-reduce | flops 2688 | bytes 21504 | tf_op jit(solution)/shard_map/psum | solution.py:321
  406.0 2.5 psum.21
  410.9 65.2 %reduce-scatter.28.cloned.1.call-done = bf16[384,96]{0,1:T(8,128)(2,1)} async-done(((bf16[384,768]{0,1:T(8,128)(2,1)}), bf16[384,96]{0,1:T(8,128)(2,1)}) %reduce-scatter.28.cloned.1.call-update) | async-done | bytes 73744 | tf_op jit(solution)/shard_map/reduce_scatter | solution.py:310
  476.1 1.6 bitcast_convert_fusion.3
  477.7 67.0 %reduce-scatter.26.cloned.1.call-done = bf16[96,1152]{1,0:T(8,128)(2,1)} async-done(((bf16[768,1152]{1,0:T(8,128)(2,1)}), bf16[96,1152]{1,0:T(8,128)(2,1)}) %reduce-scatter.26.cloned.1.call-update) | async-done | bytes 221200 | tf_op jit(solution)/shard_map/reduce_scatter | solution.py:307
  544.6 1.7 bitcast_convert_fusion.2
  546.4 70.2 %reduce-scatter.30.cloned.1.call-done = bf16[96,1536]{1,0:T(8,128)(2,1)} async-done(((bf16[768,1536]{1,0:T(8,128)(2,1)}), bf16[96,1536]{1,0:T(8,128)(2,1)}) %reduce-scatter.30.cloned.1.call-update) | async-done | bytes 294928 | tf_op jit(solution)/shard_map/reduce_scatter | solution.py:313
  616.6 1.8 bitcast_convert_fusion.1
  618.4 70.2 %reduce-scatter.32.cloned.1.call-done = bf16[1536,96]{0,1:T(8,128)(2,1)} async-done(((bf16[1536,768]{0,1:T(8,128)(2,1)}), bf16[1536,96]{0,1:T(8,128)(2,1)}) %reduce-scatter.32.cloned.1.call-update) | async-done | bytes 294928 | tf_op jit(solution)/shard_map/reduce_scatter | solution.py:316
  688.6 1.8 bitcast_convert_fusion
  (618 shorter events, 91.7 us)
Async XLA Ops:
  7.2 6.6 copy-start.51
  7.2 6.6 copy-start.176
  7.2 6.6 copy-start.177
  7.2 6.6 copy-start.178
  7.2 6.6 copy-start.179
  7.2 6.6 copy-start.180
  7.2 34.6 %copy-start.172 = (bf16[1,1536]{1,0:T(2,128)(2,1)S(1)}, bf16[1,1536]{1,0:T(2,128)(2,1)}, u32[]{:S(2)}) copy-start(bf16[1,1536]{1,0:T(2,128)(2,1)} %param.24) | copy-start | bytes 9220
  7.3 71.0 %all-gather.7.cloned.1.call-start = ((), (), s32[]{:S(2)}) async-start(), calls=%async_computation.11 | async-start | bytes 1990656 | tf_op jit(solution)/shard_map/all_gather | solution.py:256
  8.0 38.2 %copy-start.93 = (bf16[1,384,96]{1,2,0:T(8,128)(2,1)S(1)}, bf16[1,384,96]{1,2,0:T(8,128)(2,1)}, u32[]{:S(2)}) copy-start(bf16[1,384,96]{1,2,0:T(8,128)(2,1)} %param.22) | copy-start | bytes 221188
  8.0 107.7 %all-gather.9.cloned.1.call-start = ((), (), s32[]{:S(2)}) async-start(), calls=%async_computation.12 | async-start | bytes 2654208 | tf_op jit(solution)/shard_map/all_gather | solution.py:258
  8.7 159.8 %all-gather.11.cloned.1.call-start = ((), (), s32[]{:S(2)}) async-start(), calls=%async_computation.13 | async-start | bytes 2654208 | tf_op jit(solution)/shard_map/all_gather | solution.py:259
  9.5 171.4 %reduce-scatter.14.cloned.1.call-start = ((), (), s32[]{:S(2)}) async-start(), calls=%async_computation.14 | async-start | bytes 884736 | tf_op jit(solution)/shard_map/reduce_scatter | solution.py:147
  11.4 66.8 %copy-start.156 = (s32[192]{0:T(256)}, s32[192]{0:T(256)S(1)}, u32[]{:S(2)}) copy-start(s32[192]{0:T(256)S(1)} %convert_reduce_fusion.18) | copy-start | bytes 2308
  13.7 66.6 %copy-start.166 = (f32[1152]{0:T(1024)}, f32[1152]{0:T(1024)S(1)}, u32[]{:S(2)}) copy-start(f32[1152]{0:T(1024)S(1)} %convert_reduce_fusion.16) | copy-start | bytes 13828
  45.1 35.3 %copy-start.95 = (f32[768]{0:T(1024)}, f32[768]{0:T(1024)S(1)}, u32[]{:S(2)}) copy-start(f32[768]{0:T(1024)S(1)} %get-tuple-element.49) | copy-start | bytes 9220
  45.2 35.2 %copy-start.128 = (f32[192]{0:T(256)}, f32[192]{0:T(256)S(1)}, u32[]{:S(2)}) copy-start(f32[192]{0:T(256)S(1)} %broadcast_multiply_fusion.7) | copy-start | bytes 2308
  45.5 34.9 %copy-start.146 = (f32[192]{0:T(256)}, f32[192]{0:T(256)S(1)}, u32[]{:S(2)}) copy-start(f32[192]{0:T(256)S(1)} %add_rsqrt_fusion.2) | copy-start | bytes 2308
  83.1 34.9 %copy-start.88 = (bf16[6,64,192]{2,1,0:T(8,128)(2,1)}, bf16[6,64,192]{2,1,0:T(8,128)(2,1)S(1)}, u32[]{:S(2)}) copy-start(bf16[6,64,192]{2,1,0:T(8,128)(2,1)S(1)} %convolution_convert_fusion.2) | copy-start | bytes 442372
  83.1 32.6 %copy-start.110 = (f32[768]{0:T(1024)S(1)}, f32[768]{0:T(1024)}, u32[]{:S(2)}) copy-start(f32[768]{0:T(1024)} %get-tuple-element.47) | copy-start | bytes 9220
  83.2 32.6 %copy-start.129 = (f32[192]{0:T(256)S(1)}, f32[192]{0:T(256)}, u32[]{:S(2)}) copy-start(f32[192]{0:T(256)} %copy-done.128) | copy-start | bytes 2308
  83.2 32.6 %copy-start.147 = (f32[192]{0:T(256)S(1)}, f32[192]{0:T(256)}, u32[]{:S(2)}) copy-start(f32[192]{0:T(256)} %copy-done.146) | copy-start | bytes 2308
  83.2 32.6 %copy-start.163 = (f32[1536]{0:T(1024)S(1)}, f32[1536]{0:T(1024)}, u32[]{:S(2)}) copy-start(f32[1536]{0:T(1024)} %convert_reduce_fusion.15) | copy-start | bytes 18436
  118.1 56.1 %copy-start.189 = (f32[192,1536]{1,0:T(8,128)}, f32[192,1536]{1,0:T(8,128)S(1)}, u32[]{:S(2)}) copy-start(f32[192,1536]{1,0:T(8,128)S(1)} %convolution_add_fusion.6) | copy-start | bytes 3538948
  118.1 56.1 %copy-start.53 = (bf16[2,96,768]{2,1,0:T(8,128)(2,1)S(1)}, bf16[2,96,768]{2,1,0:T(8,128)(2,1)}, u32[]{:S(2)}) copy-start(bf16[2,96,768]{2,1,0:T(8,128)(2,1)} %param.27) | copy-start | bytes 884740
  174.2 43.8 %reduce-scatter.16.cloned.1.call-start = ((), (), s32[]{:S(2)}) async-start(), calls=%async_computation.15 | async-start | bytes 884736 | tf_op jit(solution)/shard_map/reduce_scatter | solution.py:147
  174.9 14.3 %copy-start.43 = (bf16[1,96,768]{2,1,0:T(8,128)(2,1)}, bf16[1,96,768]{2,1,0:T(8,128)(2,1)S(1)}, u32[]{:S(2)}) copy-start(bf16[1,96,768]{2,1,0:T(8,128)(2,1)S(1)} %get-tuple-element.60) | copy-start | bytes 442372
  176.9 34.1 %copy-start.12 = (bf16[1,192,768]{2,1,0:T(8,128)(2,1)}, bf16[1,192,768]{2,1,0:T(8,128)(2,1)S(1)}, u32[]{:S(2)}) copy-start(bf16[1,192,768]{2,1,0:T(8,128)(2,1)S(1)} %all-gather.1) | copy-start | bytes 884740
  179.3 13.1 %copy-start = (bf16[1,768,1152]{2,1,0:T(8,128)(2,1)S(1)}, bf16[1,768,1152]{2,1,0:T(8,128)(2,1)}, u32[]{:S(2)}) copy-start(bf16[1,768,1152]{2,1,0:T(8,128)(2,1)} %all-gather.7.cloned.1.call-done) | copy-start | bytes 5308420
  180.9 11.5 %copy-start.96 = (f32[768]{0:T(1024)S(1)}, f32[768]{0:T(1024)}, u32[]{:S(2)}) copy-start(f32[768]{0:T(1024)} %copy-done.95) | copy-start | bytes 9220
  180.9 11.5 %copy-start.167 = (f32[1152]{0:T(1024)S(1)}, f32[1152]{0:T(1024)}, u32[]{:S(2)}) copy-start(f32[1152]{0:T(1024)} %copy-done.166) | copy-start | bytes 13828
  181.9 7.2 %copy-start.65 = (bf16[96,768]{1,0:T(8,128)(2,1)}, bf16[96,768]{1,0:T(8,128)(2,1)S(1)}, u32[]{:S(2)}) copy-start(bf16[96,768]{1,0:T(8,128)(2,1)S(1)} %fusion.302) | copy-start | bytes 442372
  181.9 7.2 %collective-permute-start = (bf16[96,768]{1,0:T(8,128)(2,1)S(1)}, bf16[96,768]{1,0:T(8,128)(2,1)S(1)}, u32[]{:S(2)}, u32[]{:S(2)}) collective-permute-start(bf16[96,768]{1,0:T(8,128)(2,1)S(1)} %fusion.302), channel_id=1, source_target_pairs={{0,16},{1,17},{2,18},{3,19},{4,20},{5,21},{6,22},{7,23},{8,24},{9,... | collective-permute-start | bytes 442376 | tf_op jit(solution)/shard_map/ppermute | solution.py:19
  192.2 9.8 %copy-start.126 = (f32[192]{0:T(256)}, f32[192]{0:T(256)S(1)}, u32[]{:S(2)}) copy-start(f32[192]{0:T(256)S(1)} %broadcast_multiply_fusion.6) | copy-start | bytes 2308
  192.4 9.6 %copy-start.141 = (f32[192]{0:T(256)}, f32[192]{0:T(256)S(1)}, u32[]{:S(2)}) copy-start(f32[192]{0:T(256)S(1)} %add_rsqrt_fusion.1) | copy-start | bytes 2308
  203.9 4.0 copy-start.155
  203.9 5.8 copy-start.150
  207.9 51.7 %reduce-scatter.20.cloned.1.call-start = ((), (), s32[]{:S(2)}) async-start(), calls=%async_computation.17 | async-start | bytes 442368 | tf_op jit(solution)/shard_map/reduce_scatter | solution.py:208
  209.7 14.3 %copy-start.20 = (bf16[192,384]{0,1:T(8,128)(2,1)}, bf16[192,384]{0,1:T(8,128)(2,1)S(1)}, u32[]{:S(2)}) copy-start(bf16[192,384]{0,1:T(8,128)(2,1)S(1)} %copy.196) | copy-start | bytes 442372
  211.0 7.0 copy-start.94
  219.8 7.6 %copy-start.57 = (bf16[96,768]{1,0:T(8,128)(2,1)}, bf16[96,768]{1,0:T(8,128)(2,1)S(1)}, u32[]{:S(2)}) copy-start(bf16[96,768]{1,0:T(8,128)(2,1)S(1)} %get-tuple-element.80) | copy-start | bytes 442372
  219.8 7.6 %copy-start.52 = (bf16[2,96,768]{2,1,0:T(8,128)(2,1)S(1)}, bf16[2,96,768]{2,1,0:T(8,128)(2,1)}, u32[]{:S(2)}) copy-start(bf16[2,96,768]{2,1,0:T(8,128)(2,1)} %param.14) | copy-start | bytes 884740
  219.8 7.6 %collective-permute-start.1 = (bf16[96,768]{1,0:T(8,128)(2,1)S(1)}, bf16[96,768]{1,0:T(8,128)(2,1)S(1)}, u32[]{:S(2)}, u32[]{:S(2)}) collective-permute-start(bf16[96,768]{1,0:T(8,128)(2,1)S(1)} %get-tuple-element.80), channel_id=1, source_target_pairs={{0,16},{1,17},{2,18},{3,19},{4,20},{5,21},{6,22},{7,23},{8,24},{9,... | collective-permute-start | bytes 442376 | tf_op jit(solution)/shard_map/ppermute | solution.py:19
  227.4 4.9 copy-start.97
  227.4 4.9 copy-start.168
  249.8 50.7 %reduce-scatter.22.cloned.1.call-start = ((), (), s32[]{:S(2)}) async-start(), calls=%async_computation.18 | async-start | bytes 442368 | tf_op jit(solution)/shard_map/reduce_scatter | solution.py:208
  249.8 4.0 copy-start.151
  249.9 4.6 copy-start.174
  249.9 6.4 copy-start.183
  260.6 9.4 %copy-start.56 = (bf16[96,768]{1,0:T(8,128)(2,1)}, bf16[96,768]{1,0:T(8,128)(2,1)S(1)}, u32[]{:S(2)}) copy-start(bf16[96,768]{1,0:T(8,128)(2,1)S(1)} %fusion.300) | copy-start | bytes 442372
  260.6 7.8 %collective-permute-start.2 = (bf16[96,768]{1,0:T(8,128)(2,1)S(1)}, bf16[96,768]{1,0:T(8,128)(2,1)S(1)}, u32[]{:S(2)}, u32[]{:S(2)}) collective-permute-start(bf16[96,768]{1,0:T(8,128)(2,1)S(1)} %fusion.300), channel_id=1, source_target_pairs={{16,0},{17,1},{18,2},{19,3},{20,4},{21,5},{22,6},{23,7},{24,8},{25... | collective-permute-start | bytes 442376 | tf_op jit(solution)/shard_map/ppermute | solution.py:19
  284.4 4.0 copy-start.10
  284.4 4.0 copy-start.160
  284.4 4.0 copy-start.184
  292.2 72.8 %reduce-scatter.18.cloned.1.call-start = ((), (), s32[]{:S(2)}) async-start(), calls=%async_computation.16 | async-start | bytes 884736 | tf_op jit(solution)/shard_map/reduce_scatter | solution.py:147
  298.4 106.8 %reduce-scatter.34.cloned.1.call-start = ((), (), s32[]{:S(2)}) async-start(), calls=%async_computation.24 | async-start | bytes 221184
  302.2 10.2 %collective-permute-start.3 = (bf16[96,768]{1,0:T(8,128)(2,1)}, bf16[96,768]{1,0:T(8,128)(2,1)}, u32[]{:S(2)}, u32[]{:S(2)}) collective-permute-start(bf16[96,768]{1,0:T(8,128)(2,1)} %get-tuple-element.66), channel_id=1, source_target_pairs={{16,0},{17,1},{18,2},{19,3},{20,4},{21,5},{22,6},{23,7},{24,8},{25... | collective-permute-start | bytes 442376 | tf_op jit(solution)/shard_map/ppermute | solution.py:19
  326.7 4.0 copy-start.6
  335.5 73.7 %reduce-scatter.24.cloned.1.call-start = ((), (), s32[]{:S(2)}) async-start(), calls=%async_computation.19 | async-start | bytes 442368 | tf_op jit(solution)/shard_map/reduce_scatter | solution.py:208
  337.9 138.2 %reduce-scatter.28.cloned.1.call-start = ((), (), s32[]{:S(2)}) async-start(), calls=%async_computation.21 | async-start | bytes 663552 | tf_op jit(solution)/shard_map/reduce_scatter | solution.py:310
  340.7 203.9 %reduce-scatter.26.cloned.1.call-start = ((), (), s32[]{:S(2)}) async-start(), calls=%async_computation.20 | async-start | bytes 1990656 | tf_op jit(solution)/shard_map/reduce_scatter | solution.py:307
  345.9 270.7 %reduce-scatter.30.cloned.1.call-start = ((), (), s32[]{:S(2)}) async-start(), calls=%async_computation.22 | async-start | bytes 2654208 | tf_op jit(solution)/shard_map/reduce_scatter | solution.py:313
  351.6 336.9 %reduce-scatter.32.cloned.1.call-start = ((), (), s32[]{:S(2)}) async-start(), calls=%async_computation.23 | async-start | bytes 2654208 | tf_op jit(solution)/shard_map/reduce_scatter | solution.py:316
  365.0 44.2 %copy-start.48 = (bf16[96,768]{1,0:T(8,128)(2,1)S(1)}, bf16[96,768]{1,0:T(8,128)(2,1)}, u32[]{:S(2)}) copy-start(bf16[96,768]{1,0:T(8,128)(2,1)} %copy-done.47) | copy-start | bytes 442372
  365.0 45.2 %copy-start.59 = (bf16[1,96,768]{2,1,0:T(8,128)(2,1)S(1)}, bf16[1,96,768]{2,1,0:T(8,128)(2,1)}, u32[]{:S(2)}) copy-start(bf16[1,96,768]{2,1,0:T(8,128)(2,1)} %get-tuple-element.65) | copy-start | bytes 442372
  (152 other events, 231.5 us)
Sparse Core Ops, SparseCore 0:
  10.3 52.1 all-gather.6
  64.7 51.0 all-gather.8
  117.9 50.6 all-gather.10
  174.3 6.5 reduce-scatter.13
  208.0 9.9 reduce-scatter.15
  249.9 9.6 reduce-scatter.19
  292.3 8.0 reduce-scatter.21
  303.3 9.1 reduce-scatter.17
  335.7 63.9 reduce-scatter.33
  402.4 6.7 reduce-scatter.23
  412.8 63.2 reduce-scatter.27
  479.4 65.1 reduce-scatter.25
  548.5 68.0 reduce-scatter.29
  620.3 68.1 reduce-scatter.31
where the time goes:
time: 706 us; the launch traced here: 697 us
  waiting for transfers between devices  370 us (52%)
  blocking collectives  113 us (16%)
  matrix products  90.7 us (13%)
  local copies, waits for them, and re-layouts  49.4 us (7%)
  other arithmetic  46.3 us (7%)
  between operations  16.9 us (2%)
  starting transfers between devices  11.2 us (2%)
    reduce_scatter x1, waiting for transfers between devices, local(): lax.psum_scatter(totals[3].astype(jnp.bfloat16), 'dp', scatter_dimension=...  70.2 us
    reduce_scatter x1, waiting for transfers between devices, local(): lax.psum_scatter(totals[4].astype(jnp.bfloat16), 'dp', scatter_dimension=...  70.2 us
    reduce_scatter x1, waiting for transfers between devices, local(): lax.psum_scatter(totals[1].astype(jnp.bfloat16), 'dp', scatter_dimension=...  67 us
    reduce_scatter x1, waiting for transfers between devices, local(): lax.psum_scatter(totals[2].astype(jnp.bfloat16), 'dp', scatter_dimension=...  65.2 us
    all_gather x1, waiting for transfers between devices, local(): lax.all_gather(proj_weight, 'dp', axis=2, tiled=True)  50.4 us
    psum x1, blocking collectives, local(): bias_grads = lax.psum((totals[5], totals[6]), 'dp')  37.4 us
    all_gather x1, waiting for transfers between devices, local(): lax.all_gather(fc_weight, 'dp', axis=1, tiled=True)  32.2 us
    all_gather x1, blocking collectives, local(): lax.all_gather(out_weight, 'dp', axis=2, tiled=True)  32 us
  transfers between devices with their start and end apart: 18, of which 14 were waited for; matrix products, arithmetic and copies ran while one was open for 15% of the time, Pallas kernels for 0%

commit v1 on v0

v1 whole, which is shorter than its diff:
```python
import functools
import math

import jax
import jax.numpy as jnp
from jax import lax
from jax.experimental import pallas as pl
from jax.experimental.pallas import tpu as pltpu
from jax.sharding import PartitionSpec as P

HEAD = 64
ROT = 16
EPSILON = 1e-05
NEG_BIG = -1e30
VMEM_LIMIT = 48 * 1024 * 1024
BF = jnp.bfloat16
F32 = jnp.float32
SMALL = 128


def ring_device(place, count):
    if count == 8:
        return jnp.where(place < 4, 2 * place, 15 - 2 * place)
    if count == 32:
        folded = jnp.where(place < 16, place, 31 - place)
        row, column = folded // 4, folded % 4
        column = jnp.where(row % 2 == 0, column, 3 - column)
        return row * 4 + column + jnp.where(place < 16, 0, 16)
    return place


def ring_place(device, count):
    if count == 8:
        half = device // 2
        return jnp.where(device % 2 == 0, half, 7 - half)
    if count == 32:
        within = device % 16
        row, column = within // 4, within % 4
        column = jnp.where(row % 2 == 0, column, 3 - column)
        folded = row * 4 + column
        return jnp.where(device < 16, folded, 31 - folded)
    return device


def ring_list(count):
    if count == 8:
        return [0, 2, 4, 6, 7, 5, 3, 1]
    if count == 32:
        snake = []
        for row in range(4):
            line = [row * 4 + column for column in range(4)]
            snake += line if row % 2 == 0 else line[::-1]
        return snake + [16 + item for item in reversed(snake)]
    return list(range(count))


def ring_routes(count):
    order = ring_list(count)
    ahead = [(order[i], order[(i + 1) % count]) for i in range(count)]
    return ahead, [(target, source) for source, target in ahead]


def ring_gather(chunk, forward_steps):
    count = lax.axis_size("dp")
    ahead, behind = ring_routes(count)
    me = lax.axis_index("dp")
    place = ring_place(me, count)
    depth, width = chunk.shape
    whole = jnp.zeros((count * depth, width), chunk.dtype)
    whole = lax.dynamic_update_slice(whole, chunk, (me * depth, 0))
    backward_steps = count - 1 - forward_steps
    front = back = chunk
    for step in range(1, max(forward_steps, backward_steps) + 1):
        if step <= forward_steps:
            front = lax.ppermute(front, "dp", ahead)
            owner = ring_device((place + count - step) % count, count)
            whole = lax.dynamic_update_slice(whole, front, (owner * depth, 0))
        if step <= backward_steps:
            back = lax.ppermute(back, "dp", behind)
            owner = ring_device((place + step) % count, count)
            whole = lax.dynamic_update_slice(whole, back, (owner * depth, 0))
    return whole


def ring_scatter(terms, forward_steps):
    count = lax.axis_size("dp")
    ahead, behind = ring_routes(count)
    place = ring_place(lax.axis_index("dp"), count)
    depth = terms.shape[0] // count
    backward_steps = count - 1 - forward_steps

    def term(distance):
        owner = ring_device((place + count + distance) % count, count)
        return lax.dynamic_slice(terms, (owner * depth, 0), (depth, terms.shape[1]))

    front = back = None
    for step in range(max(forward_steps, backward_steps)):
        if step < forward_steps:
            own = term(forward_steps - step)
            if front is not None:
                own = (own.astype(F32) + front.astype(F32)).astype(BF)
            front = lax.ppermute(own, "dp", ahead)
        if step < backward_steps:
            own = term(step - backward_steps)
            if back is not None:
                own = (own.astype(F32) + back.astype(F32)).astype(BF)
            back = lax.ppermute(own, "dp", behind)
    return term(0).astype(F32) + front.astype(F32) + back.astype(F32)


def swap(block, axis):
    return lax.ppermute(block, axis, [(0, 1), (1, 0)])


def dot(left, right):
    return jnp.dot(left, right, preferred_element_type=F32)


def dot_last(left, right):
    return lax.dot_general(left, right, (((1,), (1,)), ((), ())), preferred_element_type=F32)


def dot_first(left, right):
    return lax.dot_general(left, right, (((0,), (0,)), ((), ())), preferred_element_type=F32)


def softmax_rows(queries, keys, bias):
    scores = dot_last(queries, keys) * (1.0 / math.sqrt(HEAD)) + bias
    peak = jnp.max(scores, axis=-1, keepdims=True)
    expons = jnp.exp(scores - peak)
    return expons / jnp.sum(expons, axis=-1, keepdims=True)


def head_parts(packed, index):
    base = index * 3 * HEAD
    return tuple(packed[:, base + j * HEAD : base + (j + 1) * HEAD] for j in range(3))


def turn(values, cosine, upper, lower):
    width = values.shape[1]
    return (
        values * cosine
        + pltpu.roll(values, width - ROT // 2, 1) * upper
        + pltpu.roll(values, ROT // 2, 1) * lower
    )


def forward_kernel(
    heads,
    own_ref,
    far_ref,
    first_w_ref,
    second_w_ref,
    qkv_bias_ref,
    fc_bias_ref,
    cos_ref,
    upper_ref,
    lower_ref,
    bias_ref,
    mine_ref,
    other_ref,
    norm1_ref,
    norm2_ref,
    xhat_ref,
    scale_ref,
    packed_ref,
    mixed_ref,
    pre_ref,
    act_ref,
    vector_ref,
):
    rows = own_ref.shape[0]
    qkv_width = heads * 3 * HEAD
    out_width = heads * HEAD
    wide = cos_ref.shape[1]
    hidden = fc_bias_ref.shape[1]
    small = first_w_ref[:, qkv_width + out_width :].astype(F32)
    vectors = jnp.transpose(small)[:8]
    vector_ref[...] = vectors
    values = jnp.concatenate([own_ref[...], far_ref[...]], axis=0).astype(F32)
    centred = values - jnp.mean(values, axis=-1, keepdims=True)
    scale = lax.rsqrt(jnp.mean(centred * centred, axis=-1, keepdims=True) + EPSILON)
    xhat = centred * scale
    xhat_ref[...] = xhat
    scale_ref[...] = jnp.broadcast_to(scale, scale_ref.shape)
    first = (xhat * vectors[0:1] + vectors[1:2]).astype(BF)
    second = (xhat * vectors[2:3] + vectors[3:4]).astype(BF)
    norm1_ref[...] = first
    norm2_ref[...] = second
    packed = dot(first, first_w_ref[:, :wide]) + qkv_bias_ref[...]
    packed = turn(packed, cos_ref[...], upper_ref[...], lower_ref[...]).astype(BF)
    packed_ref[...] = packed
    bias = bias_ref[...]
    mixed = []
    for index in range(heads):
        queries, keys, held = head_parts(packed, index)
        weights = softmax_rows(queries, keys, bias).astype(BF)
        mixed.append(dot(weights, held))
    mixed = jnp.concatenate(mixed, axis=1).astype(BF)
    mixed_ref[...] = mixed
    pre = dot(second, second_w_ref[:, :hidden]) + fc_bias_ref[...]
    pre_ref[...] = pre
    act = (pre * (0.5 + 0.5 * lax.erf(pre * math.sqrt(0.5)))).astype(BF)
    act_ref[...] = act
    total = dot_last(act, second_w_ref[:, hidden:])
    total = total + dot_last(mixed, first_w_ref[:, qkv_width : qkv_width + out_width])
    mine_ref[...] = total[:rows]
    other_ref[...] = total[rows:]


def backward_kernel(
    heads,
    own_ref,
    far_ref,
    first_w_ref,
    second_w_ref,
    cos_ref,
    upper_ref,
    lower_ref,
    bias_ref,
    xhat_ref,
    scale_ref,
    packed_ref,
    pre_ref,
    vector_ref,
    mine_ref,
    other_ref,
    d_packed_ref,
    d_pre_ref,
    sums_ref,
):
    rows = own_ref.shape[0]
    qkv_width = heads * 3 * HEAD
    out_width = heads * HEAD
    wide = cos_ref.shape[1]
    hidden = pre_ref.shape[1]
    grad = jnp.concatenate([own_ref[...], far_ref[...]], axis=0)
    d_act = dot(grad, second_w_ref[:, hidden:])
    pre = pre_ref[...]
    slope = 0.5 + 0.5 * lax.erf(pre * math.sqrt(0.5))
    slope = slope + pre * (jnp.exp(pre * pre * -0.5) * (1.0 / math.sqrt(2.0 * math.pi)))
    d_pre = (d_act * slope).astype(BF)
    d_pre_ref[...] = d_pre
    d_second = dot_last(d_pre, second_w_ref[:, :hidden])
    d_mixed = dot(grad, first_w_ref[:, qkv_width : qkv_width + out_width]).astype(BF)
    bias = bias_ref[...]
    packed = packed_ref[...]
    parts = []
    for index in range(heads):
        queries, keys, held = head_parts(packed, index)
        weights = softmax_rows(queries, keys, bias)
        given = d_mixed[:, index * HEAD : (index + 1) * HEAD]
        d_held = dot_first(weights.astype(BF), given)
        d_weights = dot_last(given, held)
        row_dot = jnp.sum(weights * d_weights, axis=-1, keepdims=True)
        d_scores = (weights * (d_weights - row_dot)).astype(BF)
        parts.append(dot(d_scores, keys) * (1.0 / math.sqrt(HEAD)))
        parts.append(dot_first(d_scores, queries) * (1.0 / math.sqrt(HEAD)))
        parts.append(d_held)
    if wide > qkv_width:
        parts.append(jnp.zeros((2 * rows, wide - qkv_width), F32))
    d_packed = jnp.concatenate(parts, axis=1)
    d_packed = turn(d_packed, cos_ref[...], -upper_ref[...], -lower_ref[...]).astype(BF)
    d_packed_ref[...] = d_packed
    d_first = dot_last(d_packed, first_w_ref[:, :wide])
    xhat = xhat_ref[...]
    inner = d_first * vector_ref[0:1] + d_second * vector_ref[2:3]
    average = jnp.mean(inner, axis=-1, keepdims=True)
    along = jnp.mean(inner * xhat, axis=-1, keepdims=True)
    total = (inner - average - xhat * along) * scale_ref[:, 0:1]
    mine_ref[...] = total[:rows]
    other_ref[...] = total[rows:]

    def add_rows(block):
        return jnp.sum(block, axis=0, keepdims=True)

    width = sums_ref.shape[1]
    packed_sum = add_rows(d_packed.astype(F32))
    if wide < width:
        packed_sum = jnp.concatenate([packed_sum, jnp.zeros((1, width - wide), F32)], axis=1)
    sums_ref[...] = jnp.concatenate(
        [
            add_rows(d_first * xhat),
            add_rows(d_first),
            add_rows(d_second * xhat),
            add_rows(d_second),
            add_rows(grad.astype(F32)) * 0.25,
            add_rows(d_pre.astype(F32)),
            packed_sum,
            jnp.zeros((1, width), F32),
        ],
        axis=0,
    )


def weight_kernel(heads, depth, count, *refs):
    refs = list(refs)
    groups = [refs[i * 9 : (i + 1) * 9] for i in range(count)]
    first_out_ref, second_out_ref, full_refs = (
        refs[9 * count + count],
        refs[9 * count + count + 1],
        refs[9 * count : 9 * count + count],
    )
    qkv_width = heads * 3 * HEAD
    tile = first_out_ref.shape[0]

    def both(index):
        return jnp.concatenate([group[index][...] for group in groups], axis=0)

    def both_grads():
        parts = []
        for group in groups:
            parts += [group[2][...], group[3][...]]
        return jnp.concatenate(parts, axis=0)

    first, second, grad = both(0), both(1), both_grads()
    d_packed, d_pre, mixed, act = both(4), both(5), both(6), both(7)
    hidden = d_pre.shape[1]
    sums = sum(group[8][...] for group in groups[1:]) + groups[0][8][...]
    full = sum(item[...] for item in full_refs[1:]) + full_refs[0][...]
    long_row = jnp.concatenate([full[6:7, :qkv_width], full[5:6, :hidden]], axis=1)
    pieces = long_row.shape[1] // depth
    stacked = jnp.concatenate(
        [long_row[:, i * depth : (i + 1) * depth] for i in range(pieces)], axis=0
    )
    stacked = jnp.concatenate([stacked] * (tile // depth), axis=1)
    rest = SMALL - 8 - pieces
    small = jnp.concatenate([sums, stacked, jnp.zeros((rest, tile), F32)], axis=0)
    first_out_ref[...] = jnp.concatenate(
        [
            dot_first(first, d_packed)[:, :qkv_width],
            dot_first(grad, mixed),
            jnp.transpose(small),
        ],
        axis=1,
    ).astype(BF)
    second_out_ref[:, :hidden] = dot_first(second, d_pre).astype(BF)
    second_out_ref[:, hidden:] = dot_first(grad, act).astype(BF)


def cost(flops, moved):
    return pl.CostEstimate(flops=int(flops), bytes_accessed=int(moved), transcendentals=0)


def forward_call(own, far, weights, biases, layout, heads):
    rows, model = own.shape
    full = 2 * rows
    first_w, second_w = weights
    hidden = second_w.shape[1] // 2
    wide = layout[0].shape[1]

    def shape(height, width, kind):
        return jax.ShapeDtypeStruct((height, width), kind)

    outs = (
        shape(rows, model, F32),
        shape(rows, model, F32),
        shape(full, model, BF),
        shape(full, model, BF),
        shape(full, model, F32),
        shape(full, 128, F32),
        shape(full, wide, BF),
        shape(full, heads * HEAD, BF),
        shape(full, hidden, F32),
        shape(full, hidden, BF),
        shape(8, model, F32),
    )
    return pl.pallas_call(
        functools.partial(forward_kernel, heads),
        out_shape=outs,
        compiler_params=pltpu.CompilerParams(vmem_limit_bytes=VMEM_LIMIT),
        cost_estimate=cost(4e9, 8e6),
        name="forward",
    )(own, far, first_w, second_w, biases[0], biases[1], *layout)


def backward_call(own, far, weights, layout, kept, heads):
    rows, model = own.shape
    full = 2 * rows
    first_w, second_w = weights
    hidden = second_w.shape[1] // 2
    wide = layout[0].shape[1]
    norm1, norm2, xhat, scale, packed, mixed, pre, act, vectors = kept
    outs = (
        jax.ShapeDtypeStruct((rows, model), F32),
        jax.ShapeDtypeStruct((rows, model), F32),
        jax.ShapeDtypeStruct((full, wide), BF),
        jax.ShapeDtypeStruct((full, hidden), BF),
        jax.ShapeDtypeStruct((8, model), F32),
    )
    return pl.pallas_call(
        functools.partial(backward_kernel, heads),
        out_shape=outs,
        compiler_params=pltpu.CompilerParams(vmem_limit_bytes=VMEM_LIMIT),
        cost_estimate=cost(8e9, 10e6),
        name="backward",
    )(own, far, first_w, second_w, *layout, xhat, scale, packed, pre, vectors)


def weight_call(grads, kept, backs, heads, depth):
    model = kept[0][0].shape[1]
    hidden = kept[0][7].shape[1]
    tile = model // 2
    first_width = heads * 4 * HEAD + SMALL
    operands, specs = [], []

    def tiled(array):
        operands.append(array)
        specs.append(pl.BlockSpec((array.shape[0], tile), lambda i: (0, i)))

    def whole(array):
        operands.append(array)
        specs.append(pl.BlockSpec(array.shape, lambda i: (0, 0)))

    for (own, far), keep, back in zip(grads, kept, backs):
        tiled(keep[0])
        tiled(keep[1])
        tiled(own)
        tiled(far)
        whole(back[2])
        whole(back[3])
        whole(keep[5])
        whole(keep[7])
        tiled(back[4])
    for back in backs:
        whole(back[4])
    return pl.pallas_call(
        functools.partial(weight_kernel, heads, depth, len(grads)),
        grid=(2,),
        in_specs=specs,
        out_specs=(
            pl.BlockSpec((tile, first_width), lambda i: (i, 0)),
            pl.BlockSpec((tile, 2 * hidden), lambda i: (i, 0)),
        ),
        out_shape=(
            jax.ShapeDtypeStruct((model, first_width), BF),
            jax.ShapeDtypeStruct((model, 2 * hidden), BF),
        ),
        compiler_params=pltpu.CompilerParams(vmem_limit_bytes=VMEM_LIMIT),
        cost_estimate=cost(8e9, 10e6),
        name="weights",
    )(*operands)


def layout_of(lengths, rows, first_row, heads):
    full = 2 * rows
    ends = jnp.cumsum(lengths)
    places = (jnp.arange(full, dtype=jnp.int32) + first_row) % full
    segment = jnp.sum((places[:, None] >= ends[None, :]).astype(jnp.int32), axis=1)
    picked = segment[:, None] == jnp.arange(lengths.shape[0], dtype=jnp.int32)[None, :]
    position = places - jnp.sum(jnp.where(picked, (ends - lengths)[None, :], 0), axis=1)
    allowed = (segment[:, None] == segment[None, :]) & (places[:, None] >= places[None, :])
    bias = jnp.where(allowed, 0.0, NEG_BIG).astype(F32)
    half = ROT // 2
    inverse = jnp.exp(jnp.arange(half, dtype=F32) * (-2.0 * math.log(10000.0) / ROT))
    angles = position.astype(F32)[:, None] * inverse
    cosine, sine = jnp.cos(angles), jnp.sin(angles)
    plain = jnp.ones((full, HEAD - ROT), F32)
    empty = jnp.zeros((full, HEAD - ROT), F32)
    none = jnp.zeros((full, half), F32)
    cos_head = jnp.concatenate([cosine, cosine, plain], axis=1)
    upper_head = jnp.concatenate([-sine, none, empty], axis=1)
    lower_head = jnp.concatenate([none, sine, empty], axis=1)

    def spread(head, fill):
        rest = jnp.full((full, HEAD), fill, F32)
        table = jnp.concatenate([head, head, rest] * heads, axis=1)
        pad = -table.shape[1] % 128
        return jnp.concatenate([table, jnp.full((full, pad), fill, F32)], axis=1) if pad else table

    return spread(cos_head, 1.0), spread(upper_head, 0.0), spread(lower_head, 0.0), bias


def local(
    inputs,
    lengths,
    ln1_gain,
    ln1_shift,
    ln2_gain,
    ln2_shift,
    qkv_weight,
    qkv_bias,
    out_weight,
    fc_weight,
    fc_bias,
    proj_weight,
    branch_bias,
    cotangent,
):
    micro, rows, model = inputs.shape
    count = lax.axis_size("dp")
    pipe = lax.axis_index("pipe")
    core = lax.axis_index("tensor")
    leading = pipe == 0
    depth = qkv_weight.shape[1]
    qkv_width = qkv_weight.shape[2] // 2
    out_width = out_weight.shape[1] // 2
    hidden = fc_weight.shape[2] // 2
    heads = out_width // HEAD
    ahead_steps = count // 2

    vectors = jnp.concatenate([ln1_gain, ln1_shift, ln2_gain, ln2_shift, branch_bias], axis=0)
    vectors = jnp.pad(jnp.transpose(vectors), ((0, 0), (0, SMALL - 5)))
    out_turned = jnp.transpose(out_weight[0])
    proj_turned = jnp.transpose(proj_weight[0])

    def cut(array, width, index):
        return array[:, index * width : (index + 1) * width]

    def quarter(index):
        first = jnp.concatenate(
            [cut(qkv_weight[0], qkv_width, index), cut(out_turned, out_width, index), vectors],
            axis=1,
        )
        second = jnp.concatenate(
            [cut(fc_weight[0], hidden, index), cut(proj_turned, hidden, index)], axis=1
        )
        bias = jnp.concatenate([cut(qkv_bias, qkv_width, index), cut(fc_bias, hidden, index)], 1)
        return first, second, bias

    lower_part, upper_part = quarter(0), quarter(1)
    chunks = []
    for low_item, high_item in zip(lower_part, upper_part):
        kept_item = jnp.where(leading, low_item, high_item)
        sent_item = jnp.where(leading, high_item, low_item)
        came_item = swap(sent_item, "pipe")
        chunks.append(
            (
                jnp.where(leading, kept_item, came_item),
                jnp.where(leading, came_item, kept_item),
            )
        )
    weights, biases = [], []
    for section in range(2):
        weights.append(
            (
                ring_gather(chunks[0][section], ahead_steps),
                ring_gather(chunks[1][section], count - 1 - ahead_steps),
            )
        )
        long_bias = chunks[2][section].astype(F32)
        first_bias = long_bias[:, :qkv_width]
        pad = -qkv_width % 128
        biases.append((jnp.pad(first_bias, ((0, 0), (0, pad))), long_bias[:, qkv_width:]))

    layouts = [layout_of(lengths[m, 0], rows, core * rows, heads) for m in range(micro)]

    def complete(half, base):
        came = swap(half, "pipe")
        return (base + (half.astype(F32) + came.astype(F32))).astype(BF)

    def half_sum(mine, other):
        return (mine + swap(other, "tensor")).astype(BF)

    current = [(inputs[m], swap(inputs[m], "tensor")) for m in range(micro)]
    cotangents = [(cotangent[m], swap(cotangent[m], "tensor")) for m in range(micro)]
    stored, outputs = [], []
    for section in range(2):
        kept_rows, results = [], []
        for m in range(micro):
            own, far = current[m]
            found = forward_call(own, far, weights[section], biases[section], layouts[m], heads)
            kept_rows.append(found[2:])
            half = half_sum(found[0], found[1])
            base = own.astype(F32) + found[-1][4:5]
            results.append(complete(half, base))
        if section == 0:
            current = [(item, swap(item, "tensor")) for item in results]
        stored.append(kept_rows)
        outputs.append(results)

    grads = cotangents
    back_outputs, reduced = [None, None], [None, None]
    for section in (1, 0):
        backs, results = [], []
        for m in range(micro):
            own, far = grads[m]
            found = backward_call(
                own, far, weights[section], layouts[m], stored[section][m], heads
            )
            backs.append(found)
            half = half_sum(found[0], found[1])
            results.append(complete(half, own.astype(F32)))
        first_terms, second_terms = weight_call(grads, stored[section], backs, heads, depth)
        reduced[section] = (
            ring_scatter(first_terms, ahead_steps),
            ring_scatter(second_terms, count - 1 - ahead_steps),
        )
        back_outputs[section] = results
        if section == 1:
            grads = [(item, swap(item, "tensor")) for item in results]

    activations = jnp.where(leading, jnp.stack(outputs[0]), jnp.stack(outputs[1]))[None]
    input_grads = jnp.where(leading, jnp.stack(back_outputs[0]), jnp.stack(back_outputs[1]))[None]

    halves = []
    for index in range(2):
        own = jnp.where(leading, reduced[0][index], reduced[1][index])
        given = jnp.where(leading, reduced[1][index], reduced[0][index]).astype(BF)
        came = swap(given, "pipe").astype(F32)
        halves.append((own, came))

    def joined(index, start, width):
        own, came = (item[:, start : start + width] for item in halves[index])
        lower_item = jnp.where(leading, own, came)
        upper_item = jnp.where(leading, came, own)
        return jnp.concatenate([lower_item, upper_item], axis=1)

    small_start = qkv_width + out_width
    own_small, came_small = (item[:, small_start:] for item in halves[0])
    vector_grads = own_small[:, :8] + came_small[:, :8]
    vector_grads = jnp.transpose(vector_grads + swap(vector_grads, "tensor"))
    pieces = (qkv_width + hidden) // depth

    def flat(block):
        return jnp.transpose(block[:, 8 : 8 + pieces]).reshape(1, -1)

    own_bias, came_bias = flat(own_small), flat(came_small)
    lower_bias = jnp.where(leading, own_bias, came_bias)
    upper_bias = jnp.where(leading, came_bias, own_bias)
    qkv_bias_grad = jnp.concatenate([lower_bias[:, :qkv_width], upper_bias[:, :qkv_width]], axis=1)
    fc_bias_grad = jnp.concatenate([lower_bias[:, qkv_width:], upper_bias[:, qkv_width:]], axis=1)
    return (
        activations,
        input_grads,
        vector_grads[0:1],
        vector_grads[1:2],
        vector_grads[2:3],
        vector_grads[3:4],
        joined(0, 0, qkv_width)[None],
        qkv_bias_grad,
        jnp.transpose(joined(0, qkv_width, out_width))[None],
        joined(1, 0, hidden)[None],
        fc_bias_grad,
        jnp.transpose(joined(1, hidden, hidden))[None],
        vector_grads[4:5],
    )


def solution(mesh):
    rows = P(None, ("dp", "tensor"), None)
    vector = P("pipe", "dp")
    bias = P("pipe", "tensor")
    wide = P("pipe", "dp", "tensor")
    tall = P("pipe", "tensor", "dp")
    result = P("pipe", None, ("dp", "tensor"), None)
    return jax.shard_map(
        local,
        mesh=mesh,
        in_specs=(
            rows,
            P(None, "dp", None),
            vector,
            vector,
            vector,
            vector,
            wide,
            bias,
            tall,
            wide,
            bias,
            tall,
            vector,
            rows,
        ),
        out_specs=(
            result,
            result,
            vector,
            vector,
            vector,
            vector,
            wide,
            bias,
            tall,
            wide,
            bias,
            tall,
            vector,
        ),
        check_vma=False,
    )
```

time: 706 us -> 342 us (0.48)
  waiting for transfers between devices: 370 us -> 133 us
  blocking collectives: 113 us -> 0 us
  matrix products: 90.7 us -> 0 us
  starting transfers between devices: 11.2 us -> 88.2 us
  Pallas kernels: 0 us -> 59.6 us
  local copies, waits for them, and re-layouts: 49.4 us -> 29.8 us
  other arithmetic: 46.3 us -> 27 us
  between operations: 16.9 us -> 2.92 us
    reduce_scatter x10 -> x0, waiting for transfers between devices: 277 us -> none  [the longest x1 70.2 us: local(): lax.psum_scatter(totals[3].astype(jnp.bfloat16), 'dp', scatter_dimension=...]
    ppermute x4 -> x86, waiting for transfers between devices: 8.19 us -> 133 us  [the longest x14 35.7 us: ring_scatter(): front = lax.ppermute(own, 'dp', ahead)]
    dot_general x57 -> x0, matrix products: 90.7 us -> none  [the longest x12 23.9 us: times_transposed(): lax.dot_general(left, right, (((1,), (1,)), ((), ())), preferred_element_...]
    all_gather x3 -> x0, waiting for transfers between devices: 82.6 us -> none  [the longest x1 50.4 us: local(): lax.all_gather(proj_weight, 'dp', axis=2, tiled=True)]
    ppermute x4 -> x86, starting transfers between devices: 10.4 us -> 88.2 us  [the longest x14 22.2 us: ring_gather(): front = lax.ppermute(front, 'dp', ahead)]
    all_gather x8 -> x0, blocking collectives: 73.1 us -> none  [the longest x1 32 us: local(): lax.all_gather(out_weight, 'dp', axis=2, tiled=True)]
    pallas_call x0 -> x10, Pallas kernels: none -> 59.6 us  [the longest x4 34.4 us: backward_call(): pl.pallas_call(functools.partial(backward_kernel, heads), out_shape=outs,...]
    psum x2 -> x0, blocking collectives: 39.8 us -> none  [the longest x1 37.4 us: local(): bias_grads = lax.psum((totals[5], totals[6]), 'dp')]
  transfers between devices with their start and end apart: 18 -> 86, of which waited for: 14 -> 42; matrix products, arithmetic and copies ran while one was open for 15% -> 13% of each run, Pallas kernels for 0% -> 18%
where the time goes in v1:
time: 342 us; the launch traced here: 340 us
  waiting for transfers between devices  133 us (39%)
  starting transfers between devices  88.2 us (26%)
  Pallas kernels  59.6 us (17%)
  local copies, waits for them, and re-layouts  29.8 us (9%)
  other arithmetic  27 us (8%)
    ppermute x14, waiting for transfers between devices, ring_scatter(): front = lax.ppermute(own, 'dp', ahead)  35.7 us
    pallas_call x4, Pallas kernels, backward_call(): pl.pallas_call(functools.partial(backward_kernel, heads), out_shape=outs,...  34.4 us
    ppermute x14, waiting for transfers between devices, ring_gather(): front = lax.ppermute(front, 'dp', ahead)  28.9 us
    ppermute x30, waiting for transfers between devices, swap(): return lax.ppermute(block, axis, [(0, 1), (1, 0)])  23.6 us
    ppermute x14, waiting for transfers between devices, ring_scatter(): back = lax.ppermute(own, 'dp', behind)  22.6 us
    ppermute x14, starting transfers between devices, ring_gather(): front = lax.ppermute(front, 'dp', ahead)  22.2 us
    ppermute x14, waiting for transfers between devices, ring_gather(): back = lax.ppermute(back, 'dp', behind)  21.9 us
    ppermute x30, starting transfers between devices, swap(): return lax.ppermute(block, axis, [(0, 1), (1, 0)])  21.8 us
  transfers between devices with their start and end apart: 86, of which 42 were waited for; matrix products, arithmetic and copies ran while one was open for 13% of the time, Pallas kernels for 18%

profile of v1, /device:TPU:0, one launch (start us, length us, event | category | flops | bytes accessed | tf_op | source)
XLA Modules:
  0.0 340.0 jit_solution(8258674673584843042)
XLA Ops:
  0.7 1.7 slice_bitcast_fusion.3
  6.6 2.5 collective-permute-start.1
  12.0 2.0 collective-permute-start.17
  21.4 2.6 concatenate.141.lower_ref
  27.1 1.6 collective-permute-start.2
  30.4 1.6 collective-permute-start.24
  38.9 1.6 collective-permute-start.4
  40.6 1.6 collective-permute-start.26
  42.3 8.7 %collective-permute-done.4 = bf16[96,896]{1,0:T(8,128)(2,1)S(1)} collective-permute-done((bf16[96,896]{1,0:T(8,128)(2,1)S(1)}, bf16[96,896]{1,0:T(8,128)(2,1)S(1)}, u32[]{:S(2)}, u32[]{:S(2)}) %collective-permute-start.4) | collective-permute-done | bytes 172064 | tf_op jit(solution)/shard_map/ppermute | solution.py:75
  54.5 3.6 %collective-permute-done.5 = bf16[96,896]{1,0:T(8,128)(2,1)S(1)} collective-permute-done((bf16[96,896]{1,0:T(8,128)(2,1)S(1)}, bf16[96,896]{1,0:T(8,128)(2,1)S(1)}, u32[]{:S(2)}, u32[]{:S(2)}) %collective-permute-start.5) | collective-permute-done | bytes 172064 | tf_op jit(solution)/shard_map/ppermute | solution.py:79
  59.6 2.2 collective-permute-done.27
  64.0 4.2 %collective-permute-done.11 = bf16[96,1536]{1,0:T(8,128)(2,1)S(1)} collective-permute-done((bf16[96,1536]{1,0:T(8,128)(2,1)S(1)}, bf16[96,1536]{1,0:T(8,128)(2,1)S(1)}, u32[]{:S(2)}, u32[]{:S(2)}) %collective-permute-start.11) | collective-permute-done | bytes 294944 | tf_op jit(solution)/shard_map/ppermute | solution.py:79
  71.9 2.1 collective-permute-done.32
  76.2 4.7 %collective-permute-done.28 = bf16[96,896]{1,0:T(8,128)(2,1)S(1)} collective-permute-done((bf16[96,896]{1,0:T(8,128)(2,1)S(1)}, bf16[96,896]{1,0:T(8,128)(2,1)S(1)}, u32[]{:S(2)}, u32[]{:S(2)}) %collective-permute-start.28) | collective-permute-done | bytes 172064 | tf_op jit(solution)/shard_map/ppermute | solution.py:75
  82.4 1.6 collective-permute-start.8
  84.1 1.7 collective-permute-start.30
  85.9 6.0 %collective-permute-done.8 = bf16[96,896]{1,0:T(8,128)(2,1)S(1)} collective-permute-done((bf16[96,896]{1,0:T(8,128)(2,1)S(1)}, bf16[96,896]{1,0:T(8,128)(2,1)S(1)}, u32[]{:S(2)}, u32[]{:S(2)}) %collective-permute-start.8) | collective-permute-done | bytes 172064 | tf_op jit(solution)/shard_map/ppermute | solution.py:75
  91.9 2.1 collective-permute-start.13
  100.1 4.3 %collective-permute-done.33 = bf16[96,1536]{1,0:T(8,128)(2,1)S(1)} collective-permute-done((bf16[96,1536]{1,0:T(8,128)(2,1)S(1)}, bf16[96,1536]{1,0:T(8,128)(2,1)S(1)}, u32[]{:S(2)}, u32[]{:S(2)}) %collective-permute-start.33) | collective-permute-done | bytes 294944 | tf_op jit(solution)/shard_map/ppermute | solution.py:75
  104.4 2.3 collective-permute-start.15
  108.9 1.9 collective-permute-start.36
  110.8 3.9 %collective-permute-done.15 = bf16[96,1536]{1,0:T(8,128)(2,1)S(1)} collective-permute-done((bf16[96,1536]{1,0:T(8,128)(2,1)S(1)}, bf16[96,1536]{1,0:T(8,128)(2,1)S(1)}, u32[]{:S(2)}, u32[]{:S(2)}) %collective-permute-start.15) | collective-permute-done | bytes 294944 | tf_op jit(solution)/shard_map/ppermute | solution.py:79
  114.8 1.9 collective-permute-start.16
  118.0 3.7 %collective-permute-done.16 = bf16[96,1536]{1,0:T(8,128)(2,1)S(1)} collective-permute-done((bf16[96,1536]{1,0:T(8,128)(2,1)S(1)}, bf16[96,1536]{1,0:T(8,128)(2,1)S(1)}, u32[]{:S(2)}, u32[]{:S(2)}) %collective-permute-start.16) | collective-permute-done | bytes 294944 | tf_op jit(solution)/shard_map/ppermute | solution.py:79
  121.7 2.1 collective-permute-start.37
  125.3 4.4 %forward.4 = (f32[96,768]{1,0:T(8,128)S(1)}, f32[96,768]{1,0:T(8,128)S(1)}, bf16[192,768]{1,0:T(8,128)(2,1)S(1)}, bf16[192,768]{1,0:T(8,128)(2,1)S(1)}, f32[192,...) custom-call(bf16[96,768]{1,0:T(8,128)(2,1)} %get-tuple-element.260.o, ...), custom_call_target="tpu_custom_call" | custom-call | flops 4000000000 | bytes 8000000 | tf_op jit(solution)/shard_map/forward/pallas_call | solution.py:368
  131.1 4.6 %forward.5 = (f32[96,768]{1,0:T(8,128)S(1)}, f32[96,768]{1,0:T(8,128)S(1)}, bf16[192,768]{1,0:T(8,128)(2,1)S(1)}, bf16[192,768]{1,0:T(8,128)(2,1)S(1)}, f32[192,...) custom-call(bf16[96,768]{1,0:T(8,128)(2,1)S(1)} %get-tuple-element.2, ...), custom_call_target="tpu_custom_call" | custom-call | flops 4000000000 | bytes 8000000 | tf_op jit(solution)/shard_map/forward/pallas_call | solution.py:368
  138.4 4.5 %collective-permute-done.19 = bf16[96,768]{1,0:T(8,128)(2,1)S(1)} collective-permute-done((bf16[96,768]{1,0:T(8,128)(2,1)S(1)}, bf16[96,768]{1,0:T(8,128)(2,1)S(1)}, u32[]{:S(2)}, u32[]{:S(2)}) %collective-permute-start.19) | collective-permute-done | bytes 147488 | tf_op jit(solution)/shard_map/ppermute | solution.py:112
  142.9 2.5 collective-permute-done.22
  147.1 4.3 %forward.7 = (f32[96,768]{1,0:T(8,128)S(1)}, f32[96,768]{1,0:T(8,128)S(1)}, bf16[192,768]{1,0:T(8,128)(2,1)S(1)}, bf16[192,768]{1,0:T(8,128)(2,1)S(1)}, f32[192,...) custom-call(bf16[96,768]{1,0:T(8,128)(2,1)S(1)} %get-tuple-element.2, ...), custom_call_target="tpu_custom_call" | custom-call | flops 4000000000 | bytes 8000000 | tf_op jit(solution)/shard_map/forward/pallas_call | solution.py:368
  153.3 4.3 %forward.6 = (f32[96,768]{1,0:T(8,128)S(1)}, f32[96,768]{1,0:T(8,128)S(1)}, bf16[192,768]{1,0:T(8,128)(2,1)S(1)}, bf16[192,768]{1,0:T(8,128)(2,1)S(1)}, f32[192,...) custom-call(bf16[96,768]{1,0:T(8,128)(2,1)S(1)} %get-tuple-element.2, ...), custom_call_target="tpu_custom_call" | custom-call | flops 4000000000 | bytes 8000000 | tf_op jit(solution)/shard_map/forward/pallas_call | solution.py:368
  161.1 5.3 %backward.4 = (f32[96,768]{1,0:T(8,128)S(1)}, f32[96,768]{1,0:T(8,128)S(1)}, bf16[192,640]{1,0:T(8,128)(2,1)S(1)}, bf16[192,768]{1,0:T(8,128)(2,1)S(1)}, f32[8,768]{1,0:T(8,128)S(1)}) custom-call(bf16[96,768]{1,0:T(8,128)(2,1)S(1)} %copy-done.4, bf16[96,768]{1,0:T(8,128)(2,1)S(1)} %collective-permute-done.43.far_ref.refs_3_, bf16[768,896]{1,0:T(8,128)(2,1)S(1)} %copy-done.1, ...), custom_call_target="tpu_custom_call" | custom-call | flops 8000000000 | bytes 10000000 | tf_op jit(solution)/shard_map/backward/pallas_call | solution.py:391
  168.3 18.3 %backward.6 = (f32[96,768]{1,0:T(8,128)S(1)}, f32[96,768]{1,0:T(8,128)S(1)}, bf16[192,640]{1,0:T(8,128)(2,1)S(1)}, bf16[192,768]{1,0:T(8,128)(2,1)S(1)}, f32[8,768]{1,0:T(8,128)S(1)}) custom-call(bf16[96,768]{1,0:T(8,128)(2,1)S(1)} %copy-done.5, bf16[96,768]{1,0:T(8,128)(2,1)S(1)} %collective-permute-done.49.far_ref.refs_12_, ...), custom_call_target="tpu_custom_call" | custom-call | flops 8000000000 | bytes 10000000 | tf_op jit(solution)/shard_map/backward/pallas_call | solution.py:391
  186.7 3.8 %weights.3 = (bf16[768,896]{1,0:T(8,128)(2,1)S(1)}, bf16[768,1536]{1,0:T(8,128)(2,1)}) custom-call(bf16[192,768]{1,0:T(8,128)(2,1)S(1)} %copy-done.25, bf16[192,768]{1,0:T(8,128)(2,1)S(1)} %copy-done.27, bf16[96,768]{1,0:T(8,128)(2,1)S(1)} %copy-done.4, bf16[96,768]{1,0:T(8,128)(2,1)S(1)} %collective-permute-done.43.far_ref.refs_3_, ...), custom_call_target="tpu_custom_call" | custom-call | flops 8000000000 | bytes 10000000 | tf_op jit(solution)/shard_map/weights/pallas_call | solution.py:427
  193.5 4.3 %collective-permute-done.62 = bf16[96,896]{1,0:T(8,128)(2,1)S(1)} collective-permute-done((bf16[96,896]{1,0:T(8,128)(2,1)S(1)}, bf16[96,896]{1,0:T(8,128)(2,1)S(1)}, u32[]{:S(2)}, u32[]{:S(2)}) %collective-permute-start.62) | collective-permute-done | bytes 172064 | tf_op jit(solution)/shard_map/ppermute | solution.py:102
  197.9 5.4 %collective-permute-done.78 = bf16[96,1536]{1,0:T(8,128)(2,1)S(1)} collective-permute-done((bf16[96,1536]{1,0:T(8,128)(2,1)S(1)}, bf16[96,1536]{1,0:T(8,128)(2,1)S(1)}, u32[]{:S(2)}, u32[]{:S(2)}) %collective-permute-start.78) | collective-permute-done | bytes 294944 | tf_op jit(solution)/shard_map/ppermute | solution.py:102
  205.0 1.6 collective-permute-start.81
  210.4 1.7 collective-permute-done.63
  212.8 3.8 %collective-permute-done.45 = bf16[96,768]{1,0:T(8,128)(2,1)S(1)} collective-permute-done((bf16[96,768]{1,0:T(8,128)(2,1)S(1)}, bf16[96,768]{1,0:T(8,128)(2,1)S(1)}, u32[]{:S(2)}, u32[]{:S(2)}) %collective-permute-start.45) | collective-permute-done | bytes 147488 | tf_op jit(solution)/shard_map/ppermute | solution.py:112
  217.7 1.6 collective-permute-done.51
  223.1 5.4 %collective-permute-done.64 = bf16[96,896]{1,0:T(8,128)(2,1)S(1)} collective-permute-done((bf16[96,896]{1,0:T(8,128)(2,1)S(1)}, bf16[96,896]{1,0:T(8,128)(2,1)S(1)}, u32[]{:S(2)}, u32[]{:S(2)}) %collective-permute-start.64) | collective-permute-done | bytes 172064 | tf_op jit(solution)/shard_map/ppermute | solution.py:102
  229.3 1.6 collective-permute-start.67
  232.3 1.6 collective-permute-start.82
  233.9 5.4 %backward.7 = (f32[96,768]{1,0:T(8,128)S(1)}, f32[96,768]{1,0:T(8,128)S(1)}, bf16[192,640]{1,0:T(8,128)(2,1)S(1)}, bf16[192,768]{1,0:T(8,128)(2,1)S(1)}, f32[8,768]{1,0:T(8,128)S(1)}) custom-call(bf16[96,768]{1,0:T(8,128)(2,1)S(1)} %get-tuple-element.255.own_ref.refs_11_, bf16[96,768]{1,0:T(8,128)(2,1)S(1)} %collective-permute-done.52.far_ref.refs_12_, ...), custom_call_target="tpu_custom_call" | custom-call | flops 8000000000 | bytes 10000000 | tf_op jit(solution)/shard_map/backward/pallas_call | solution.py:391
  239.5 5.4 %backward.5 = (f32[96,768]{1,0:T(8,128)S(1)}, f32[96,768]{1,0:T(8,128)S(1)}, bf16[192,640]{1,0:T(8,128)(2,1)S(1)}, bf16[192,768]{1,0:T(8,128)(2,1)S(1)}, f32[8,768]{1,0:T(8,128)S(1)}) custom-call(bf16[96,768]{1,0:T(8,128)(2,1)S(1)} %get-tuple-element.254.own_ref.refs_2_, bf16[96,768]{1,0:T(8,128)(2,1)S(1)} %collective-permute-done.46.far_ref.refs_3_, ...), custom_call_target="tpu_custom_call" | custom-call | flops 8000000000 | bytes 10000000 | tf_op jit(solution)/shard_map/backward/pallas_call | solution.py:391
  245.5 3.8 %weights.2 = (bf16[768,896]{1,0:T(8,128)(2,1)S(1)}, bf16[768,1536]{1,0:T(8,128)(2,1)}) custom-call(bf16[192,768]{1,0:T(8,128)(2,1)S(1)} %get-tuple-element.117.refs_0_, bf16[192,768]{1,0:T(8,128)(2,1)S(1)} %copy-done.9, bf16[96,768]{1,0:T(8,128)(2,1)S(1)} %get-tuple-element.254.own_ref.refs_2_, bf16[96,768]{1,0:T(8,128)(2,1)S(1)} %collective-permute-done.46.far_ref.refs_3_, ...), custom_call_target="tpu_custom_call" | custom-call | flops 8000000000 | bytes 10000000 | tf_op jit(solution)/shard_map/weights/pallas_call | solution.py:427
  252.0 5.0 %collective-permute-done.55 = bf16[96,896]{1,0:T(8,128)(2,1)S(1)} collective-permute-done((bf16[96,896]{1,0:T(8,128)(2,1)S(1)}, bf16[96,896]{1,0:T(8,128)(2,1)S(1)}, u32[]{:S(2)}, u32[]{:S(2)}) %collective-permute-start.55) | collective-permute-done | bytes 172064 | tf_op jit(solution)/shard_map/ppermute | solution.py:102
  259.1 7.2 %collective-permute-done.71 = bf16[96,1536]{1,0:T(8,128)(2,1)S(1)} collective-permute-done((bf16[96,1536]{1,0:T(8,128)(2,1)S(1)}, bf16[96,1536]{1,0:T(8,128)(2,1)S(1)}, u32[]{:S(2)}, u32[]{:S(2)}) %collective-permute-start.71) | collective-permute-done | bytes 294944 | tf_op jit(solution)/shard_map/ppermute | solution.py:102
  266.7 1.8 collective-permute-start.56
  268.5 2.0 collective-permute-start.54
  272.2 2.0 collective-permute-start.48
  277.3 1.7 collective-permute-start.57
  280.2 5.1 %collective-permute-done.57 = bf16[96,896]{1,0:T(8,128)(2,1)S(1)} collective-permute-done((bf16[96,896]{1,0:T(8,128)(2,1)S(1)}, bf16[96,896]{1,0:T(8,128)(2,1)S(1)}, u32[]{:S(2)}, u32[]{:S(2)}) %collective-permute-start.57) | collective-permute-done | bytes 172064 | tf_op jit(solution)/shard_map/ppermute | solution.py:102
  285.5 2.1 collective-permute-start.58
  288.4 7.7 %collective-permute-done.60 = bf16[96,896]{1,0:T(8,128)(2,1)S(1)} collective-permute-done((bf16[96,896]{1,0:T(8,128)(2,1)S(1)}, bf16[96,896]{1,0:T(8,128)(2,1)S(1)}, u32[]{:S(2)}, u32[]{:S(2)}) %collective-permute-start.60) | collective-permute-done | bytes 172064 | tf_op jit(solution)/shard_map/ppermute | solution.py:107
  297.1 2.0 collective-permute-start.80
  299.1 2.1 collective-permute-start.73
  301.2 7.1 %collective-permute-done.61 = bf16[96,896]{1,0:T(8,128)(2,1)S(1)} collective-permute-done((bf16[96,896]{1,0:T(8,128)(2,1)S(1)}, bf16[96,896]{1,0:T(8,128)(2,1)S(1)}, u32[]{:S(2)}, u32[]{:S(2)}) %collective-permute-start.61) | collective-permute-done | bytes 172064 | tf_op jit(solution)/shard_map/ppermute | solution.py:107
  309.3 2.6 collective-permute-start.69
  312.7 2.6 collective-permute-done.69
  317.4 2.4 collective-permute-done.76
  322.5 5.4 %collective-permute-done.77 = bf16[96,1536]{1,0:T(8,128)(2,1)S(1)} collective-permute-done((bf16[96,1536]{1,0:T(8,128)(2,1)S(1)}, bf16[96,1536]{1,0:T(8,128)(2,1)S(1)}, u32[]{:S(2)}, u32[]{:S(2)}) %collective-permute-start.77) | collective-permute-done | bytes 294944 | tf_op jit(solution)/shard_map/ppermute | solution.py:107
  329.4 2.1 collective-permute-start.85
  334.5 3.4 %collective-permute-done.85 = bf16[96,1536]{1,0:T(8,128)(2,1)S(1)} collective-permute-done((bf16[96,1536]{1,0:T(8,128)(2,1)S(1)}, bf16[96,1536]{1,0:T(8,128)(2,1)S(1)}, u32[]{:S(2)}, u32[]{:S(2)}) %collective-permute-start.85) | collective-permute-done | bytes 294944 | tf_op jit(solution)/shard_map/ppermute | solution.py:112
  (417 shorter events, 106.6 us)
Async XLA Ops:
  2.4 121.4 %collective-permute-start = (bf16[96,768]{1,0:T(8,128)(2,1)}, bf16[96,768]{1,0:T(8,128)(2,1)}, u32[]{:S(2)}, u32[]{:S(2)}) collective-permute-start(bf16[96,768]{1,0:T(8,128)(2,1)} %get-tuple-element.260.own_ref), channel_id=1, source_target_pairs={{0,1},{1,0},{2,3},{3,2},{4,5},{5,4},{6,7},{7,6},{8,9},{9,8},{10,11... | collective-permute-start | bytes 442376 | tf_op jit(solution)/shard_map/ppermute | solution.py:112
  6.6 19.2 %collective-permute-start.1 = (bf16[96,896]{1,0:T(8,128)(2,1)}, bf16[96,896]{1,0:T(8,128)(2,1)}, u32[]{:S(2)}, u32[]{:S(2)}) collective-permute-start(bf16[96,896]{1,0:T(8,128)(2,1)} %broadcast_select_fusion.6), channel_id=1, source_target_pairs={{0,16},{16,0},{1,17},{17,1},{2,18},{18,2},{3,19},{19,3},{4,20},{20... | collective-permute-start | bytes 516104 | tf_op jit(solution)/shard_map/ppermute | solution.py:112
  11.2 19.2 %collective-permute-start.9 = (bf16[96,1536]{1,0:T(8,128)(2,1)}, bf16[96,1536]{1,0:T(8,128)(2,1)}, u32[]{:S(2)}, u32[]{:S(2)}) collective-permute-start(bf16[96,1536]{1,0:T(8,128)(2,1)} %broadcast_select_fusion.2), channel_id=1, source_target_pairs={{0,16},{16,0},{1,17},{17,1},{2,18},{18,2},{3,19},{19,3},{4,20},{20... | collective-permute-start | bytes 884744 | tf_op jit(solution)/shard_map/ppermute | solution.py:112
  12.0 12.1 %collective-permute-start.17 = (bf16[1,1344]{1,0:T(2,128)(2,1)}, bf16[1,1344]{1,0:T(2,128)(2,1)}, u32[]{:S(2)}, u32[]{:S(2)}) collective-permute-start(bf16[1,1344]{1,0:T(2,128)(2,1)} %broadcast_select_fusion.10), channel_id=1, source_target_pairs={{0,16},{16,0},{1,17},{17,1},{2,18},{18,2},{3,19},{19,3},{4,20},{20... | collective-permute-start | bytes 8072 | tf_op jit(solution)/shard_map/ppermute | solution.py:112
  14.0 117.1 %collective-permute-start.20 = (bf16[96,768]{1,0:T(8,128)(2,1)S(1)}, bf16[96,768]{1,0:T(8,128)(2,1)}, u32[]{:S(2)}, u32[]{:S(2)}) collective-permute-start(bf16[96,768]{1,0:T(8,128)(2,1)S(1)} %get-tuple-element.261.own_ref), channel_id=1, source_target_pairs={{0,1},{1,0},{2,3},{3,2},{4,5},{5,4},{6,7},{7,6},{8,9},{9,8},{10,11... | collective-permute-start | bytes 442376 | tf_op jit(solution)/shard_map/ppermute | solution.py:112
  28.7 10.2 %collective-permute-start.3 = (bf16[96,896]{1,0:T(8,128)(2,1)S(1)}, bf16[96,896]{1,0:T(8,128)(2,1)S(1)}, u32[]{:S(2)}, u32[]{:S(2)}) collective-permute-start(bf16[96,896]{1,0:T(8,128)(2,1)S(1)} %get-tuple-element.223), channel_id=1, source_target_pairs={{4,0},{8,4},{12,8},{14,12},{10,14},{6,10},{2,6},{0,2},{5,1},{9,5},... | collective-permute-start | bytes 516104 | tf_op jit(solution)/shard_map/ppermute | solution.py:79
  37.3 26.1 %collective-permute-start.10 = (bf16[96,1536]{1,0:T(8,128)(2,1)S(1)}, bf16[96,1536]{1,0:T(8,128)(2,1)S(1)}, u32[]{:S(2)}, u32[]{:S(2)}) collective-permute-start(bf16[96,1536]{1,0:T(8,128)(2,1)S(1)} %get-tuple-element.221), channel_id=1, source_target_pairs={{0,4},{4,8},{8,12},{12,14},{14,10},{10,6},{6,2},{2,0},{1,5},{5,9},... | collective-permute-start | bytes 884744 | tf_op jit(solution)/shard_map/ppermute | solution.py:75
  38.9 12.0 %collective-permute-start.4 = (bf16[96,896]{1,0:T(8,128)(2,1)S(1)}, bf16[96,896]{1,0:T(8,128)(2,1)S(1)}, u32[]{:S(2)}, u32[]{:S(2)}) collective-permute-start(bf16[96,896]{1,0:T(8,128)(2,1)S(1)} %collective-permute-done.2), channel_id=1, source_target_pairs={{0,4},{4,8},{8,12},{12,14},{14,10},{10,6},{6,2},{2,0},{1,5},{5,9},... | collective-permute-start | bytes 516104 | tf_op jit(solution)/shard_map/ppermute | solution.py:75
  40.6 12.4 %collective-permute-start.26 = (bf16[96,896]{1,0:T(8,128)(2,1)S(1)}, bf16[96,896]{1,0:T(8,128)(2,1)S(1)}, u32[]{:S(2)}, u32[]{:S(2)}) collective-permute-start(bf16[96,896]{1,0:T(8,128)(2,1)S(1)} %collective-permute-done.24), channel_id=1, source_target_pairs={{0,4},{4,8},{8,12},{12,14},{14,10},{10,6},{6,2},{2,0},{1,5},{5,9},... | collective-permute-start | bytes 516104 | tf_op jit(solution)/shard_map/ppermute | solution.py:75
  53.0 8.8 %collective-permute-start.27 = (bf16[96,896]{1,0:T(8,128)(2,1)S(1)}, bf16[96,896]{1,0:T(8,128)(2,1)S(1)}, u32[]{:S(2)}, u32[]{:S(2)}) collective-permute-start(bf16[96,896]{1,0:T(8,128)(2,1)S(1)} %collective-permute-done.25), channel_id=1, source_target_pairs={{4,0},{8,4},{12,8},{14,12},{10,14},{6,10},{2,6},{0,2},{5,1},{9,5},... | collective-permute-start | bytes 516104 | tf_op jit(solution)/shard_map/ppermute | solution.py:79
  58.1 10.0 %collective-permute-start.11 = (bf16[96,1536]{1,0:T(8,128)(2,1)S(1)}, bf16[96,1536]{1,0:T(8,128)(2,1)S(1)}, u32[]{:S(2)}, u32[]{:S(2)}) collective-permute-start(bf16[96,1536]{1,0:T(8,128)(2,1)S(1)} %get-tuple-element.221), channel_id=1, source_target_pairs={{4,0},{8,4},{12,8},{14,12},{10,14},{6,10},{2,6},{0,2},{5,1},{9,5},... | collective-permute-start | bytes 884744 | tf_op jit(solution)/shard_map/ppermute | solution.py:79
  61.8 8.6 %collective-permute-start.31 = (bf16[96,1536]{1,0:T(8,128)(2,1)S(1)}, bf16[96,1536]{1,0:T(8,128)(2,1)S(1)}, u32[]{:S(2)}, u32[]{:S(2)}) collective-permute-start(bf16[96,1536]{1,0:T(8,128)(2,1)S(1)} %get-tuple-element.217), channel_id=1, source_target_pairs={{0,4},{4,8},{8,12},{12,14},{14,10},{10,6},{6,2},{2,0},{1,5},{5,9},... | collective-permute-start | bytes 884744 | tf_op jit(solution)/shard_map/ppermute | solution.py:75
  63.4 10.6 %collective-permute-start.32 = (bf16[96,1536]{1,0:T(8,128)(2,1)S(1)}, bf16[96,1536]{1,0:T(8,128)(2,1)S(1)}, u32[]{:S(2)}, u32[]{:S(2)}) collective-permute-start(bf16[96,1536]{1,0:T(8,128)(2,1)S(1)} %get-tuple-element.217), channel_id=1, source_target_pairs={{4,0},{8,4},{12,8},{14,12},{10,14},{6,10},{2,6},{0,2},{5,1},{9,5},... | collective-permute-start | bytes 884744 | tf_op jit(solution)/shard_map/ppermute | solution.py:79
  68.1 7.5 %collective-permute-start.6 = (bf16[96,896]{1,0:T(8,128)(2,1)S(1)}, bf16[96,896]{1,0:T(8,128)(2,1)S(1)}, u32[]{:S(2)}, u32[]{:S(2)}) collective-permute-start(bf16[96,896]{1,0:T(8,128)(2,1)S(1)} %collective-permute-done.4), channel_id=1, source_target_pairs={{0,4},{4,8},{8,12},{12,14},{14,10},{10,6},{6,2},{2,0},{1,5},{5,9},... | collective-permute-start | bytes 516104 | tf_op jit(solution)/shard_map/ppermute | solution.py:75
  70.4 12.1 %collective-permute-start.7 = (bf16[96,896]{1,0:T(8,128)(2,1)S(1)}, bf16[96,896]{1,0:T(8,128)(2,1)S(1)}, u32[]{:S(2)}, u32[]{:S(2)}) collective-permute-start(bf16[96,896]{1,0:T(8,128)(2,1)S(1)} %collective-permute-done.5), channel_id=1, source_target_pairs={{4,0},{8,4},{12,8},{14,12},{10,14},{6,10},{2,6},{0,2},{5,1},{9,5},... | collective-permute-start | bytes 516104 | tf_op jit(solution)/shard_map/ppermute | solution.py:79
  75.6 8.5 %collective-permute-start.29 = (bf16[96,896]{1,0:T(8,128)(2,1)S(1)}, bf16[96,896]{1,0:T(8,128)(2,1)S(1)}, u32[]{:S(2)}, u32[]{:S(2)}) collective-permute-start(bf16[96,896]{1,0:T(8,128)(2,1)S(1)} %collective-permute-done.27), channel_id=1, source_target_pairs={{4,0},{8,4},{12,8},{14,12},{10,14},{6,10},{2,6},{0,2},{5,1},{9,5},... | collective-permute-start | bytes 516104 | tf_op jit(solution)/shard_map/ppermute | solution.py:79
  80.8 16.2 %collective-permute-start.12 = (bf16[96,1536]{1,0:T(8,128)(2,1)S(1)}, bf16[96,1536]{1,0:T(8,128)(2,1)S(1)}, u32[]{:S(2)}, u32[]{:S(2)}) collective-permute-start(bf16[96,1536]{1,0:T(8,128)(2,1)S(1)} %collective-permute-done.10), channel_id=1, source_target_pairs={{0,4},{4,8},{8,12},{12,14},{14,10},{10,6},{6,2},{2,0},{1,5},{5,9},... | collective-permute-start | bytes 884744 | tf_op jit(solution)/shard_map/ppermute | solution.py:75
  82.4 9.4 %collective-permute-start.8 = (bf16[96,896]{1,0:T(8,128)(2,1)S(1)}, bf16[96,896]{1,0:T(8,128)(2,1)S(1)}, u32[]{:S(2)}, u32[]{:S(2)}) collective-permute-start(bf16[96,896]{1,0:T(8,128)(2,1)S(1)} %collective-permute-done.6), channel_id=1, source_target_pairs={{0,4},{4,8},{8,12},{12,14},{14,10},{10,6},{6,2},{2,0},{1,5},{5,9},... | collective-permute-start | bytes 516104 | tf_op jit(solution)/shard_map/ppermute | solution.py:75
  84.1 11.4 %collective-permute-start.30 = (bf16[96,896]{1,0:T(8,128)(2,1)S(1)}, bf16[96,896]{1,0:T(8,128)(2,1)S(1)}, u32[]{:S(2)}, u32[]{:S(2)}) collective-permute-start(bf16[96,896]{1,0:T(8,128)(2,1)S(1)} %collective-permute-done.28), channel_id=1, source_target_pairs={{0,4},{4,8},{8,12},{12,14},{14,10},{10,6},{6,2},{2,0},{1,5},{5,9},... | collective-permute-start | bytes 516104 | tf_op jit(solution)/shard_map/ppermute | solution.py:75
  95.6 8.9 %collective-permute-start.33 = (bf16[96,1536]{1,0:T(8,128)(2,1)S(1)}, bf16[96,1536]{1,0:T(8,128)(2,1)S(1)}, u32[]{:S(2)}, u32[]{:S(2)}) collective-permute-start(bf16[96,1536]{1,0:T(8,128)(2,1)S(1)} %collective-permute-done.31), channel_id=1, source_target_pairs={{0,4},{4,8},{8,12},{12,14},{14,10},{10,6},{6,2},{2,0},{1,5},{5,9},... | collective-permute-start | bytes 884744 | tf_op jit(solution)/shard_map/ppermute | solution.py:75
  97.0 10.0 %collective-permute-start.34 = (bf16[96,1536]{1,0:T(8,128)(2,1)S(1)}, bf16[96,1536]{1,0:T(8,128)(2,1)S(1)}, u32[]{:S(2)}, u32[]{:S(2)}) collective-permute-start(bf16[96,1536]{1,0:T(8,128)(2,1)S(1)} %collective-permute-done.32), channel_id=1, source_target_pairs={{4,0},{8,4},{12,8},{14,12},{10,14},{6,10},{2,6},{0,2},{5,1},{9,5},... | collective-permute-start | bytes 884744 | tf_op jit(solution)/shard_map/ppermute | solution.py:79
  98.6 10.3 %collective-permute-start.14 = (bf16[96,1536]{1,0:T(8,128)(2,1)S(1)}, bf16[96,1536]{1,0:T(8,128)(2,1)S(1)}, u32[]{:S(2)}, u32[]{:S(2)}) collective-permute-start(bf16[96,1536]{1,0:T(8,128)(2,1)S(1)} %collective-permute-done.12), channel_id=1, source_target_pairs={{0,4},{4,8},{8,12},{12,14},{14,10},{10,6},{6,2},{2,0},{1,5},{5,9},... | collective-permute-start | bytes 884744 | tf_op jit(solution)/shard_map/ppermute | solution.py:75
  104.4 10.4 %collective-permute-start.15 = (bf16[96,1536]{1,0:T(8,128)(2,1)S(1)}, bf16[96,1536]{1,0:T(8,128)(2,1)S(1)}, u32[]{:S(2)}, u32[]{:S(2)}) collective-permute-start(bf16[96,1536]{1,0:T(8,128)(2,1)S(1)} %collective-permute-done.13), channel_id=1, source_target_pairs={{4,0},{8,4},{12,8},{14,12},{10,14},{6,10},{2,6},{0,2},{5,1},{9,5},... | collective-permute-start | bytes 884744 | tf_op jit(solution)/shard_map/ppermute | solution.py:79
  107.0 9.8 %collective-permute-start.35 = (bf16[96,1536]{1,0:T(8,128)(2,1)S(1)}, bf16[96,1536]{1,0:T(8,128)(2,1)S(1)}, u32[]{:S(2)}, u32[]{:S(2)}) collective-permute-start(bf16[96,1536]{1,0:T(8,128)(2,1)S(1)} %collective-permute-done.33), channel_id=1, source_target_pairs={{0,4},{4,8},{8,12},{12,14},{14,10},{10,6},{6,2},{2,0},{1,5},{5,9},... | collective-permute-start | bytes 884744 | tf_op jit(solution)/shard_map/ppermute | solution.py:75
  108.9 9.0 %collective-permute-start.36 = (bf16[96,1536]{1,0:T(8,128)(2,1)S(1)}, bf16[96,1536]{1,0:T(8,128)(2,1)S(1)}, u32[]{:S(2)}, u32[]{:S(2)}) collective-permute-start(bf16[96,1536]{1,0:T(8,128)(2,1)S(1)} %collective-permute-done.34), channel_id=1, source_target_pairs={{4,0},{8,4},{12,8},{14,12},{10,14},{6,10},{2,6},{0,2},{5,1},{9,5},... | collective-permute-start | bytes 884744 | tf_op jit(solution)/shard_map/ppermute | solution.py:79
  116.8 43.3 %collective-permute-start.43 = (bf16[96,768]{1,0:T(8,128)(2,1)S(1)}, bf16[96,768]{1,0:T(8,128)(2,1)S(1)}, u32[]{:S(2)}, u32[]{:S(2)}) collective-permute-start(bf16[96,768]{1,0:T(8,128)(2,1)S(1)} %copy-done.4), channel_id=1, source_target_pairs={{0,1},{1,0},{2,3},{3,2},{4,5},{5,4},{6,7},{7,6},{8,9},{9,8},{10,11... | collective-permute-start | bytes 442376 | tf_op jit(solution)/shard_map/ppermute | solution.py:112
  118.0 50.3 %collective-permute-start.49 = (bf16[96,768]{1,0:T(8,128)(2,1)S(1)}, bf16[96,768]{1,0:T(8,128)(2,1)S(1)}, u32[]{:S(2)}, u32[]{:S(2)}) collective-permute-start(bf16[96,768]{1,0:T(8,128)(2,1)S(1)} %copy-done.5), channel_id=1, source_target_pairs={{0,1},{1,0},{2,3},{3,2},{4,5},{5,4},{6,7},{7,6},{8,9},{9,8},{10,11... | collective-permute-start | bytes 442376 | tf_op jit(solution)/shard_map/ppermute | solution.py:112
  121.7 23.9 %collective-permute-start.37 = (bf16[96,1536]{1,0:T(8,128)(2,1)S(1)}, bf16[96,1536]{1,0:T(8,128)(2,1)S(1)}, u32[]{:S(2)}, u32[]{:S(2)}) collective-permute-start(bf16[96,1536]{1,0:T(8,128)(2,1)S(1)} %collective-permute-done.36), channel_id=1, source_target_pairs={{4,0},{8,4},{12,8},{14,12},{10,14},{6,10},{2,6},{0,2},{5,1},{9,5},... | collective-permute-start | bytes 884744 | tf_op jit(solution)/shard_map/ppermute | solution.py:79
  137.4 7.9 %collective-permute-start.22 = (bf16[96,768]{1,0:T(8,128)(2,1)S(1)}, bf16[96,768]{1,0:T(8,128)(2,1)S(1)}, u32[]{:S(2)}, u32[]{:S(2)}) collective-permute-start(bf16[96,768]{1,0:T(8,128)(2,1)S(1)} %add_convert_fusion.33), channel_id=1, source_target_pairs={{0,16},{16,0},{1,17},{17,1},{2,18},{18,2},{3,19},{19,3},{4,20},{20... | collective-permute-start | bytes 442376 | tf_op jit(solution)/shard_map/ppermute | solution.py:112
  145.7 7.7 %collective-permute-start.23 = (bf16[96,768]{1,0:T(8,128)(2,1)S(1)}, bf16[96,768]{1,0:T(8,128)(2,1)S(1)}, u32[]{:S(2)}, u32[]{:S(2)}) collective-permute-start(bf16[96,768]{1,0:T(8,128)(2,1)S(1)} %get-tuple-element.258.own_ref), channel_id=1, source_target_pairs={{0,1},{1,0},{2,3},{3,2},{4,5},{5,4},{6,7},{7,6},{8,9},{9,8},{10,11... | collective-permute-start | bytes 442376 | tf_op jit(solution)/shard_map/ppermute | solution.py:112
  152.8 52.1 %collective-permute-start.41 = (f32[96,768]{1,0:T(8,128)S(1)}, f32[96,768]{1,0:T(8,128)S(1)}, u32[]{:S(2)}, u32[]{:S(2)}) collective-permute-start(f32[96,768]{1,0:T(8,128)S(1)} %get-tuple-element.92), channel_id=1, source_target_pairs={{0,1},{1,0},{2,3},{3,2},{4,5},{5,4},{6,7},{7,6},{8,9},{9,8},{10,11... | collective-permute-start | bytes 884744 | tf_op jit(solution)/shard_map/ppermute | solution.py:112
  159.9 46.7 %collective-permute-start.38 = (f32[96,768]{1,0:T(8,128)S(1)}, f32[96,768]{1,0:T(8,128)S(1)}, u32[]{:S(2)}, u32[]{:S(2)}) collective-permute-start(f32[96,768]{1,0:T(8,128)S(1)} %get-tuple-element.89), channel_id=1, source_target_pairs={{0,1},{1,0},{2,3},{3,2},{4,5},{5,4},{6,7},{7,6},{8,9},{9,8},{10,11... | collective-permute-start | bytes 884744 | tf_op jit(solution)/shard_map/ppermute | solution.py:112
  167.9 39.3 %collective-permute-start.44 = (f32[96,768]{1,0:T(8,128)S(1)}, f32[96,768]{1,0:T(8,128)}, u32[]{:S(2)}, u32[]{:S(2)}) collective-permute-start(f32[96,768]{1,0:T(8,128)S(1)} %get-tuple-element.98), channel_id=1, source_target_pairs={{0,1},{1,0},{2,3},{3,2},{4,5},{5,4},{6,7},{7,6},{8,9},{9,8},{10,11... | collective-permute-start | bytes 884744 | tf_op jit(solution)/shard_map/ppermute | solution.py:112
  192.0 11.3 %collective-permute-start.78 = (bf16[96,1536]{1,0:T(8,128)(2,1)S(1)}, bf16[96,1536]{1,0:T(8,128)(2,1)S(1)}, u32[]{:S(2)}, u32[]{:S(2)}) collective-permute-start(bf16[96,1536]{1,0:T(8,128)(2,1)S(1)} %get-tuple-element.230), channel_id=1, source_target_pairs={{0,4},{4,8},{8,12},{12,14},{14,10},{10,6},{6,2},{2,0},{1,5},{5,9},... | collective-permute-start | bytes 884744 | tf_op jit(solution)/shard_map/ppermute | solution.py:102
  197.8 11.0 %collective-permute-start.50 = (f32[96,768]{1,0:T(8,128)S(1)}, f32[96,768]{1,0:T(8,128)S(1)}, u32[]{:S(2)}, u32[]{:S(2)}) collective-permute-start(f32[96,768]{1,0:T(8,128)S(1)} %get-tuple-element.110), channel_id=1, source_target_pairs={{0,1},{1,0},{2,3},{3,2},{4,5},{5,4},{6,7},{7,6},{8,9},{9,8},{10,11... | collective-permute-start | bytes 884744 | tf_op jit(solution)/shard_map/ppermute | solution.py:112
  203.3 19.3 %collective-permute-start.66 = (bf16[96,896]{1,0:T(8,128)(2,1)S(1)}, bf16[96,896]{1,0:T(8,128)(2,1)S(1)}, u32[]{:S(2)}, u32[]{:S(2)}) collective-permute-start(bf16[96,896]{1,0:T(8,128)(2,1)S(1)} %get-tuple-element.239), channel_id=1, source_target_pairs={{4,0},{8,4},{12,8},{14,12},{10,14},{6,10},{2,6},{0,2},{5,1},{9,5},... | collective-permute-start | bytes 516104 | tf_op jit(solution)/shard_map/ppermute | solution.py:107
  205.0 26.0 %collective-permute-start.81 = (bf16[96,1536]{1,0:T(8,128)(2,1)S(1)}, bf16[96,1536]{1,0:T(8,128)(2,1)S(1)}, u32[]{:S(2)}, u32[]{:S(2)}) collective-permute-start(bf16[96,1536]{1,0:T(8,128)(2,1)S(1)} %get-tuple-element.231), channel_id=1, source_target_pairs={{4,0},{8,4},{12,8},{14,12},{10,14},{6,10},{2,6},{0,2},{5,1},{9,5},... | collective-permute-start | bytes 884744 | tf_op jit(solution)/shard_map/ppermute | solution.py:107
  207.2 12.8 %collective-permute-start.42 = (bf16[96,768]{1,0:T(8,128)(2,1)S(1)}, bf16[96,768]{1,0:T(8,128)(2,1)S(1)}, u32[]{:S(2)}, u32[]{:S(2)}) collective-permute-start(bf16[96,768]{1,0:T(8,128)(2,1)S(1)} %add_convert_fusion.29), channel_id=1, source_target_pairs={{0,16},{16,0},{1,17},{17,1},{2,18},{18,2},{3,19},{19,3},{4,20},{20... | collective-permute-start | bytes 442376 | tf_op jit(solution)/shard_map/ppermute | solution.py:112
  208.9 7.7 %collective-permute-start.45 = (bf16[96,768]{1,0:T(8,128)(2,1)S(1)}, bf16[96,768]{1,0:T(8,128)(2,1)S(1)}, u32[]{:S(2)}, u32[]{:S(2)}) collective-permute-start(bf16[96,768]{1,0:T(8,128)(2,1)S(1)} %add_convert_fusion.27), channel_id=1, source_target_pairs={{0,16},{16,0},{1,17},{17,1},{2,18},{18,2},{3,19},{19,3},{4,20},{20... | collective-permute-start | bytes 442376 | tf_op jit(solution)/shard_map/ppermute | solution.py:112
  219.4 12.0 %collective-permute-start.79 = (bf16[96,1536]{1,0:T(8,128)(2,1)S(1)}, bf16[96,1536]{1,0:T(8,128)(2,1)S(1)}, u32[]{:S(2)}, u32[]{:S(2)}) collective-permute-start(bf16[96,1536]{1,0:T(8,128)(2,1)S(1)} %add_convert_fusion.4), channel_id=1, source_target_pairs={{0,4},{4,8},{8,12},{12,14},{14,10},{10,6},{6,2},{2,0},{1,5},{5,9},... | collective-permute-start | bytes 884744 | tf_op jit(solution)/shard_map/ppermute | solution.py:102
  220.0 8.5 %collective-permute-start.64 = (bf16[96,896]{1,0:T(8,128)(2,1)S(1)}, bf16[96,896]{1,0:T(8,128)(2,1)S(1)}, u32[]{:S(2)}, u32[]{:S(2)}) collective-permute-start(bf16[96,896]{1,0:T(8,128)(2,1)S(1)} %add_convert_fusion.13), channel_id=1, source_target_pairs={{0,4},{4,8},{8,12},{12,14},{14,10},{10,6},{6,2},{2,0},{1,5},{5,9},... | collective-permute-start | bytes 516104 | tf_op jit(solution)/shard_map/ppermute | solution.py:102
  221.7 12.1 %collective-permute-start.52 = (bf16[96,768]{1,0:T(8,128)(2,1)S(1)}, bf16[96,768]{1,0:T(8,128)(2,1)S(1)}, u32[]{:S(2)}, u32[]{:S(2)}) collective-permute-start(bf16[96,768]{1,0:T(8,128)(2,1)S(1)} %get-tuple-element.255.own_ref.refs_11_), channel_id=1, source_target_pairs={{0,1},{1,0},{2,3},{3,2},{4,5},{5,4},{6,7},{7,6},{8,9},{9,8},{10,11... | collective-permute-start | bytes 442376 | tf_op jit(solution)/shard_map/ppermute | solution.py:112
  222.6 16.8 %collective-permute-start.46 = (bf16[96,768]{1,0:T(8,128)(2,1)S(1)}, bf16[96,768]{1,0:T(8,128)(2,1)S(1)}, u32[]{:S(2)}, u32[]{:S(2)}) collective-permute-start(bf16[96,768]{1,0:T(8,128)(2,1)S(1)} %get-tuple-element.254.own_ref.refs_2_), channel_id=1, source_target_pairs={{0,1},{1,0},{2,3},{3,2},{4,5},{5,4},{6,7},{7,6},{8,9},{9,8},{10,11... | collective-permute-start | bytes 442376 | tf_op jit(solution)/shard_map/ppermute | solution.py:112
  229.3 21.2 %collective-permute-start.67 = (bf16[96,896]{1,0:T(8,128)(2,1)}, bf16[96,896]{1,0:T(8,128)(2,1)}, u32[]{:S(2)}, u32[]{:S(2)}) collective-permute-start(bf16[96,896]{1,0:T(8,128)(2,1)} %get-tuple-element.237), channel_id=1, source_target_pairs={{4,0},{8,4},{12,8},{14,12},{10,14},{6,10},{2,6},{0,2},{5,1},{9,5},... | collective-permute-start | bytes 516104 | tf_op jit(solution)/shard_map/ppermute | solution.py:107
  231.0 66.1 %collective-permute-start.65 = (bf16[96,896]{1,0:T(8,128)(2,1)}, bf16[96,896]{1,0:T(8,128)(2,1)}, u32[]{:S(2)}, u32[]{:S(2)}) collective-permute-start(bf16[96,896]{1,0:T(8,128)(2,1)} %get-tuple-element.236), channel_id=1, source_target_pairs={{0,4},{4,8},{8,12},{12,14},{14,10},{10,6},{6,2},{2,0},{1,5},{5,9},... | collective-permute-start | bytes 516104 | tf_op jit(solution)/shard_map/ppermute | solution.py:102
  232.3 26.2 %collective-permute-start.82 = (bf16[96,1536]{1,0:T(8,128)(2,1)S(1)}, bf16[96,1536]{1,0:T(8,128)(2,1)S(1)}, u32[]{:S(2)}, u32[]{:S(2)}) collective-permute-start(bf16[96,1536]{1,0:T(8,128)(2,1)S(1)} %get-tuple-element.229), channel_id=1, source_target_pairs={{4,0},{8,4},{12,8},{14,12},{10,14},{6,10},{2,6},{0,2},{5,1},{9,5},... | collective-permute-start | bytes 884744 | tf_op jit(solution)/shard_map/ppermute | solution.py:107
  239.3 27.4 %collective-permute-start.53 = (f32[96,768]{1,0:T(8,128)S(1)}, f32[96,768]{1,0:T(8,128)S(1)}, u32[]{:S(2)}, u32[]{:S(2)}) collective-permute-start(f32[96,768]{1,0:T(8,128)S(1)} %get-tuple-element.116), channel_id=1, source_target_pairs={{0,1},{1,0},{2,3},{3,2},{4,5},{5,4},{6,7},{7,6},{8,9},{9,8},{10,11... | collective-permute-start | bytes 884744 | tf_op jit(solution)/shard_map/ppermute | solution.py:112
  244.9 23.6 %collective-permute-start.47 = (f32[96,768]{1,0:T(8,128)S(1)}, f32[96,768]{1,0:T(8,128)S(1)}, u32[]{:S(2)}, u32[]{:S(2)}) collective-permute-start(f32[96,768]{1,0:T(8,128)S(1)} %get-tuple-element.104), channel_id=1, source_target_pairs={{0,1},{1,0},{2,3},{3,2},{4,5},{5,4},{6,7},{7,6},{8,9},{9,8},{10,11... | collective-permute-start | bytes 884744 | tf_op jit(solution)/shard_map/ppermute | solution.py:112
  256.9 23.0 %collective-permute-start.59 = (bf16[96,896]{1,0:T(8,128)(2,1)S(1)}, bf16[96,896]{1,0:T(8,128)(2,1)S(1)}, u32[]{:S(2)}, u32[]{:S(2)}) collective-permute-start(bf16[96,896]{1,0:T(8,128)(2,1)S(1)} %get-tuple-element.243), channel_id=1, source_target_pairs={{4,0},{8,4},{12,8},{14,12},{10,14},{6,10},{2,6},{0,2},{5,1},{9,5},... | collective-permute-start | bytes 516104 | tf_op jit(solution)/shard_map/ppermute | solution.py:107
  258.4 7.9 %collective-permute-start.71 = (bf16[96,1536]{1,0:T(8,128)(2,1)S(1)}, bf16[96,1536]{1,0:T(8,128)(2,1)S(1)}, u32[]{:S(2)}, u32[]{:S(2)}) collective-permute-start(bf16[96,1536]{1,0:T(8,128)(2,1)S(1)} %get-tuple-element.234), channel_id=1, source_target_pairs={{0,4},{4,8},{8,12},{12,14},{14,10},{10,6},{6,2},{2,0},{1,5},{5,9},... | collective-permute-start | bytes 884744 | tf_op jit(solution)/shard_map/ppermute | solution.py:102
  266.3 19.1 %collective-permute-start.74 = (bf16[96,1536]{1,0:T(8,128)(2,1)S(1)}, bf16[96,1536]{1,0:T(8,128)(2,1)S(1)}, u32[]{:S(2)}, u32[]{:S(2)}) collective-permute-start(bf16[96,1536]{1,0:T(8,128)(2,1)S(1)} %get-tuple-element.235), channel_id=1, source_target_pairs={{4,0},{8,4},{12,8},{14,12},{10,14},{6,10},{2,6},{0,2},{5,1},{9,5},... | collective-permute-start | bytes 884744 | tf_op jit(solution)/shard_map/ppermute | solution.py:107
  274.9 10.6 %collective-permute-start.72 = (bf16[96,1536]{1,0:T(8,128)(2,1)S(1)}, bf16[96,1536]{1,0:T(8,128)(2,1)S(1)}, u32[]{:S(2)}, u32[]{:S(2)}) collective-permute-start(bf16[96,1536]{1,0:T(8,128)(2,1)S(1)} %add_convert_fusion.9), channel_id=1, source_target_pairs={{0,4},{4,8},{8,12},{12,14},{14,10},{10,6},{6,2},{2,0},{1,5},{5,9},... | collective-permute-start | bytes 884744 | tf_op jit(solution)/shard_map/ppermute | solution.py:102
  277.3 8.0 %collective-permute-start.57 = (bf16[96,896]{1,0:T(8,128)(2,1)S(1)}, bf16[96,896]{1,0:T(8,128)(2,1)S(1)}, u32[]{:S(2)}, u32[]{:S(2)}) collective-permute-start(bf16[96,896]{1,0:T(8,128)(2,1)S(1)} %add_convert_fusion.18), channel_id=1, source_target_pairs={{0,4},{4,8},{8,12},{12,14},{14,10},{10,6},{6,2},{2,0},{1,5},{5,9},... | collective-permute-start | bytes 516104 | tf_op jit(solution)/shard_map/ppermute | solution.py:102
  279.9 19.2 %collective-permute-start.68 = (bf16[96,896]{1,0:T(8,128)(2,1)S(1)}, bf16[96,896]{1,0:T(8,128)(2,1)S(1)}, u32[]{:S(2)}, u32[]{:S(2)}) collective-permute-start(bf16[96,896]{1,0:T(8,128)(2,1)S(1)} %add_convert_fusion.10), channel_id=1, source_target_pairs={{4,0},{8,4},{12,8},{14,12},{10,14},{6,10},{2,6},{0,2},{5,1},{9,5},... | collective-permute-start | bytes 516104 | tf_op jit(solution)/shard_map/ppermute | solution.py:107
  285.3 10.9 %collective-permute-start.83 = (bf16[96,1536]{1,0:T(8,128)(2,1)S(1)}, bf16[96,1536]{1,0:T(8,128)(2,1)S(1)}, u32[]{:S(2)}, u32[]{:S(2)}) collective-permute-start(bf16[96,1536]{1,0:T(8,128)(2,1)S(1)} %add_convert_fusion.1), channel_id=1, source_target_pairs={{4,0},{8,4},{12,8},{14,12},{10,14},{6,10},{2,6},{0,2},{5,1},{9,5},... | collective-permute-start | bytes 884744 | tf_op jit(solution)/shard_map/ppermute | solution.py:107
  285.4 10.7 %collective-permute-start.60 = (bf16[96,896]{1,0:T(8,128)(2,1)S(1)}, bf16[96,896]{1,0:T(8,128)(2,1)S(1)}, u32[]{:S(2)}, u32[]{:S(2)}) collective-permute-start(bf16[96,896]{1,0:T(8,128)(2,1)S(1)} %get-tuple-element.241), channel_id=1, source_target_pairs={{4,0},{8,4},{12,8},{14,12},{10,14},{6,10},{2,6},{0,2},{5,1},{9,5},... | collective-permute-start | bytes 516104 | tf_op jit(solution)/shard_map/ppermute | solution.py:107
  285.5 13.6 %collective-permute-start.58 = (bf16[96,896]{1,0:T(8,128)(2,1)S(1)}, bf16[96,896]{1,0:T(8,128)(2,1)S(1)}, u32[]{:S(2)}, u32[]{:S(2)}) collective-permute-start(bf16[96,896]{1,0:T(8,128)(2,1)S(1)} %get-tuple-element.240), channel_id=1, source_target_pairs={{0,4},{4,8},{8,12},{12,14},{14,10},{10,6},{6,2},{2,0},{1,5},{5,9},... | collective-permute-start | bytes 516104 | tf_op jit(solution)/shard_map/ppermute | solution.py:102
  296.1 15.8 %collective-permute-start.75 = (bf16[96,1536]{1,0:T(8,128)(2,1)S(1)}, bf16[96,1536]{1,0:T(8,128)(2,1)S(1)}, u32[]{:S(2)}, u32[]{:S(2)}) collective-permute-start(bf16[96,1536]{1,0:T(8,128)(2,1)S(1)} %get-tuple-element.233), channel_id=1, source_target_pairs={{4,0},{8,4},{12,8},{14,12},{10,14},{6,10},{2,6},{0,2},{5,1},{9,5},... | collective-permute-start | bytes 884744 | tf_op jit(solution)/shard_map/ppermute | solution.py:107
  296.2 12.0 %collective-permute-start.61 = (bf16[96,896]{1,0:T(8,128)(2,1)S(1)}, bf16[96,896]{1,0:T(8,128)(2,1)S(1)}, u32[]{:S(2)}, u32[]{:S(2)}) collective-permute-start(bf16[96,896]{1,0:T(8,128)(2,1)S(1)} %add_convert_fusion.15), channel_id=1, source_target_pairs={{4,0},{8,4},{12,8},{14,12},{10,14},{6,10},{2,6},{0,2},{5,1},{9,5},... | collective-permute-start | bytes 516104 | tf_op jit(solution)/shard_map/ppermute | solution.py:107
  297.1 25.4 %collective-permute-start.80 = (bf16[96,1536]{1,0:T(8,128)(2,1)}, bf16[96,1536]{1,0:T(8,128)(2,1)}, u32[]{:S(2)}, u32[]{:S(2)}) collective-permute-start(bf16[96,1536]{1,0:T(8,128)(2,1)} %get-tuple-element.228), channel_id=1, source_target_pairs={{0,4},{4,8},{8,12},{12,14},{14,10},{10,6},{6,2},{2,0},{1,5},{5,9},... | collective-permute-start | bytes 884744 | tf_op jit(solution)/shard_map/ppermute | solution.py:102
  299.1 23.4 %collective-permute-start.84 = (bf16[96,1536]{1,0:T(8,128)(2,1)}, bf16[96,1536]{1,0:T(8,128)(2,1)}, u32[]{:S(2)}, u32[]{:S(2)}) collective-permute-start(bf16[96,1536]{1,0:T(8,128)(2,1)} %add_convert_fusion), channel_id=1, source_target_pairs={{4,0},{8,4},{12,8},{14,12},{10,14},{6,10},{2,6},{0,2},{5,1},{9,5},... | collective-permute-start | bytes 884744 | tf_op jit(solution)/shard_map/ppermute | solution.py:107
  299.1 23.4 %collective-permute-start.73 = (bf16[96,1536]{1,0:T(8,128)(2,1)}, bf16[96,1536]{1,0:T(8,128)(2,1)}, u32[]{:S(2)}, u32[]{:S(2)}) collective-permute-start(bf16[96,1536]{1,0:T(8,128)(2,1)} %get-tuple-element.232), channel_id=1, source_target_pairs={{0,4},{4,8},{8,12},{12,14},{14,10},{10,6},{6,2},{2,0},{1,5},{5,9},... | collective-permute-start | bytes 884744 | tf_op jit(solution)/shard_map/ppermute | solution.py:102
  316.0 15.4 %collective-permute-start.70 = (f32[96,8]{1,0:T(8,128)S(1)}, f32[96,8]{1,0:T(8,128)S(1)}, u32[]{:S(2)}, u32[]{:S(2)}) collective-permute-start(f32[96,8]{1,0:T(8,128)S(1)} %slice_add_fusion), channel_id=1, source_target_pairs={{0,1},{1,0},{2,3},{3,2},{4,5},{5,4},{6,7},{7,6},{8,9},{9,8},{10,11... | collective-permute-start | bytes 9224 | tf_op jit(solution)/shard_map/ppermute | solution.py:112
  329.4 8.6 %collective-permute-start.85 = (bf16[96,1536]{1,0:T(8,128)(2,1)S(1)}, bf16[96,1536]{1,0:T(8,128)(2,1)S(1)}, u32[]{:S(2)}, u32[]{:S(2)}) collective-permute-start(bf16[96,1536]{1,0:T(8,128)(2,1)S(1)} %get-tuple-element.225), channel_id=1, source_target_pairs={{0,16},{16,0},{1,17},{17,1},{2,18},{18,2},{3,19},{19,3},{4,20},{20... | collective-permute-start | bytes 884744 | tf_op jit(solution)/shard_map/ppermute | solution.py:112
  (98 other events, 840.2 us)

commit v2 on v1

--- a/solution.py
+++ b/solution.py
@@ -12,10 +12,11 @@
 ROT = 16
 EPSILON = 1e-05
 NEG_BIG = -1e30
-VMEM_LIMIT = 48 * 1024 * 1024
+VMEM_LIMIT = 16 * 1024 * 1024
 BF = jnp.bfloat16
 F32 = jnp.float32
 SMALL = 128
+TIES = 2
 
 
 def ring_device(place, count):
@@ -60,52 +61,96 @@
     return ahead, [(target, source) for source, target in ahead]
 
 
-def ring_gather(chunk, forward_steps):
-    count = lax.axis_size("dp")
-    ahead, behind = ring_routes(count)
-    me = lax.axis_index("dp")
-    place = ring_place(me, count)
-    depth, width = chunk.shape
-    whole = jnp.zeros((count * depth, width), chunk.dtype)
-    whole = lax.dynamic_update_slice(whole, chunk, (me * depth, 0))
-    backward_steps = count - 1 - forward_steps
-    front = back = chunk
-    for step in range(1, max(forward_steps, backward_steps) + 1):
-        if step <= forward_steps:
-            front = lax.ppermute(front, "dp", ahead)
-            owner = ring_device((place + count - step) % count, count)
-            whole = lax.dynamic_update_slice(whole, front, (owner * depth, 0))
-        if step <= backward_steps:
-            back = lax.ppermute(back, "dp", behind)
-            owner = ring_device((place + step) % count, count)
-            whole = lax.dynamic_update_slice(whole, back, (owner * depth, 0))
-    return whole
-
-
-def ring_scatter(terms, forward_steps):
-    count = lax.axis_size("dp")
-    ahead, behind = ring_routes(count)
-    place = ring_place(lax.axis_index("dp"), count)
-    depth = terms.shape[0] // count
-    backward_steps = count - 1 - forward_steps
-
-    def term(distance):
-        owner = ring_device((place + count + distance) % count, count)
-        return lax.dynamic_slice(terms, (owner * depth, 0), (depth, terms.shape[1]))
-
-    front = back = None
-    for step in range(max(forward_steps, backward_steps)):
-        if step < forward_steps:
-            own = term(forward_steps - step)
+def after(value, *earlier):
+    return lax.optimization_barrier((value, *earlier))[0]
+
+
+def tie(values, earlier):
+    present = [item for item in values if item is not None]
+    if not earlier or not present:
+        return values
+    tied = list(lax.optimization_barrier((*present, *earlier))[: len(present)])
+    return [None if item is None else tied.pop(0) for item in values]
+
+
+class RingGather:
+    def __init__(self, chunk, whole, forward_steps):
+        self.count = lax.axis_size("dp")
+        self.ahead, self.behind = ring_routes(self.count)
+        self.place = ring_place(lax.axis_index("dp"), self.count)
+        self.depth = chunk.shape[0]
+        self.limits = (forward_steps, self.count - 1 - forward_steps)
+        self.steps = max(self.limits)
+        self.step = 0
+        self.front = self.back = chunk
+        self.whole = lax.dynamic_update_slice(
+            whole, chunk, (lax.axis_index("dp") * self.depth, 0)
+        )
+
+    def put(self, block, distance):
+        owner = ring_device((self.place + self.count + distance) % self.count, self.count)
+        self.whole = lax.dynamic_update_slice(self.whole, block, (owner * self.depth, 0))
+
+    def advance(self, *earlier):
+        self.step += 1
+        front = self.front if self.step <= self.limits[0] else None
+        back = self.back if self.step <= self.limits[1] else None
+        front, back = tie([front, back], earlier)
+        if front is not None:
+            self.front = lax.ppermute(front, "dp", self.ahead)
+            self.put(self.front, -self.step)
+        if back is not None:
+            self.back = lax.ppermute(back, "dp", self.behind)
+            self.put(self.back, self.step)
+        return [item for item in (front, back) if item is not None]
+
+    def result(self):
+        while self.step < self.steps:
+            self.advance()
+        return self.whole
+
+
+class RingScatter:
+    def __init__(self, terms, forward_steps):
+        self.terms = terms
+        self.count = lax.axis_size("dp")
+        self.place = ring_place(lax.axis_index("dp"), self.count)
+        self.depth = terms.shape[0] // self.count
+        self.ahead, self.behind = ring_routes(self.count)
+        self.forward_steps = forward_steps
+        self.backward_steps = self.count - 1 - forward_steps
+        self.steps = max(self.forward_steps, self.backward_steps)
+        self.step = 0
+        self.front = self.back = None
+
+    def term(self, distance):
+        owner = ring_device((self.place + self.count + distance) % self.count, self.count)
+        width = self.terms.shape[1]
+        return lax.dynamic_slice(self.terms, (owner * self.depth, 0), (self.depth, width))
+
+    def advance(self, *earlier):
+        marks = []
+        front, back = tie([self.front, self.back], earlier)
+        if self.step < self.forward_steps:
+            own = self.term(self.forward_steps - self.step)
             if front is not None:
                 own = (own.astype(F32) + front.astype(F32)).astype(BF)
-            front = lax.ppermute(own, "dp", ahead)
-        if step < backward_steps:
-            own = term(step - backward_steps)
+            marks.append(own)
+            front = lax.ppermute(own, "dp", self.ahead)
+        if self.step < self.backward_steps:
+            own = self.term(self.step - self.backward_steps)
             if back is not None:
                 own = (own.astype(F32) + back.astype(F32)).astype(BF)
-            back = lax.ppermute(own, "dp", behind)
-    return term(0).astype(F32) + front.astype(F32) + back.astype(F32)
+            marks.append(own)
+            back = lax.ppermute(own, "dp", self.behind)
+        self.front, self.back = front, back
+        self.step += 1
+        return marks
+
+    def result(self):
+        while self.step < self.steps:
+            self.advance()
+        return self.term(0).astype(F32) + self.front.astype(F32) + self.back.astype(F32)
 
 
 def swap(block, axis):
@@ -145,14 +190,68 @@
     )
 
 
+def pack_kernel(pipe_ref, *refs):
+    sources, (kept_ref, sent_ref) = refs[:6], refs[6:8]
+    held, marks = refs[10:16], refs[16]
+    copies = [
+        pltpu.make_async_copy(source, target, marks.at[i])
+        for i, (source, target) in enumerate(zip(sources, held))
+    ]
+    for copy in copies:
+        copy.start()
+    for copy in copies:
+        copy.wait()
+    qkv_ref, out_ref, fc_ref, proj_ref = held[:4]
+    depth = qkv_ref.shape[0]
+    rows = [held[4][...]]
+    long_bias = held[5][...]
+    qkv_width, out_width = qkv_ref.shape[1] // 2, out_ref.shape[1] // 2
+    hidden = fc_ref.shape[1] // 2
+    start = qkv_width + out_width
+    qkv_bias, fc_bias = long_bias[:, : 2 * qkv_width], long_bias[:, 2 * qkv_width :]
+
+    def fill(target, index):
+        target[:, :start] = jnp.concatenate(
+            [
+                qkv_ref[:, index * qkv_width : (index + 1) * qkv_width],
+                out_ref[:, index * out_width : (index + 1) * out_width],
+            ],
+            axis=1,
+        )
+        target[:, start : start + hidden] = fc_ref[:, index * hidden : (index + 1) * hidden]
+        target[:, start + hidden : start + 2 * hidden] = proj_ref[
+            :, index * hidden : (index + 1) * hidden
+        ]
+        bias = jnp.concatenate(
+            [
+                qkv_bias[:, index * qkv_width : (index + 1) * qkv_width],
+                fc_bias[:, index * hidden : (index + 1) * hidden],
+            ],
+            axis=1,
+        )
+        pieces = bias.shape[1] // depth
+        small = rows + [bias[:, i * depth : (i + 1) * depth] for i in range(pieces)]
+        small.append(jnp.zeros((SMALL - 8 - pieces, depth), F32))
+        small = jnp.transpose(jnp.concatenate(small, axis=0))
+        target[:, start + 2 * hidden :] = small.astype(BF)
+
+    @pl.when(pipe_ref[0] == 0)
+    def _():
+        fill(kept_ref, 0)
+        fill(sent_ref, 1)
+
+    @pl.when(pipe_ref[0] != 0)
+    def _():
+        fill(kept_ref, 1)
+        fill(sent_ref, 0)
+
+
 def forward_kernel(
     heads,
+    depth,
     own_ref,
     far_ref,
-    first_w_ref,
-    second_w_ref,
-    qkv_bias_ref,
-    fc_bias_ref,
+    weight_ref,
     cos_ref,
     upper_ref,
     lower_ref,
@@ -171,12 +270,18 @@
 ):
     rows = own_ref.shape[0]
     qkv_width = heads * 3 * HEAD
-    out_width = heads * HEAD
+    start = heads * 4 * HEAD
     wide = cos_ref.shape[1]
-    hidden = fc_bias_ref.shape[1]
-    small = first_w_ref[:, qkv_width + out_width :].astype(F32)
-    vectors = jnp.transpose(small)[:8]
+    hidden = pre_ref.shape[1]
+    pieces = (qkv_width + hidden) // depth
+    small = jnp.transpose(weight_ref[:, start + 2 * hidden :].astype(F32))
+    vectors = small[:8]
     vector_ref[...] = vectors
+    long_bias = jnp.concatenate([small[8 + i : 9 + i, :depth] for i in range(pieces)], axis=1)
+    qkv_bias = jnp.concatenate(
+        [long_bias[:, :qkv_width], jnp.zeros((1, wide - qkv_width), F32)], axis=1
+    )
+    fc_bias = long_bias[:, qkv_width:]
     values = jnp.concatenate([own_ref[...], far_ref[...]], axis=0).astype(F32)
     centred = values - jnp.mean(values, axis=-1, keepdims=True)
     scale = lax.rsqrt(jnp.mean(centred * centred, axis=-1, keepdims=True) + EPSILON)
@@ -187,7 +292,7 @@
     second = (xhat * vectors[2:3] + vectors[3:4]).astype(BF)
     norm1_ref[...] = first
     norm2_ref[...] = second
-    packed = dot(first, first_w_ref[:, :wide]) + qkv_bias_ref[...]
+    packed = dot(first, weight_ref[:, :wide]) + qkv_bias
     packed = turn(packed, cos_ref[...], upper_ref[...], lower_ref[...]).astype(BF)
     packed_ref[...] = packed
     bias = bias_ref[...]
@@ -198,12 +303,12 @@
         mixed.append(dot(weights, held))
     mixed = jnp.concatenate(mixed, axis=1).astype(BF)
     mixed_ref[...] = mixed
-    pre = dot(second, second_w_ref[:, :hidden]) + fc_bias_ref[...]
+    pre = dot(second, weight_ref[:, start : start + hidden]) + fc_bias
     pre_ref[...] = pre
     act = (pre * (0.5 + 0.5 * lax.erf(pre * math.sqrt(0.5)))).astype(BF)
     act_ref[...] = act
-    total = dot_last(act, second_w_ref[:, hidden:])
-    total = total + dot_last(mixed, first_w_ref[:, qkv_width : qkv_width + out_width])
+    total = dot_last(act, weight_ref[:, start + hidden : start + 2 * hidden])
+    total = total + dot_last(mixed, weight_ref[:, qkv_width:start])
     mine_ref[...] = total[:rows]
     other_ref[...] = total[rows:]
 
@@ -212,8 +317,7 @@
     heads,
     own_ref,
     far_ref,
-    first_w_ref,
-    second_w_ref,
+    weight_ref,
     cos_ref,
     upper_ref,
     lower_ref,
@@ -231,18 +335,18 @@
 ):
     rows = own_ref.shape[0]
     qkv_width = heads * 3 * HEAD
-    out_width = heads * HEAD
+    start = heads * 4 * HEAD
     wide = cos_ref.shape[1]
     hidden = pre_ref.shape[1]
     grad = jnp.concatenate([own_ref[...], far_ref[...]], axis=0)
-    d_act = dot(grad, second_w_ref[:, hidden:])
+    d_act = dot(grad, weight_ref[:, start + hidden : start + 2 * hidden])
     pre = pre_ref[...]
     slope = 0.5 + 0.5 * lax.erf(pre * math.sqrt(0.5))
     slope = slope + pre * (jnp.exp(pre * pre * -0.5) * (1.0 / math.sqrt(2.0 * math.pi)))
     d_pre = (d_act * slope).astype(BF)
     d_pre_ref[...] = d_pre
-    d_second = dot_last(d_pre, second_w_ref[:, :hidden])
-    d_mixed = dot(grad, first_w_ref[:, qkv_width : qkv_width + out_width]).astype(BF)
+    d_second = dot_last(d_pre, weight_ref[:, start : start + hidden])
+    d_mixed = dot(grad, weight_ref[:, qkv_width:start]).astype(BF)
     bias = bias_ref[...]
     packed = packed_ref[...]
     parts = []
@@ -262,7 +366,7 @@
     d_packed = jnp.concatenate(parts, axis=1)
     d_packed = turn(d_packed, cos_ref[...], -upper_ref[...], -lower_ref[...]).astype(BF)
     d_packed_ref[...] = d_packed
-    d_first = dot_last(d_packed, first_w_ref[:, :wide])
+    d_first = dot_last(d_packed, weight_ref[:, :wide])
     xhat = xhat_ref[...]
     inner = d_first * vector_ref[0:1] + d_second * vector_ref[2:3]
     average = jnp.mean(inner, axis=-1, keepdims=True)
@@ -296,13 +400,10 @@
 def weight_kernel(heads, depth, count, *refs):
     refs = list(refs)
     groups = [refs[i * 9 : (i + 1) * 9] for i in range(count)]
-    first_out_ref, second_out_ref, full_refs = (
-        refs[9 * count + count],
-        refs[9 * count + count + 1],
-        refs[9 * count : 9 * count + count],
-    )
+    terms_ref, full_refs = refs[10 * count], refs[9 * count : 10 * count]
     qkv_width = heads * 3 * HEAD
-    tile = first_out_ref.shape[0]
+    start = heads * 4 * HEAD
+    tile = terms_ref.shape[0]
 
     def both(index):
         return jnp.concatenate([group[index][...] for group in groups], axis=0)
@@ -326,27 +427,114 @@
     stacked = jnp.concatenate([stacked] * (tile // depth), axis=1)
     rest = SMALL - 8 - pieces
     small = jnp.concatenate([sums, stacked, jnp.zeros((rest, tile), F32)], axis=0)
-    first_out_ref[...] = jnp.concatenate(
-        [
-            dot_first(first, d_packed)[:, :qkv_width],
-            dot_first(grad, mixed),
-            jnp.transpose(small),
-        ],
-        axis=1,
+    terms_ref[:, :start] = jnp.concatenate(
+        [dot_first(first, d_packed)[:, :qkv_width], dot_first(grad, mixed)], axis=1
     ).astype(BF)
-    second_out_ref[:, :hidden] = dot_first(second, d_pre).astype(BF)
-    second_out_ref[:, hidden:] = dot_first(grad, act).astype(BF)
+    terms_ref[:, start : start + hidden] = dot_first(second, d_pre).astype(BF)
+    terms_ref[:, start + hidden : start + 2 * hidden] = dot_first(grad, act).astype(BF)
+    terms_ref[:, start + 2 * hidden :] = jnp.transpose(small).astype(BF)
+
+
+def unpack_kernel(
+    pipe_ref,
+    own_ref,
+    came_ref,
+    own_small_ref,
+    came_small_ref,
+    qkv_ref,
+    qkv_bias_ref,
+    out_ref,
+    fc_ref,
+    fc_bias_ref,
+    proj_ref,
+    *vector_refs,
+):
+    depth = qkv_ref.shape[0]
+    qkv_width, out_width = qkv_ref.shape[1] // 2, out_ref.shape[1] // 2
+    hidden = fc_ref.shape[1] // 2
+    start = qkv_width + out_width
+    pieces = (qkv_width + hidden) // depth
+    smalls = [jnp.transpose(ref[...]) for ref in (own_small_ref, came_small_ref)]
+    vectors = smalls[0][:8] + smalls[1][:8]
+    for index, ref in enumerate(vector_refs):
+        ref[...] = vectors[index : index + 1]
+    longs = [
+        jnp.concatenate([small[8 + i : 9 + i] for i in range(pieces)], axis=1) for small in smalls
+    ]
+
+    def fill(lower, upper, low_bias, high_bias):
+        for index, (block, bias) in enumerate(((lower, low_bias), (upper, high_bias))):
+            columns = slice(index * qkv_width, (index + 1) * qkv_width)
+            qkv_ref[:, columns] = block[:, :qkv_width].astype(F32)
+            qkv_bias_ref[:, columns] = bias[:, :qkv_width]
+            lines = slice(index * out_width, (index + 1) * out_width)
+            out_ref[:, lines] = block[:, qkv_width:start].astype(F32)
+            units = slice(index * hidden, (index + 1) * hidden)
+            fc_ref[:, units] = block[:, start : start + hidden].astype(F32)
+            fc_bias_ref[:, units] = bias[:, qkv_width:]
+            proj_ref[:, units] = block[:, start + hidden : start + 2 * hidden].astype(F32)
+
+    @pl.when(pipe_ref[0] == 0)
+    def _():
+        fill(own_ref, came_ref, longs[0], longs[1])
+
+    @pl.when(pipe_ref[0] != 0)
+    def _():
+        fill(came_ref, own_ref, longs[1], longs[0])
 
 
 def cost(flops, moved):
     return pl.CostEstimate(flops=int(flops), bytes_accessed=int(moved), transcendentals=0)
 
 
-def forward_call(own, far, weights, biases, layout, heads):
+def in_vmem():
+    return pl.BlockSpec(memory_space=pltpu.VMEM)
+
+
+def pack_call(pipe, arrays, count):
+    qkv, out, fc = arrays[:3]
+    width = (qkv.shape[1] + out.shape[1]) // 2 + fc.shape[1] + SMALL
+    packet = jax.ShapeDtypeStruct((qkv.shape[0], width), BF)
+    whole = jax.ShapeDtypeStruct((count * qkv.shape[0], width), BF)
+    return pl.pallas_call(
+        pack_kernel,
+        out_shape=(packet, packet, whole, whole),
+        out_specs=(in_vmem(), in_vmem())
+        + (pl.BlockSpec(memory_space=pl.ANY), pl.BlockSpec(memory_space=pl.ANY)),
+        in_specs=[pl.BlockSpec(memory_space=pltpu.SMEM)]
+        + [pl.BlockSpec(memory_space=pl.ANY)] * len(arrays),
+        scratch_shapes=[pltpu.VMEM(item.shape, item.dtype) for item in arrays]
+        + [pltpu.SemaphoreType.DMA((len(arrays),))],
+        compiler_params=pltpu.CompilerParams(vmem_limit_bytes=VMEM_LIMIT),
+        cost_estimate=cost(0, 4e6),
+        name="pack",
+    )(pipe, *arrays)
+
+
+def unpack_call(pipe, own, came, own_small, came_small, widths):
+    depth = own.shape[0]
+    qkv_width, out_width, hidden = widths
+    shapes = (
+        (depth, 2 * qkv_width),
+        (1, 2 * qkv_width),
+        (depth, 2 * out_width),
+        (depth, 2 * hidden),
+        (1, 2 * hidden),
+        (depth, 2 * hidden),
+    ) + ((1, depth),) * 5
+    return pl.pallas_call(
+        unpack_kernel,
+        out_shape=tuple(jax.ShapeDtypeStruct(shape, F32) for shape in shapes),
+        in_specs=[pl.BlockSpec(memory_space=pltpu.SMEM)] + [in_vmem()] * 4,
+        compiler_params=pltpu.CompilerParams(vmem_limit_bytes=VMEM_LIMIT),
+        cost_estimate=cost(0, 6e6),
+        name="unpack",
+    )(pipe, own, came, own_small, came_small)
+
+
+def forward_call(own, far, weight, layout, heads, hidden, depth):
     rows, model = own.shape
     full = 2 * rows
-    first_w, second_w = weights
-    hidden = second_w.shape[1] // 2
     wide = layout[0].shape[1]
 
     def shape(height, width, kind):
@@ -366,42 +554,40 @@
         shape(8, model, F32),
     )
     return pl.pallas_call(
-        functools.partial(forward_kernel, heads),
+        functools.partial(forward_kernel, heads, depth),
         out_shape=outs,
         compiler_params=pltpu.CompilerParams(vmem_limit_bytes=VMEM_LIMIT),
         cost_estimate=cost(4e9, 8e6),
         name="forward",
-    )(own, far, first_w, second_w, biases[0], biases[1], *layout)
-
-
-def backward_call(own, far, weights, layout, kept, heads):
+    )(own, far, weight, *layout)
+
+
+def backward_call(own, far, weight, layout, kept, heads):
     rows, model = own.shape
     full = 2 * rows
-    first_w, second_w = weights
-    hidden = second_w.shape[1] // 2
     wide = layout[0].shape[1]
     norm1, norm2, xhat, scale, packed, mixed, pre, act, vectors = kept
     outs = (
         jax.ShapeDtypeStruct((rows, model), F32),
         jax.ShapeDtypeStruct((rows, model), F32),
         jax.ShapeDtypeStruct((full, wide), BF),
-        jax.ShapeDtypeStruct((full, hidden), BF),
+        jax.ShapeDtypeStruct((full, pre.shape[1]), BF),
         jax.ShapeDtypeStruct((8, model), F32),
     )
     return pl.pallas_call(
         functools.partial(backward_kernel, heads),
         out_shape=outs,
         compiler_params=pltpu.CompilerParams(vmem_limit_bytes=VMEM_LIMIT),
-        cost_estimate=cost(8e9, 10e6),
+        cost_estimate=cost(5e9, 10e6),
         name="backward",
-    )(own, far, first_w, second_w, *layout, xhat, scale, packed, pre, vectors)
+    )(own, far, weight, *layout, xhat, scale, packed, pre, vectors)
 
 
 def weight_call(grads, kept, backs, heads, depth):
     model = kept[0][0].shape[1]
     hidden = kept[0][7].shape[1]
     tile = model // 2
-    first_width = heads * 4 * HEAD + SMALL
+    width = heads * 4 * HEAD + 2 * hidden + SMALL
     operands, specs = [], []
 
     def tiled(array):
@@ -428,14 +614,8 @@
         functools.partial(weight_kernel, heads, depth, len(grads)),
         grid=(2,),
         in_specs=specs,
-        out_specs=(
-            pl.BlockSpec((tile, first_width), lambda i: (i, 0)),
-            pl.BlockSpec((tile, 2 * hidden), lambda i: (i, 0)),
-        ),
-        out_shape=(
-            jax.ShapeDtypeStruct((model, first_width), BF),
-            jax.ShapeDtypeStruct((model, 2 * hidden), BF),
-        ),
+        out_specs=pl.BlockSpec((tile, width), lambda i: (i, 0)),
+        out_shape=jax.ShapeDtypeStruct((model, width), BF),
         compiler_params=pltpu.CompilerParams(vmem_limit_bytes=VMEM_LIMIT),
         cost_estimate=cost(8e9, 10e6),
         name="weights",
@@ -499,50 +679,37 @@
     heads = out_width // HEAD
     ahead_steps = count // 2
 
+    pipe_word = pipe.astype(jnp.int32).reshape(1)
     vectors = jnp.concatenate([ln1_gain, ln1_shift, ln2_gain, ln2_shift, branch_bias], axis=0)
-    vectors = jnp.pad(jnp.transpose(vectors), ((0, 0), (0, SMALL - 5)))
-    out_turned = jnp.transpose(out_weight[0])
-    proj_turned = jnp.transpose(proj_weight[0])
-
-    def cut(array, width, index):
-        return array[:, index * width : (index + 1) * width]
-
-    def quarter(index):
-        first = jnp.concatenate(
-            [cut(qkv_weight[0], qkv_width, index), cut(out_turned, out_width, index), vectors],
-            axis=1,
-        )
-        second = jnp.concatenate(
-            [cut(fc_weight[0], hidden, index), cut(proj_turned, hidden, index)], axis=1
-        )
-        bias = jnp.concatenate([cut(qkv_bias, qkv_width, index), cut(fc_bias, hidden, index)], 1)
-        return first, second, bias
-
-    lower_part, upper_part = quarter(0), quarter(1)
-    chunks = []
-    for low_item, high_item in zip(lower_part, upper_part):
-        kept_item = jnp.where(leading, low_item, high_item)
-        sent_item = jnp.where(leading, high_item, low_item)
-        came_item = swap(sent_item, "pipe")
-        chunks.append(
-            (
-                jnp.where(leading, kept_item, came_item),
-                jnp.where(leading, came_item, kept_item),
-            )
-        )
-    weights, biases = [], []
-    for section in range(2):
-        weights.append(
-            (
-                ring_gather(chunks[0][section], ahead_steps),
-                ring_gather(chunks[1][section], count - 1 - ahead_steps),
-            )
-        )
-        long_bias = chunks[2][section].astype(F32)
-        first_bias = long_bias[:, :qkv_width]
-        pad = -qkv_width % 128
-        biases.append((jnp.pad(first_bias, ((0, 0), (0, pad))), long_bias[:, qkv_width:]))
-
+    vectors = jnp.pad(vectors.astype(F32), ((0, 3), (0, 0)))
+    kept_part, sent_part, first_whole, second_whole = pack_call(
+        pipe_word,
+        (
+            qkv_weight[0],
+            jnp.transpose(out_weight[0]),
+            fc_weight[0],
+            jnp.transpose(proj_weight[0]),
+            vectors,
+            jnp.concatenate([qkv_bias, fc_bias], axis=1).astype(F32),
+        ),
+        count,
+    )
+    came_part = swap(sent_part, "pipe")
+    chunk = jnp.where(leading, kept_part, came_part)
+    gather = RingGather(chunk, first_whole, ahead_steps)
+    gather.advance()
+    later = RingGather(
+        jnp.where(leading, came_part, kept_part), second_whole, count - 1 - ahead_steps
+    )
+    order = []
+    for _ in range(gather.steps - 1):
+        order = gather.advance(*order)
+        if later.step < later.steps - 1:
+            order = later.advance(*order)
+    weights = [gather.result(), None]
+
+    lengths = after(lengths, chunk)
+    inputs, cotangent = after(inputs, sent_part), after(cotangent, chunk)
     layouts = [layout_of(lengths[m, 0], rows, core * rows, heads) for m in range(micro)]
 
     def complete(half, base):
@@ -559,8 +726,11 @@
         kept_rows, results = [], []
         for m in range(micro):
             own, far = current[m]
-            found = forward_call(own, far, weights[section], biases[section], layouts[m], heads)
+            found = forward_call(own, far, weights[section], layouts[m], heads, hidden, depth)
             kept_rows.append(found[2:])
+            if section == 0 and m + 1 == micro:
+                later.advance(found[-1])
+                weights[1] = later.result()
             half = half_sum(found[0], found[1])
             base = own.astype(F32) + found[-1][4:5]
             results.append(complete(half, base))
@@ -569,71 +739,71 @@
         stored.append(kept_rows)
         outputs.append(results)
 
-    grads = cotangents
-    back_outputs, reduced = [None, None], [None, None]
-    for section in (1, 0):
-        backs, results = [], []
-        for m in range(micro):
-            own, far = grads[m]
-            found = backward_call(
-                own, far, weights[section], layouts[m], stored[section][m], heads
-            )
-            backs.append(found)
-            half = half_sum(found[0], found[1])
-            results.append(complete(half, own.astype(F32)))
-        first_terms, second_terms = weight_call(grads, stored[section], backs, heads, depth)
-        reduced[section] = (
-            ring_scatter(first_terms, ahead_steps),
-            ring_scatter(second_terms, count - 1 - ahead_steps),
-        )
-        back_outputs[section] = results
-        if section == 1:
-            grads = [(item, swap(item, "tensor")) for item in results]
+    back_outputs = [None, None]
+    backs, results, halves = [], [], []
+    for m in range(micro):
+        own, far = cotangents[m]
+        found = backward_call(own, far, weights[1], layouts[m], stored[1][m], heads)
+        backs.append(found)
+        halves.append(half_sum(found[0], found[1]))
+        results.append(complete(halves[m], own.astype(F32)))
+    back_outputs[1] = results
+    grads = [(item, swap(item, "tensor")) for item in results]
+    backs[-1] = (*backs[-1][:4], after(backs[-1][4], halves[-1]))
+    scatter = RingScatter(weight_call(cotangents, stored[1], backs, heads, depth), ahead_steps)
+    scatter.advance()
+    backs, results, marks = [], [], ()
+    for m in range(micro):
+        own, far = grads[m]
+        found = backward_call(own, far, weights[0], layouts[m], stored[0][m], heads)
+        backs.append(found)
+        results.append(complete(half_sum(found[0], found[1]), own.astype(F32)))
+        if m + 1 < micro:
+            marks = scatter.advance(found[4])
+    back_outputs[0] = results
+    backs[-1] = (*backs[-1][:4], after(backs[-1][4], *marks[:TIES]))
+    terms = weight_call(grads, stored[0], backs, heads, depth)
+    last = RingScatter(terms, count - 1 - ahead_steps)
+    order = last.advance()
+    while scatter.step < scatter.steps or last.step < last.steps:
+        if scatter.step < scatter.steps:
+            order = scatter.advance(*order[:TIES])
+        if last.step < last.steps:
+            order = last.advance(*order[:TIES])
+    reduced = [last.result(), scatter.result()]
 
     activations = jnp.where(leading, jnp.stack(outputs[0]), jnp.stack(outputs[1]))[None]
     input_grads = jnp.where(leading, jnp.stack(back_outputs[0]), jnp.stack(back_outputs[1]))[None]
 
-    halves = []
-    for index in range(2):
-        own = jnp.where(leading, reduced[0][index], reduced[1][index])
-        given = jnp.where(leading, reduced[1][index], reduced[0][index]).astype(BF)
-        came = swap(given, "pipe").astype(F32)
-        halves.append((own, came))
-
-    def joined(index, start, width):
-        own, came = (item[:, start : start + width] for item in halves[index])
-        lower_item = jnp.where(leading, own, came)
-        upper_item = jnp.where(leading, came, own)
-        return jnp.concatenate([lower_item, upper_item], axis=1)
-
-    small_start = qkv_width + out_width
-    own_small, came_small = (item[:, small_start:] for item in halves[0])
-    vector_grads = own_small[:, :8] + came_small[:, :8]
-    vector_grads = jnp.transpose(vector_grads + swap(vector_grads, "tensor"))
-    pieces = (qkv_width + hidden) // depth
-
-    def flat(block):
-        return jnp.transpose(block[:, 8 : 8 + pieces]).reshape(1, -1)
-
-    own_bias, came_bias = flat(own_small), flat(came_small)
-    lower_bias = jnp.where(leading, own_bias, came_bias)
-    upper_bias = jnp.where(leading, came_bias, own_bias)
-    qkv_bias_grad = jnp.concatenate([lower_bias[:, :qkv_width], upper_bias[:, :qkv_width]], axis=1)
-    fc_bias_grad = jnp.concatenate([lower_bias[:, qkv_width:], upper_bias[:, qkv_width:]], axis=1)
+    start = qkv_width + out_width
+    own_part = jnp.where(leading, reduced[0], reduced[1])
+    given_part = jnp.where(leading, reduced[1], reduced[0])
+    came_part = swap(given_part[:, : start + 2 * hidden].astype(BF), "pipe")
+    smalls = jnp.concatenate(
+        [own_part[:, start + 2 * hidden :], given_part[:, start + 2 * hidden :]], axis=0
+    )
+    lane = lax.broadcasted_iota(jnp.int32, smalls.shape, 1)
+    smalls = jnp.where(lane < 8, smalls + swap(smalls, "tensor"), smalls)
+    came_small = swap(smalls[depth:], "pipe")
+    grads_out = unpack_call(
+        pipe_word, own_part, came_part, smalls[:depth], came_small, (qkv_width, out_width, hidden)
+    )
+    qkv_grad, qkv_bias_grad, out_grad, fc_grad, fc_bias_grad, proj_grad = grads_out[:6]
+    vector_grads = grads_out[6:]
     return (
         activations,
         input_grads,
-        vector_grads[0:1],
-        vector_grads[1:2],
-        vector_grads[2:3],
-        vector_grads[3:4],
-        joined(0, 0, qkv_width)[None],
+        vector_grads[0],
+        vector_grads[1],
+        vector_grads[2],
+        vector_grads[3],
+        qkv_grad[None],
         qkv_bias_grad,
-        jnp.transpose(joined(0, qkv_width, out_width))[None],
-        joined(1, 0, hidden)[None],
+        jnp.transpose(out_grad)[None],
+        fc_grad[None],
         fc_bias_grad,
-        jnp.transpose(joined(1, hidden, hidden))[None],
-        vector_grads[4:5],
+        jnp.transpose(proj_grad)[None],
+        vector_grads[4],
     )
 
 

time: 342 us -> 258 us (0.75)
  starting transfers between devices: 88.2 us -> 46.6 us
  Pallas kernels: 59.6 us -> 31.5 us
  other arithmetic: 27 us -> 8.37 us
  waiting for transfers between devices: 133 us -> 139 us
    ppermute x56 -> x28, starting transfers between devices: 66.4 us -> 27.7 us  [the longest x7 11.2 us: advance(): self.front = lax.ppermute(front, 'dp', self.ahead)]
    pallas_call x4, Pallas kernels: 34.4 us -> 14.8 us  [backward_call(): pl.pallas_call(functools.partial(backward_kernel, heads), out_shape=outs,...]
    dynamic_update_slice x28 -> x14, local copies, waits for them, and re-layouts: 0.64 us -> 11.1 us  [put(): lax.dynamic_update_slice(self.whole, block, (owner * self.depth, 0))]
    ppermute x30 -> x28, waiting for transfers between devices: 23.6 us -> 32.9 us  [swap(): return lax.ppermute(block, axis, [(0, 1), (1, 0)])]
    pallas_call x4 -> x6, Pallas kernels: 17.6 us -> 11.3 us  [the longest x4 8.94 us: forward_call(): pl.pallas_call(functools.partial(forward_kernel, heads, depth), out_shape...]
    convert_element_type x19 -> x7, other arithmetic: 7.64 us -> 2.05 us  [the longest x5 1.21 us: advance(): own = (own.astype(F32) + back.astype(F32)).astype(BF)]
    select_n x9 -> x2, other arithmetic: 5.19 us -> 0.42 us  [the longest x1 0.41 us: local(): given_part = jnp.where(leading, reduced[1], reduced[0])]
    slice x12 -> x4, local copies, waits for them, and re-layouts: 3.71 us -> 0.07 us  [the longest x1 0.05 us: local(): came_part = swap(given_part[:, :start + 2 * hidden].astype(BF), 'pipe')]
  transfers between devices with their start and end apart: 86 -> 56, of which waited for: 42 -> 28; matrix products, arithmetic and copies ran while one was open for 13% -> 11% of each run, Pallas kernels for 18% -> 11%
where the time goes in v2:
time: 258 us; the launch traced here: 257 us
  waiting for transfers between devices  139 us (54%)
  starting transfers between devices  46.6 us (18%)
  Pallas kernels  31.5 us (12%)
  local copies, waits for them, and re-layouts  30 us (12%)
  other arithmetic  8.37 us (3%)
    ppermute x7, waiting for transfers between devices, advance(): front = lax.ppermute(own, 'dp', self.ahead)  41.8 us
    ppermute x28, waiting for transfers between devices, swap(): return lax.ppermute(block, axis, [(0, 1), (1, 0)])  32.9 us
    ppermute x7, waiting for transfers between devices, advance(): self.front = lax.ppermute(front, 'dp', self.ahead)  30.8 us
    ppermute x7, waiting for transfers between devices, advance(): self.back = lax.ppermute(back, 'dp', self.behind)  27.3 us
    ppermute x28, starting transfers between devices, swap(): return lax.ppermute(block, axis, [(0, 1), (1, 0)])  18.9 us
    pallas_call x4, Pallas kernels, backward_call(): pl.pallas_call(functools.partial(backward_kernel, heads), out_shape=outs,...  14.8 us
    ppermute x7, starting transfers between devices, advance(): self.front = lax.ppermute(front, 'dp', self.ahead)  11.2 us
    dynamic_update_slice x14, local copies, waits for them, and re-layouts, put(): lax.dynamic_update_slice(self.whole, block, (owner * self.depth, 0))  11.1 us
  transfers between devices with their start and end apart: 56, of which 28 were waited for; matrix products, arithmetic and copies ran while one was open for 11% of the time, Pallas kernels for 11%

profile of v2, /device:TPU:0, one launch (start us, length us, event | category | flops | bytes accessed | tf_op | source)
XLA Modules:
  0.0 257.4 jit_solution(12271676528676132021)
XLA Ops:
  6.8 1.8 copy-done.4
  8.6 1.8 copy-done.7
  10.4 3.0 %collective-permute-start.1 = (bf16[96,2432]{1,0:T(8,128)(2,1)S(1)}, bf16[96,2432]{1,0:T(8,128)(2,1)S(1)}, u32[]{:S(2)}, u32[]{:S(2)}) collective-permute-start(bf16[96,2432]{1,0:T(8,128)(2,1)S(1)} %get-tuple-element.119), channel_id=1, source_target_pairs={{0,16},{16,0},{1,17},{17,1},{2,18},{18,2},{3,19},{19,3},{4,20},{20... | collective-permute-start | bytes 1400840 | tf_op jit(solution)/shard_map/ppermute | solution.py:157
  14.8 9.3 %collective-permute-done.1 = bf16[96,2432]{1,0:T(8,128)(2,1)S(1)} collective-permute-done((bf16[96,2432]{1,0:T(8,128)(2,1)S(1)}, bf16[96,2432]{1,0:T(8,128)(2,1)S(1)}, u32[]{:S(2)}, u32[]{:S(2)}) %collective-permute-start.1) | collective-permute-done | bytes 466976 | tf_op jit(solution)/shard_map/ppermute | solution.py:157
  24.1 1.4 constant_dynamic-update-slice_fusion.7
  25.6 1.8 collective-permute-start.2
  28.2 1.4 multiply_sine_fusion.1
  33.6 2.3 concatenate.82.lower_ref
  37.8 1.2 collective-permute-done.3
  38.9 1.6 collective-permute-start.8
  41.0 1.6 collective-permute-start.4
  43.0 1.9 constant_dynamic-update-slice_fusion.14
  44.8 1.8 constant_dynamic-update-slice_fusion.13
  46.7 12.8 %collective-permute-done.4 = bf16[96,2432]{1,0:T(8,128)(2,1)S(1)} collective-permute-done((bf16[96,2432]{1,0:T(8,128)(2,1)}, bf16[96,2432]{1,0:T(8,128)(2,1)S(1)}, u32[]{:S(2)}, u32[]{:S(2)}) %collective-permute-start.4) | collective-permute-done | bytes 466976 | tf_op jit(solution)/shard_map/ppermute | solution.py:100
  59.5 1.3 collective-permute-done.5
  60.8 1.6 collective-permute-start.6
  62.4 1.5 collective-permute-start.17
  67.2 16.8 %collective-permute-done.17 = bf16[96,2432]{1,0:T(8,128)(2,1)S(1)} collective-permute-done((bf16[96,2432]{1,0:T(8,128)(2,1)S(1)}, bf16[96,2432]{1,0:T(8,128)(2,1)S(1)}, u32[]{:S(2)}, u32[]{:S(2)}) %collective-permute-start.17) | collective-permute-done | bytes 466976 | tf_op jit(solution)/shard_map/ppermute | solution.py:100
  86.9 10.6 %collective-permute-done.18 = bf16[96,2432]{1,0:T(8,128)(2,1)S(1)} collective-permute-done((bf16[96,2432]{1,0:T(8,128)(2,1)S(1)}, bf16[96,2432]{1,0:T(8,128)(2,1)S(1)}, u32[]{:S(2)}, u32[]{:S(2)}) %collective-permute-start.18) | collective-permute-done | bytes 466976 | tf_op jit(solution)/shard_map/ppermute | solution.py:103
  97.5 1.6 collective-permute-start.10
  99.9 6.4 %collective-permute-done.7 = bf16[96,2432]{1,0:T(8,128)(2,1)S(1)} collective-permute-done((bf16[96,2432]{1,0:T(8,128)(2,1)S(1)}, bf16[96,2432]{1,0:T(8,128)(2,1)S(1)}, u32[]{:S(2)}, u32[]{:S(2)}) %collective-permute-start.7) | collective-permute-done | bytes 466976 | tf_op jit(solution)/shard_map/ppermute | solution.py:103
  107.7 1.6 collective-permute-start.19
  110.5 2.1 copy-done.5
  112.6 2.2 forward.4
  114.9 2.2 forward.5
  117.2 5.2 %collective-permute-done.20 = bf16[96,2432]{1,0:T(8,128)(2,1)S(1)} collective-permute-done((bf16[96,2432]{1,0:T(8,128)(2,1)S(1)}, bf16[96,2432]{1,0:T(8,128)(2,1)S(1)}, u32[]{:S(2)}, u32[]{:S(2)}) %collective-permute-start.20) | collective-permute-done | bytes 466976 | tf_op jit(solution)/shard_map/ppermute | solution.py:103
  122.9 1.6 collective-permute-start.12
  125.7 4.0 %collective-permute-done.12 = bf16[96,768]{1,0:T(8,128)(2,1)S(1)} collective-permute-done((bf16[96,768]{1,0:T(8,128)(2,1)S(1)}, bf16[96,768]{1,0:T(8,128)(2,1)S(1)}, u32[]{:S(2)}, u32[]{:S(2)}) %collective-permute-start.12) | collective-permute-done | bytes 147488 | tf_op jit(solution)/shard_map/ppermute | solution.py:157
  129.6 2.5 collective-permute-done.15
  132.8 2.7 %collective-permute-done.21 = bf16[96,2432]{1,0:T(8,128)(2,1)S(1)} collective-permute-done((bf16[96,2432]{1,0:T(8,128)(2,1)S(1)}, bf16[96,2432]{1,0:T(8,128)(2,1)S(1)}, u32[]{:S(2)}, u32[]{:S(2)}) %collective-permute-start.21) | collective-permute-done | bytes 466976 | tf_op jit(solution)/shard_map/ppermute | solution.py:103
  135.5 2.2 forward.7
  137.9 2.2 forward.6
  140.7 3.7 %backward.4 = (f32[96,768]{1,0:T(8,128)S(1)}, f32[96,768]{1,0:T(8,128)S(1)}, bf16[192,640]{1,0:T(8,128)(2,1)S(1)}, bf16[192,768]{1,0:T(8,128)(2,1)S(1)}, f32[8,768]{1,0:T(8,128)S(1)}) custom-call(bf16[96,768]{1,0:T(8,128)(2,1)S(1)} %get-tuple-element.249.own_ref.refs_2_, bf16[96,768]{1,0:T(8,128)(2,1)S(1)} %collective-permute-done.27.far_ref.refs_3_, ...), custom_call_target="tpu_custom_call" | custom-call | flops 5000000000 | bytes 10000000 | tf_op jit(solution)/shard_map/backward/pallas_call | solution.py:577
  144.5 3.7 %backward.6 = (f32[96,768]{1,0:T(8,128)S(1)}, f32[96,768]{1,0:T(8,128)S(1)}, bf16[192,640]{1,0:T(8,128)(2,1)S(1)}, bf16[192,768]{1,0:T(8,128)(2,1)S(1)}, f32[8,768]{1,0:T(8,128)S(1)}) custom-call(bf16[96,768]{1,0:T(8,128)(2,1)S(1)} %get-tuple-element.250.own_ref.refs_11_, bf16[96,768]{1,0:T(8,128)(2,1)S(1)} %collective-permute-done.33.far_ref.refs_12_, ...), custom_call_target="tpu_custom_call" | custom-call | flops 5000000000 | bytes 10000000 | tf_op jit(solution)/shard_map/backward/pallas_call | solution.py:577
  148.8 1.6 collective-permute-start.26
  151.1 1.6 collective-permute-start.29
  153.3 2.7 %weights.2 = bf16[768,2432]{1,0:T(8,128)(2,1)S(1)} custom-call(bf16[192,768]{1,0:T(8,128)(2,1)S(1)} %get-tuple-element.186.refs_0_, bf16[192,768]{1,0:T(8,128)(2,1)S(1)} %get-tuple-element.187.refs_1_, bf16[96,768]{1,0:T(8,128)(2,1)S(1)} %get-tuple-element.249.own_ref.refs_2_, bf16[96,768]{1,0:T(8,128)(2,1)S(1)} %collective-permute-done.27.far_ref.refs_3_, ...), custom_call_target="tpu_custom_call" | custom-call | flops 8000000000 | bytes 10000000 | tf_op jit(solution)/shard_map/weights/pallas_call | solution.py:613
  156.1 1.5 collective-permute-start.39
  157.6 4.4 %collective-permute-done.29 = bf16[96,768]{1,0:T(8,128)(2,1)S(1)} collective-permute-done((bf16[96,768]{1,0:T(8,128)(2,1)S(1)}, bf16[96,768]{1,0:T(8,128)(2,1)S(1)}, u32[]{:S(2)}, u32[]{:S(2)}) %collective-permute-start.29) | collective-permute-done | bytes 147488 | tf_op jit(solution)/shard_map/ppermute | solution.py:157
  162.3 1.9 collective-permute-done.35
  165.7 3.7 %backward.7 = (f32[96,768]{1,0:T(8,128)S(1)}, f32[96,768]{1,0:T(8,128)S(1)}, bf16[192,640]{1,0:T(8,128)(2,1)S(1)}, bf16[192,768]{1,0:T(8,128)(2,1)S(1)}, f32[8,768]{1,0:T(8,128)S(1)}) custom-call(bf16[96,768]{1,0:T(8,128)(2,1)S(1)} %get-tuple-element.248.own_ref.refs_11_, bf16[96,768]{1,0:T(8,128)(2,1)S(1)} %collective-permute-done.36.far_ref.refs_12_, ...), custom_call_target="tpu_custom_call" | custom-call | flops 5000000000 | bytes 10000000 | tf_op jit(solution)/shard_map/backward/pallas_call | solution.py:577
  169.6 3.7 %backward.5 = (f32[96,768]{1,0:T(8,128)S(1)}, f32[96,768]{1,0:T(8,128)S(1)}, bf16[192,640]{1,0:T(8,128)(2,1)S(1)}, bf16[192,768]{1,0:T(8,128)(2,1)S(1)}, f32[8,768]{1,0:T(8,128)S(1)}) custom-call(bf16[96,768]{1,0:T(8,128)(2,1)S(1)} %get-tuple-element.247.own_ref.refs_2_, bf16[96,768]{1,0:T(8,128)(2,1)S(1)} %collective-permute-done.30.far_ref.refs_3_, ...), custom_call_target="tpu_custom_call" | custom-call | flops 5000000000 | bytes 10000000 | tf_op jit(solution)/shard_map/backward/pallas_call | solution.py:577
  173.6 1.5 collective-permute-start.43
  175.7 2.7 %weights.3 = bf16[768,2432]{1,0:T(8,128)(2,1)S(1)} custom-call(bf16[192,768]{1,0:T(8,128)(2,1)S(1)} %get-tuple-element.172.refs_0_, bf16[192,768]{1,0:T(8,128)(2,1)S(1)} %get-tuple-element.173.refs_1_, bf16[96,768]{1,0:T(8,128)(2,1)S(1)} %get-tuple-element.247.own_ref.refs_2_, bf16[96,768]{1,0:T(8,128)(2,1)S(1)} %collective-permute-done.30.far_ref.refs_3_, ...), custom_call_target="tpu_custom_call" | custom-call | flops 8000000000 | bytes 10000000 | tf_op jit(solution)/shard_map/weights/pallas_call | solution.py:613
  178.6 1.4 collective-permute-start.41
  180.0 7.2 %collective-permute-done.43 = bf16[96,2432]{1,0:T(8,128)(2,1)S(1)} collective-permute-done((bf16[96,2432]{1,0:T(8,128)(2,1)S(1)}, bf16[96,2432]{1,0:T(8,128)(2,1)S(1)}, u32[]{:S(2)}, u32[]{:S(2)}) %collective-permute-start.43) | collective-permute-done | bytes 466976 | tf_op jit(solution)/shard_map/ppermute | solution.py:139
  188.0 1.5 collective-permute-start.47
  189.5 7.7 %collective-permute-done.41 = bf16[96,2432]{1,0:T(8,128)(2,1)S(1)} collective-permute-done((bf16[96,2432]{1,0:T(8,128)(2,1)S(1)}, bf16[96,2432]{1,0:T(8,128)(2,1)S(1)}, u32[]{:S(2)}, u32[]{:S(2)}) %collective-permute-start.41) | collective-permute-done | bytes 466976 | tf_op jit(solution)/shard_map/ppermute | solution.py:139
  197.6 1.2 collective-permute-done.42
  199.0 1.5 collective-permute-start.45
  200.5 6.7 %collective-permute-done.47 = bf16[96,2432]{1,0:T(8,128)(2,1)S(1)} collective-permute-done((bf16[96,2432]{1,0:T(8,128)(2,1)S(1)}, bf16[96,2432]{1,0:T(8,128)(2,1)S(1)}, u32[]{:S(2)}, u32[]{:S(2)}) %collective-permute-start.47) | collective-permute-done | bytes 466976 | tf_op jit(solution)/shard_map/ppermute | solution.py:139
  207.6 1.2 collective-permute-done.48
  208.9 7.7 %collective-permute-done.45 = bf16[96,2432]{1,0:T(8,128)(2,1)S(1)} collective-permute-done((bf16[96,2432]{1,0:T(8,128)(2,1)S(1)}, bf16[96,2432]{1,0:T(8,128)(2,1)S(1)}, u32[]{:S(2)}, u32[]{:S(2)}) %collective-permute-start.45) | collective-permute-done | bytes 466976 | tf_op jit(solution)/shard_map/ppermute | solution.py:139
  216.6 2.1 collective-permute-done.46
  219.1 1.5 collective-permute-start.49
  222.0 1.6 collective-permute-start.38
  223.6 1.4 collective-permute-start.52
  225.1 7.7 %collective-permute-done.49 = bf16[96,2432]{1,0:T(8,128)(2,1)S(1)} collective-permute-done((bf16[96,2432]{1,0:T(8,128)(2,1)S(1)}, bf16[96,2432]{1,0:T(8,128)(2,1)S(1)}, u32[]{:S(2)}, u32[]{:S(2)}) %collective-permute-start.49) | collective-permute-done | bytes 466976 | tf_op jit(solution)/shard_map/ppermute | solution.py:139
  233.3 1.6 collective-permute-start.32
  235.0 4.8 %collective-permute-done.52 = bf16[96,2432]{1,0:T(8,128)(2,1)S(1)} collective-permute-done((bf16[96,2432]{1,0:T(8,128)(2,1)S(1)}, bf16[96,2432]{1,0:T(8,128)(2,1)S(1)}, u32[]{:S(2)}, u32[]{:S(2)}) %collective-permute-start.52) | collective-permute-done | bytes 466976 | tf_op jit(solution)/shard_map/ppermute | solution.py:139
  239.8 1.7 collective-permute-done.51
  242.2 1.6 collective-permute-start.53
  245.7 10.1 %collective-permute-done.55.came_small_ref = f32[96,128]{1,0:T(8,128)S(1)} collective-permute-done((f32[96,128]{1,0:T(8,128)S(1)}, f32[96,128]{1,0:T(8,128)S(1)}, u32[]{:S(2)}, u32[]{:S(2)}) %collective-permute-start.55) | collective-permute-done | bytes 49184 | tf_op jit(solution)/shard_map/ppermute | solution.py:157
  255.8 1.5 unpack.1
  (173 shorter events, 39.3 us)
Async XLA Ops:
  0.6 26.9 %copy-start.15 = (s32[2,1,3]{2,1,0:T(1,128)S(1)}, s32[2,1,3]{2,1,0:T(1,128)}, u32[]{:S(2)}) copy-start(s32[2,1,3]{2,1,0:T(1,128)} %param.15) | copy-start | bytes 76
  10.4 13.7 %collective-permute-start.1 = (bf16[96,2432]{1,0:T(8,128)(2,1)S(1)}, bf16[96,2432]{1,0:T(8,128)(2,1)S(1)}, u32[]{:S(2)}, u32[]{:S(2)}) collective-permute-start(bf16[96,2432]{1,0:T(8,128)(2,1)S(1)} %get-tuple-element.119), channel_id=1, source_target_pairs={{0,16},{16,0},{1,17},{17,1},{2,18},{18,2},{3,19},{19,3},{4,20},{20... | collective-permute-start | bytes 1400840 | tf_op jit(solution)/shard_map/ppermute | solution.py:157
  14.4 95.7 %collective-permute-start = (bf16[96,768]{1,0:T(8,128)(2,1)S(1)}, bf16[96,768]{1,0:T(8,128)(2,1)S(1)}, u32[]{:S(2)}, u32[]{:S(2)}) collective-permute-start(bf16[96,768]{1,0:T(8,128)(2,1)S(1)} %get-tuple-element.253.own_ref), channel_id=1, source_target_pairs={{0,1},{1,0},{2,3},{3,2},{4,5},{5,4},{6,7},{7,6},{8,9},{9,8},{10,11... | collective-permute-start | bytes 442376 | tf_op jit(solution)/shard_map/ppermute | solution.py:157
  25.6 12.2 %collective-permute-start.2 = (bf16[96,2432]{1,0:T(8,128)(2,1)}, bf16[96,2432]{1,0:T(8,128)(2,1)}, u32[]{:S(2)}, u32[]{:S(2)}) collective-permute-start(bf16[96,2432]{1,0:T(8,128)(2,1)} %get-tuple-element.246), channel_id=1, source_target_pairs={{0,4},{4,8},{8,12},{12,14},{14,10},{10,6},{6,2},{2,0},{1,5},{5,9},... | collective-permute-start | bytes 1400840 | tf_op jit(solution)/shard_map/ppermute | solution.py:100
  27.3 11.6 %collective-permute-start.3 = (bf16[96,2432]{1,0:T(8,128)(2,1)}, bf16[96,2432]{1,0:T(8,128)(2,1)}, u32[]{:S(2)}, u32[]{:S(2)}) collective-permute-start(bf16[96,2432]{1,0:T(8,128)(2,1)} %get-tuple-element.246), channel_id=1, source_target_pairs={{4,0},{8,4},{12,8},{14,12},{10,14},{6,10},{2,6},{0,2},{5,1},{9,5},... | collective-permute-start | bytes 1400840 | tf_op jit(solution)/shard_map/ppermute | solution.py:103
  29.6 3.3 %copy-start.9 = (f32[192,48]{1,0:T(8,128)}, f32[192,48]{1,0:T(8,128)S(1)}, u32[]{:S(2)}) copy-start(f32[192,48]{1,0:T(8,128)S(1)} %broadcast.139) | copy-start | bytes 110596
  29.6 3.2 %copy-start.10 = (f32[192,64]{1,0:T(8,128)}, f32[192,64]{1,0:T(8,128)S(1)}, u32[]{:S(2)}) copy-start(f32[192,64]{1,0:T(8,128)S(1)} %broadcast.140) | copy-start | bytes 147460
  38.9 21.9 %collective-permute-start.8 = (bf16[96,2432]{1,0:T(8,128)(2,1)}, bf16[96,2432]{1,0:T(8,128)(2,1)S(1)}, u32[]{:S(2)}, u32[]{:S(2)}) collective-permute-start(bf16[96,2432]{1,0:T(8,128)(2,1)} %get-tuple-element.124), channel_id=1, source_target_pairs={{0,4},{4,8},{8,12},{12,14},{14,10},{10,6},{6,2},{2,0},{1,5},{5,9},... | collective-permute-start | bytes 1400840 | tf_op jit(solution)/shard_map/ppermute | solution.py:100
  40.5 21.9 %collective-permute-start.9 = (bf16[96,2432]{1,0:T(8,128)(2,1)}, bf16[96,2432]{1,0:T(8,128)(2,1)S(1)}, u32[]{:S(2)}, u32[]{:S(2)}) collective-permute-start(bf16[96,2432]{1,0:T(8,128)(2,1)} %get-tuple-element.124), channel_id=1, source_target_pairs={{4,0},{8,4},{12,8},{14,12},{10,14},{6,10},{2,6},{0,2},{5,1},{9,5},... | collective-permute-start | bytes 1400840 | tf_op jit(solution)/shard_map/ppermute | solution.py:103
  41.0 18.6 %collective-permute-start.4 = (bf16[96,2432]{1,0:T(8,128)(2,1)}, bf16[96,2432]{1,0:T(8,128)(2,1)S(1)}, u32[]{:S(2)}, u32[]{:S(2)}) collective-permute-start(bf16[96,2432]{1,0:T(8,128)(2,1)} %collective-permute-done.2), channel_id=1, source_target_pairs={{0,4},{4,8},{8,12},{12,14},{14,10},{10,6},{6,2},{2,0},{1,5},{5,9},... | collective-permute-start | bytes 1400840 | tf_op jit(solution)/shard_map/ppermute | solution.py:100
  42.5 18.3 %collective-permute-start.5 = (bf16[96,2432]{1,0:T(8,128)(2,1)}, bf16[96,2432]{1,0:T(8,128)(2,1)S(1)}, u32[]{:S(2)}, u32[]{:S(2)}) collective-permute-start(bf16[96,2432]{1,0:T(8,128)(2,1)} %collective-permute-done.3), channel_id=1, source_target_pairs={{4,0},{8,4},{12,8},{14,12},{10,14},{6,10},{2,6},{0,2},{5,1},{9,5},... | collective-permute-start | bytes 1400840 | tf_op jit(solution)/shard_map/ppermute | solution.py:103
  59.5 55.3 %collective-permute-start.13 = (bf16[96,768]{1,0:T(8,128)(2,1)S(1)}, bf16[96,768]{1,0:T(8,128)(2,1)S(1)}, u32[]{:S(2)}, u32[]{:S(2)}) collective-permute-start(bf16[96,768]{1,0:T(8,128)(2,1)S(1)} %get-tuple-element.254.own_ref), channel_id=1, source_target_pairs={{0,1},{1,0},{2,3},{3,2},{4,5},{5,4},{6,7},{7,6},{8,9},{9,8},{10,11... | collective-permute-start | bytes 442376 | tf_op jit(solution)/shard_map/ppermute | solution.py:157
  60.8 79.9 %collective-permute-start.27 = (bf16[96,768]{1,0:T(8,128)(2,1)S(1)}, bf16[96,768]{1,0:T(8,128)(2,1)S(1)}, u32[]{:S(2)}, u32[]{:S(2)}) collective-permute-start(bf16[96,768]{1,0:T(8,128)(2,1)S(1)} %get-tuple-element.249.own_ref.refs_2_), channel_id=1, source_target_pairs={{0,1},{1,0},{2,3},{3,2},{4,5},{5,4},{6,7},{7,6},{8,9},{9,8},{10,11... | collective-permute-start | bytes 442376 | tf_op jit(solution)/shard_map/ppermute | solution.py:157
  60.8 24.4 %collective-permute-start.6 = (bf16[96,2432]{1,0:T(8,128)(2,1)S(1)}, bf16[96,2432]{1,0:T(8,128)(2,1)S(1)}, u32[]{:S(2)}, u32[]{:S(2)}) collective-permute-start(bf16[96,2432]{1,0:T(8,128)(2,1)S(1)} %collective-permute-done.4), channel_id=1, source_target_pairs={{0,4},{4,8},{8,12},{12,14},{14,10},{10,6},{6,2},{2,0},{1,5},{5,9},... | collective-permute-start | bytes 1400840 | tf_op jit(solution)/shard_map/ppermute | solution.py:100
  62.4 21.5 %collective-permute-start.17 = (bf16[96,2432]{1,0:T(8,128)(2,1)S(1)}, bf16[96,2432]{1,0:T(8,128)(2,1)S(1)}, u32[]{:S(2)}, u32[]{:S(2)}) collective-permute-start(bf16[96,2432]{1,0:T(8,128)(2,1)S(1)} %collective-permute-done.8), channel_id=1, source_target_pairs={{0,4},{4,8},{8,12},{12,14},{14,10},{10,6},{6,2},{2,0},{1,5},{5,9},... | collective-permute-start | bytes 1400840 | tf_op jit(solution)/shard_map/ppermute | solution.py:100
  83.9 13.6 %collective-permute-start.18 = (bf16[96,2432]{1,0:T(8,128)(2,1)S(1)}, bf16[96,2432]{1,0:T(8,128)(2,1)S(1)}, u32[]{:S(2)}, u32[]{:S(2)}) collective-permute-start(bf16[96,2432]{1,0:T(8,128)(2,1)S(1)} %collective-permute-done.9), channel_id=1, source_target_pairs={{4,0},{8,4},{12,8},{14,12},{10,14},{6,10},{2,6},{0,2},{5,1},{9,5},... | collective-permute-start | bytes 1400840 | tf_op jit(solution)/shard_map/ppermute | solution.py:103
  85.2 21.1 %collective-permute-start.7 = (bf16[96,2432]{1,0:T(8,128)(2,1)S(1)}, bf16[96,2432]{1,0:T(8,128)(2,1)S(1)}, u32[]{:S(2)}, u32[]{:S(2)}) collective-permute-start(bf16[96,2432]{1,0:T(8,128)(2,1)S(1)} %collective-permute-done.5), channel_id=1, source_target_pairs={{4,0},{8,4},{12,8},{14,12},{10,14},{6,10},{2,6},{0,2},{5,1},{9,5},... | collective-permute-start | bytes 1400840 | tf_op jit(solution)/shard_map/ppermute | solution.py:103
  97.5 10.2 %collective-permute-start.10 = (bf16[96,2432]{1,0:T(8,128)(2,1)S(1)}, bf16[96,2432]{1,0:T(8,128)(2,1)S(1)}, u32[]{:S(2)}, u32[]{:S(2)}) collective-permute-start(bf16[96,2432]{1,0:T(8,128)(2,1)S(1)} %collective-permute-done.6), channel_id=1, source_target_pairs={{0,4},{4,8},{8,12},{12,14},{14,10},{10,6},{6,2},{2,0},{1,5},{5,9},... | collective-permute-start | bytes 1400840 | tf_op jit(solution)/shard_map/ppermute | solution.py:100
  106.3 38.3 %collective-permute-start.33 = (bf16[96,768]{1,0:T(8,128)(2,1)S(1)}, bf16[96,768]{1,0:T(8,128)(2,1)S(1)}, u32[]{:S(2)}, u32[]{:S(2)}) collective-permute-start(bf16[96,768]{1,0:T(8,128)(2,1)S(1)} %get-tuple-element.250.own_ref.refs_11_), channel_id=1, source_target_pairs={{0,1},{1,0},{2,3},{3,2},{4,5},{5,4},{6,7},{7,6},{8,9},{9,8},{10,11... | collective-permute-start | bytes 442376 | tf_op jit(solution)/shard_map/ppermute | solution.py:157
  107.7 14.7 %collective-permute-start.19 = (bf16[96,2432]{1,0:T(8,128)(2,1)S(1)}, bf16[96,2432]{1,0:T(8,128)(2,1)S(1)}, u32[]{:S(2)}, u32[]{:S(2)}) collective-permute-start(bf16[96,2432]{1,0:T(8,128)(2,1)S(1)} %collective-permute-done.17), channel_id=1, source_target_pairs={{0,4},{4,8},{8,12},{12,14},{14,10},{10,6},{6,2},{2,0},{1,5},{5,9},... | collective-permute-start | bytes 1400840 | tf_op jit(solution)/shard_map/ppermute | solution.py:100
  110.1 12.3 %collective-permute-start.20 = (bf16[96,2432]{1,0:T(8,128)(2,1)S(1)}, bf16[96,2432]{1,0:T(8,128)(2,1)S(1)}, u32[]{:S(2)}, u32[]{:S(2)}) collective-permute-start(bf16[96,2432]{1,0:T(8,128)(2,1)S(1)} %collective-permute-done.18), channel_id=1, source_target_pairs={{4,0},{8,4},{12,8},{14,12},{10,14},{6,10},{2,6},{0,2},{5,1},{9,5},... | collective-permute-start | bytes 1400840 | tf_op jit(solution)/shard_map/ppermute | solution.py:103
  110.5 2.1 copy-start.5
  112.6 2.3 copy-start.6
  114.8 8.0 %collective-permute-start.11 = (f32[96,768]{1,0:T(8,128)S(1)}, f32[96,768]{1,0:T(8,128)S(1)}, u32[]{:S(2)}, u32[]{:S(2)}) collective-permute-start(f32[96,768]{1,0:T(8,128)S(1)} %get-tuple-element.133), channel_id=1, source_target_pairs={{0,1},{1,0},{2,3},{3,2},{4,5},{5,4},{6,7},{7,6},{8,9},{9,8},{10,11... | collective-permute-start | bytes 884744 | tf_op jit(solution)/shard_map/ppermute | solution.py:157
  114.9 7.8 %copy-start.8 = (bf16[768,2432]{1,0:T(8,128)(2,1)S(1)}, bf16[768,2432]{1,0:T(8,128)(2,1)}, u32[]{:S(2)}) copy-start(bf16[768,2432]{1,0:T(8,128)(2,1)} %constant_dynamic-update-slice_fusion.3) | copy-start | bytes 11206660
  114.9 17.2 %copy-start.13 = (bf16[2,96,768]{2,1,0:T(8,128)(2,1)S(1)}, bf16[2,96,768]{2,1,0:T(8,128)(2,1)}, u32[]{:S(2)}) copy-start(bf16[2,96,768]{2,1,0:T(8,128)(2,1)} %param.14) | copy-start | bytes 884740
  122.4 2.2 collective-permute-start.14
  122.4 13.1 %collective-permute-start.21 = (bf16[96,2432]{1,0:T(8,128)(2,1)S(1)}, bf16[96,2432]{1,0:T(8,128)(2,1)S(1)}, u32[]{:S(2)}, u32[]{:S(2)}) collective-permute-start(bf16[96,2432]{1,0:T(8,128)(2,1)S(1)} %collective-permute-done.20), channel_id=1, source_target_pairs={{4,0},{8,4},{12,8},{14,12},{10,14},{6,10},{2,6},{0,2},{5,1},{9,5},... | collective-permute-start | bytes 1400840 | tf_op jit(solution)/shard_map/ppermute | solution.py:103
  122.9 6.7 %collective-permute-start.12 = (bf16[96,768]{1,0:T(8,128)(2,1)S(1)}, bf16[96,768]{1,0:T(8,128)(2,1)S(1)}, u32[]{:S(2)}, u32[]{:S(2)}) collective-permute-start(bf16[96,768]{1,0:T(8,128)(2,1)S(1)} %add_convert_fusion.25), channel_id=1, source_target_pairs={{0,16},{16,0},{1,17},{17,1},{2,18},{18,2},{3,19},{19,3},{4,20},{20... | collective-permute-start | bytes 442376 | tf_op jit(solution)/shard_map/ppermute | solution.py:157
  124.6 7.5 %collective-permute-start.15 = (bf16[96,768]{1,0:T(8,128)(2,1)S(1)}, bf16[96,768]{1,0:T(8,128)(2,1)S(1)}, u32[]{:S(2)}, u32[]{:S(2)}) collective-permute-start(bf16[96,768]{1,0:T(8,128)(2,1)S(1)} %add_convert_fusion.23), channel_id=1, source_target_pairs={{0,16},{16,0},{1,17},{17,1},{2,18},{18,2},{3,19},{19,3},{4,20},{20... | collective-permute-start | bytes 442376 | tf_op jit(solution)/shard_map/ppermute | solution.py:157
  132.2 3.3 %collective-permute-start.24 = (bf16[96,768]{1,0:T(8,128)(2,1)S(1)}, bf16[96,768]{1,0:T(8,128)(2,1)S(1)}, u32[]{:S(2)}, u32[]{:S(2)}) collective-permute-start(bf16[96,768]{1,0:T(8,128)(2,1)S(1)} %get-tuple-element.252.own_ref), channel_id=1, source_target_pairs={{0,1},{1,0},{2,3},{3,2},{4,5},{5,4},{6,7},{7,6},{8,9},{9,8},{10,11... | collective-permute-start | bytes 442376 | tf_op jit(solution)/shard_map/ppermute | solution.py:157
  132.3 5.6 %collective-permute-start.16 = (bf16[96,768]{1,0:T(8,128)(2,1)S(1)}, bf16[96,768]{1,0:T(8,128)(2,1)S(1)}, u32[]{:S(2)}, u32[]{:S(2)}) collective-permute-start(bf16[96,768]{1,0:T(8,128)(2,1)S(1)} %get-tuple-element.251.own_ref), channel_id=1, source_target_pairs={{0,1},{1,0},{2,3},{3,2},{4,5},{5,4},{6,7},{7,6},{8,9},{9,8},{10,11... | collective-permute-start | bytes 442376 | tf_op jit(solution)/shard_map/ppermute | solution.py:157
  137.8 11.0 %collective-permute-start.25 = (f32[96,768]{1,0:T(8,128)S(1)}, f32[96,768]{1,0:T(8,128)S(1)}, u32[]{:S(2)}, u32[]{:S(2)}) collective-permute-start(f32[96,768]{1,0:T(8,128)S(1)} %get-tuple-element.146), channel_id=1, source_target_pairs={{0,1},{1,0},{2,3},{3,2},{4,5},{5,4},{6,7},{7,6},{8,9},{9,8},{10,11... | collective-permute-start | bytes 884744 | tf_op jit(solution)/shard_map/ppermute | solution.py:157
  140.1 10.3 %collective-permute-start.22 = (f32[96,768]{1,0:T(8,128)S(1)}, f32[96,768]{1,0:T(8,128)S(1)}, u32[]{:S(2)}, u32[]{:S(2)}) collective-permute-start(f32[96,768]{1,0:T(8,128)S(1)} %get-tuple-element.143), channel_id=1, source_target_pairs={{0,1},{1,0},{2,3},{3,2},{4,5},{5,4},{6,7},{7,6},{8,9},{9,8},{10,11... | collective-permute-start | bytes 884744 | tf_op jit(solution)/shard_map/ppermute | solution.py:157
  144.4 6.6 %collective-permute-start.28 = (f32[96,768]{1,0:T(8,128)S(1)}, f32[96,768]{1,0:T(8,128)S(1)}, u32[]{:S(2)}, u32[]{:S(2)}) collective-permute-start(f32[96,768]{1,0:T(8,128)S(1)} %get-tuple-element.153), channel_id=1, source_target_pairs={{0,1},{1,0},{2,3},{3,2},{4,5},{5,4},{6,7},{7,6},{8,9},{9,8},{10,11... | collective-permute-start | bytes 884744 | tf_op jit(solution)/shard_map/ppermute | solution.py:157
  148.2 4.5 %collective-permute-start.34 = (f32[96,768]{1,0:T(8,128)S(1)}, f32[96,768]{1,0:T(8,128)S(1)}, u32[]{:S(2)}, u32[]{:S(2)}) collective-permute-start(f32[96,768]{1,0:T(8,128)S(1)} %get-tuple-element.165), channel_id=1, source_target_pairs={{0,1},{1,0},{2,3},{3,2},{4,5},{5,4},{6,7},{7,6},{8,9},{9,8},{10,11... | collective-permute-start | bytes 884744 | tf_op jit(solution)/shard_map/ppermute | solution.py:157
  148.8 15.5 %collective-permute-start.26 = (bf16[96,768]{1,0:T(8,128)(2,1)S(1)}, bf16[96,768]{1,0:T(8,128)(2,1)S(1)}, u32[]{:S(2)}, u32[]{:S(2)}) collective-permute-start(bf16[96,768]{1,0:T(8,128)(2,1)S(1)} %add_convert_fusion.19), channel_id=1, source_target_pairs={{0,16},{16,0},{1,17},{17,1},{2,18},{18,2},{3,19},{19,3},{4,20},{20... | collective-permute-start | bytes 442376 | tf_op jit(solution)/shard_map/ppermute | solution.py:157
  150.5 70.6 %collective-permute-start.23 = (bf16[96,768]{1,0:T(8,128)(2,1)S(1)}, bf16[96,768]{1,0:T(8,128)(2,1)S(1)}, u32[]{:S(2)}, u32[]{:S(2)}) collective-permute-start(bf16[96,768]{1,0:T(8,128)(2,1)S(1)} %add_convert_fusion.21), channel_id=1, source_target_pairs={{0,16},{16,0},{1,17},{17,1},{2,18},{18,2},{3,19},{19,3},{4,20},{20... | collective-permute-start | bytes 442376 | tf_op jit(solution)/shard_map/ppermute | solution.py:157
  151.1 10.9 %collective-permute-start.29 = (bf16[96,768]{1,0:T(8,128)(2,1)S(1)}, bf16[96,768]{1,0:T(8,128)(2,1)S(1)}, u32[]{:S(2)}, u32[]{:S(2)}) collective-permute-start(bf16[96,768]{1,0:T(8,128)(2,1)S(1)} %add_convert_fusion.17), channel_id=1, source_target_pairs={{0,16},{16,0},{1,17},{17,1},{2,18},{18,2},{3,19},{19,3},{4,20},{20... | collective-permute-start | bytes 442376 | tf_op jit(solution)/shard_map/ppermute | solution.py:157
  152.7 11.4 %collective-permute-start.35 = (bf16[96,768]{1,0:T(8,128)(2,1)S(1)}, bf16[96,768]{1,0:T(8,128)(2,1)S(1)}, u32[]{:S(2)}, u32[]{:S(2)}) collective-permute-start(bf16[96,768]{1,0:T(8,128)(2,1)S(1)} %add_convert_fusion.13), channel_id=1, source_target_pairs={{0,16},{16,0},{1,17},{17,1},{2,18},{18,2},{3,19},{19,3},{4,20},{20... | collective-permute-start | bytes 442376 | tf_op jit(solution)/shard_map/ppermute | solution.py:157
  153.3 10.9 %copy-start.14 = (bf16[2,96,768]{2,1,0:T(8,128)(2,1)S(1)}, bf16[2,96,768]{2,1,0:T(8,128)(2,1)}, u32[]{:S(2)}) copy-start(bf16[2,96,768]{2,1,0:T(8,128)(2,1)} %param.27) | copy-start | bytes 884740
  156.1 17.3 %collective-permute-start.39 = (bf16[96,2432]{1,0:T(8,128)(2,1)S(1)}, bf16[96,2432]{1,0:T(8,128)(2,1)S(1)}, u32[]{:S(2)}, u32[]{:S(2)}) collective-permute-start(bf16[96,2432]{1,0:T(8,128)(2,1)S(1)} %get-tuple-element.244), channel_id=1, source_target_pairs={{0,4},{4,8},{8,12},{12,14},{14,10},{10,6},{6,2},{2,0},{1,5},{5,9},... | collective-permute-start | bytes 1400840 | tf_op jit(solution)/shard_map/ppermute | solution.py:139
  161.9 11.4 %collective-permute-start.40 = (bf16[96,2432]{1,0:T(8,128)(2,1)S(1)}, bf16[96,2432]{1,0:T(8,128)(2,1)S(1)}, u32[]{:S(2)}, u32[]{:S(2)}) collective-permute-start(bf16[96,2432]{1,0:T(8,128)(2,1)S(1)} %get-tuple-element.243), channel_id=1, source_target_pairs={{4,0},{8,4},{12,8},{14,12},{10,14},{6,10},{2,6},{0,2},{5,1},{9,5},... | collective-permute-start | bytes 1400840 | tf_op jit(solution)/shard_map/ppermute | solution.py:145
  164.3 1.4 collective-permute-start.36
  164.4 5.3 %collective-permute-start.30 = (bf16[96,768]{1,0:T(8,128)(2,1)S(1)}, bf16[96,768]{1,0:T(8,128)(2,1)S(1)}, u32[]{:S(2)}, u32[]{:S(2)}) collective-permute-start(bf16[96,768]{1,0:T(8,128)(2,1)S(1)} %get-tuple-element.247.own_ref.refs_2_), channel_id=1, source_target_pairs={{0,1},{1,0},{2,3},{3,2},{4,5},{5,4},{6,7},{7,6},{8,9},{9,8},{10,11... | collective-permute-start | bytes 442376 | tf_op jit(solution)/shard_map/ppermute | solution.py:157
  169.4 52.6 %collective-permute-start.37 = (f32[96,768]{1,0:T(8,128)S(1)}, f32[96,768]{1,0:T(8,128)S(1)}, u32[]{:S(2)}, u32[]{:S(2)}) collective-permute-start(f32[96,768]{1,0:T(8,128)S(1)} %get-tuple-element.171), channel_id=1, source_target_pairs={{0,1},{1,0},{2,3},{3,2},{4,5},{5,4},{6,7},{7,6},{8,9},{9,8},{10,11... | collective-permute-start | bytes 884744 | tf_op jit(solution)/shard_map/ppermute | solution.py:157
  173.6 13.6 %collective-permute-start.43 = (bf16[96,2432]{1,0:T(8,128)(2,1)S(1)}, bf16[96,2432]{1,0:T(8,128)(2,1)S(1)}, u32[]{:S(2)}, u32[]{:S(2)}) collective-permute-start(bf16[96,2432]{1,0:T(8,128)(2,1)S(1)} %get-tuple-element.242), channel_id=1, source_target_pairs={{0,4},{4,8},{8,12},{12,14},{14,10},{10,6},{6,2},{2,0},{1,5},{5,9},... | collective-permute-start | bytes 1400840 | tf_op jit(solution)/shard_map/ppermute | solution.py:139
  175.1 12.7 %collective-permute-start.44 = (bf16[96,2432]{1,0:T(8,128)(2,1)S(1)}, bf16[96,2432]{1,0:T(8,128)(2,1)S(1)}, u32[]{:S(2)}, u32[]{:S(2)}) collective-permute-start(bf16[96,2432]{1,0:T(8,128)(2,1)S(1)} %get-tuple-element.241), channel_id=1, source_target_pairs={{4,0},{8,4},{12,8},{14,12},{10,14},{6,10},{2,6},{0,2},{5,1},{9,5},... | collective-permute-start | bytes 1400840 | tf_op jit(solution)/shard_map/ppermute | solution.py:145
  178.6 18.7 %collective-permute-start.41 = (bf16[96,2432]{1,0:T(8,128)(2,1)S(1)}, bf16[96,2432]{1,0:T(8,128)(2,1)S(1)}, u32[]{:S(2)}, u32[]{:S(2)}) collective-permute-start(bf16[96,2432]{1,0:T(8,128)(2,1)S(1)} %get-tuple-element.240), channel_id=1, source_target_pairs={{0,4},{4,8},{8,12},{12,14},{14,10},{10,6},{6,2},{2,0},{1,5},{5,9},... | collective-permute-start | bytes 1400840 | tf_op jit(solution)/shard_map/ppermute | solution.py:139
  187.2 11.6 %collective-permute-start.42 = (bf16[96,2432]{1,0:T(8,128)(2,1)S(1)}, bf16[96,2432]{1,0:T(8,128)(2,1)S(1)}, u32[]{:S(2)}, u32[]{:S(2)}) collective-permute-start(bf16[96,2432]{1,0:T(8,128)(2,1)S(1)} %get-tuple-element.239), channel_id=1, source_target_pairs={{4,0},{8,4},{12,8},{14,12},{10,14},{6,10},{2,6},{0,2},{5,1},{9,5},... | collective-permute-start | bytes 1400840 | tf_op jit(solution)/shard_map/ppermute | solution.py:145
  188.0 19.2 %collective-permute-start.47 = (bf16[96,2432]{1,0:T(8,128)(2,1)S(1)}, bf16[96,2432]{1,0:T(8,128)(2,1)S(1)}, u32[]{:S(2)}, u32[]{:S(2)}) collective-permute-start(bf16[96,2432]{1,0:T(8,128)(2,1)S(1)} %get-tuple-element.238), channel_id=1, source_target_pairs={{0,4},{4,8},{8,12},{12,14},{14,10},{10,6},{6,2},{2,0},{1,5},{5,9},... | collective-permute-start | bytes 1400840 | tf_op jit(solution)/shard_map/ppermute | solution.py:139
  197.2 11.6 %collective-permute-start.48 = (bf16[96,2432]{1,0:T(8,128)(2,1)S(1)}, bf16[96,2432]{1,0:T(8,128)(2,1)S(1)}, u32[]{:S(2)}, u32[]{:S(2)}) collective-permute-start(bf16[96,2432]{1,0:T(8,128)(2,1)S(1)} %get-tuple-element.237), channel_id=1, source_target_pairs={{4,0},{8,4},{12,8},{14,12},{10,14},{6,10},{2,6},{0,2},{5,1},{9,5},... | collective-permute-start | bytes 1400840 | tf_op jit(solution)/shard_map/ppermute | solution.py:145
  199.0 17.6 %collective-permute-start.45 = (bf16[96,2432]{1,0:T(8,128)(2,1)S(1)}, bf16[96,2432]{1,0:T(8,128)(2,1)S(1)}, u32[]{:S(2)}, u32[]{:S(2)}) collective-permute-start(bf16[96,2432]{1,0:T(8,128)(2,1)S(1)} %get-tuple-element.236), channel_id=1, source_target_pairs={{0,4},{4,8},{8,12},{12,14},{14,10},{10,6},{6,2},{2,0},{1,5},{5,9},... | collective-permute-start | bytes 1400840 | tf_op jit(solution)/shard_map/ppermute | solution.py:139
  207.2 11.6 %collective-permute-start.46 = (bf16[96,2432]{1,0:T(8,128)(2,1)S(1)}, bf16[96,2432]{1,0:T(8,128)(2,1)S(1)}, u32[]{:S(2)}, u32[]{:S(2)}) collective-permute-start(bf16[96,2432]{1,0:T(8,128)(2,1)S(1)} %get-tuple-element.235), channel_id=1, source_target_pairs={{4,0},{8,4},{12,8},{14,12},{10,14},{6,10},{2,6},{0,2},{5,1},{9,5},... | collective-permute-start | bytes 1400840 | tf_op jit(solution)/shard_map/ppermute | solution.py:145
  219.1 13.7 %collective-permute-start.49 = (bf16[96,2432]{1,0:T(8,128)(2,1)S(1)}, bf16[96,2432]{1,0:T(8,128)(2,1)S(1)}, u32[]{:S(2)}, u32[]{:S(2)}) collective-permute-start(bf16[96,2432]{1,0:T(8,128)(2,1)S(1)} %get-tuple-element.234), channel_id=1, source_target_pairs={{0,4},{4,8},{8,12},{12,14},{14,10},{10,6},{6,2},{2,0},{1,5},{5,9},... | collective-permute-start | bytes 1400840 | tf_op jit(solution)/shard_map/ppermute | solution.py:139
  220.5 12.2 %collective-permute-start.50 = (bf16[96,2432]{1,0:T(8,128)(2,1)S(1)}, bf16[96,2432]{1,0:T(8,128)(2,1)S(1)}, u32[]{:S(2)}, u32[]{:S(2)}) collective-permute-start(bf16[96,2432]{1,0:T(8,128)(2,1)S(1)} %get-tuple-element.233), channel_id=1, source_target_pairs={{4,0},{8,4},{12,8},{14,12},{10,14},{6,10},{2,6},{0,2},{5,1},{9,5},... | collective-permute-start | bytes 1400840 | tf_op jit(solution)/shard_map/ppermute | solution.py:145
  222.0 11.3 %collective-permute-start.31 = (f32[96,768]{1,0:T(8,128)S(1)}, f32[96,768]{1,0:T(8,128)S(1)}, u32[]{:S(2)}, u32[]{:S(2)}) collective-permute-start(f32[96,768]{1,0:T(8,128)S(1)} %get-tuple-element.159), channel_id=1, source_target_pairs={{0,1},{1,0},{2,3},{3,2},{4,5},{5,4},{6,7},{7,6},{8,9},{9,8},{10,11... | collective-permute-start | bytes 884744 | tf_op jit(solution)/shard_map/ppermute | solution.py:157
  222.0 12.9 %collective-permute-start.38 = (bf16[96,768]{1,0:T(8,128)(2,1)S(1)}, bf16[96,768]{1,0:T(8,128)(2,1)S(1)}, u32[]{:S(2)}, u32[]{:S(2)}) collective-permute-start(bf16[96,768]{1,0:T(8,128)(2,1)S(1)} %add_convert_fusion.11), channel_id=1, source_target_pairs={{0,16},{16,0},{1,17},{17,1},{2,18},{18,2},{3,19},{19,3},{4,20},{20... | collective-permute-start | bytes 442376 | tf_op jit(solution)/shard_map/ppermute | solution.py:157
  223.6 16.1 %collective-permute-start.52 = (bf16[96,2432]{1,0:T(8,128)(2,1)S(1)}, bf16[96,2432]{1,0:T(8,128)(2,1)S(1)}, u32[]{:S(2)}, u32[]{:S(2)}) collective-permute-start(bf16[96,2432]{1,0:T(8,128)(2,1)S(1)} %add_convert_fusion.3), channel_id=1, source_target_pairs={{0,4},{4,8},{8,12},{12,14},{14,10},{10,6},{6,2},{2,0},{1,5},{5,9},... | collective-permute-start | bytes 1400840 | tf_op jit(solution)/shard_map/ppermute | solution.py:139
  232.9 8.6 %collective-permute-start.51 = (bf16[96,2432]{1,0:T(8,128)(2,1)S(1)}, bf16[96,2432]{1,0:T(8,128)(2,1)S(1)}, u32[]{:S(2)}, u32[]{:S(2)}) collective-permute-start(bf16[96,2432]{1,0:T(8,128)(2,1)S(1)} %add_convert_fusion), channel_id=1, source_target_pairs={{4,0},{8,4},{12,8},{14,12},{10,14},{6,10},{2,6},{0,2},{5,1},{9,5},... | collective-permute-start | bytes 1400840 | tf_op jit(solution)/shard_map/ppermute | solution.py:145
  233.3 8.7 %collective-permute-start.32 = (bf16[96,768]{1,0:T(8,128)(2,1)S(1)}, bf16[96,768]{1,0:T(8,128)(2,1)S(1)}, u32[]{:S(2)}, u32[]{:S(2)}) collective-permute-start(bf16[96,768]{1,0:T(8,128)(2,1)S(1)} %add_convert_fusion.15), channel_id=1, source_target_pairs={{0,16},{16,0},{1,17},{17,1},{2,18},{18,2},{3,19},{19,3},{4,20},{20... | collective-permute-start | bytes 442376 | tf_op jit(solution)/shard_map/ppermute | solution.py:157
  241.9 1.8 collective-permute-start.54
  242.2 13.7 %collective-permute-start.53 = (bf16[96,2304]{1,0:T(8,128)(2,1)S(1)}, bf16[96,2304]{1,0:T(8,128)(2,1)S(1)}, u32[]{:S(2)}, u32[]{:S(2)}) collective-permute-start(bf16[96,2304]{1,0:T(8,128)(2,1)S(1)} %slice.91), channel_id=1, source_target_pairs={{0,16},{16,0},{1,17},{17,1},{2,18},{18,2},{3,19},{19,3},{4,20},{20... | collective-permute-start | bytes 1327112 | tf_op jit(solution)/shard_map/ppermute | solution.py:157
  243.8 12.0 %collective-permute-start.55 = (f32[96,128]{1,0:T(8,128)S(1)}, f32[96,128]{1,0:T(8,128)S(1)}, u32[]{:S(2)}, u32[]{:S(2)}) collective-permute-start(f32[96,128]{1,0:T(8,128)S(1)} %get-tuple-element.255), channel_id=1, source_target_pairs={{0,16},{16,0},{1,17},{17,1},{2,18},{18,2},{3,19},{19,3},{4,20},{20... | collective-permute-start | bytes 147464 | tf_op jit(solution)/shard_map/ppermute | solution.py:157
  (8 other events, 10.6 us)

commit v3 on v2

--- a/solution.py
+++ b/solution.py
@@ -258,21 +258,15 @@
     bias_ref,
     mine_ref,
     other_ref,
-    norm1_ref,
-    norm2_ref,
-    xhat_ref,
-    scale_ref,
-    packed_ref,
-    mixed_ref,
-    pre_ref,
-    act_ref,
+    low_ref,
+    high_ref,
     vector_ref,
 ):
-    rows = own_ref.shape[0]
+    rows, model = own_ref.shape
     qkv_width = heads * 3 * HEAD
     start = heads * 4 * HEAD
     wide = cos_ref.shape[1]
-    hidden = pre_ref.shape[1]
+    hidden = high_ref.shape[1] - model - 128
     pieces = (qkv_width + hidden) // depth
     small = jnp.transpose(weight_ref[:, start + 2 * hidden :].astype(F32))
     vectors = small[:8]
@@ -286,15 +280,16 @@
     centred = values - jnp.mean(values, axis=-1, keepdims=True)
     scale = lax.rsqrt(jnp.mean(centred * centred, axis=-1, keepdims=True) + EPSILON)
     xhat = centred * scale
-    xhat_ref[...] = xhat
-    scale_ref[...] = jnp.broadcast_to(scale, scale_ref.shape)
+    high_ref[:, :model] = xhat
+    high_ref[:, model + hidden :] = jnp.broadcast_to(scale, (2 * rows, 128))
     first = (xhat * vectors[0:1] + vectors[1:2]).astype(BF)
     second = (xhat * vectors[2:3] + vectors[3:4]).astype(BF)
-    norm1_ref[...] = first
-    norm2_ref[...] = second
+    low_ref[:, :model] = first
+    low_ref[:, model : 2 * model] = second
     packed = dot(first, weight_ref[:, :wide]) + qkv_bias
     packed = turn(packed, cos_ref[...], upper_ref[...], lower_ref[...]).astype(BF)
-    packed_ref[...] = packed
+    spot = low_ref.shape[1] - wide
+    low_ref[:, spot:] = packed
     bias = bias_ref[...]
     mixed = []
     for index in range(heads):
@@ -302,11 +297,14 @@
         weights = softmax_rows(queries, keys, bias).astype(BF)
         mixed.append(dot(weights, held))
     mixed = jnp.concatenate(mixed, axis=1).astype(BF)
-    mixed_ref[...] = mixed
+    tail = spot - 2 * model - hidden - mixed.shape[1]
+    low_ref[:, 2 * model + hidden : spot] = (
+        jnp.concatenate([mixed, jnp.zeros((2 * rows, tail), BF)], axis=1) if tail else mixed
+    )
     pre = dot(second, weight_ref[:, start : start + hidden]) + fc_bias
-    pre_ref[...] = pre
+    high_ref[:, model : model + hidden] = pre
     act = (pre * (0.5 + 0.5 * lax.erf(pre * math.sqrt(0.5)))).astype(BF)
-    act_ref[...] = act
+    low_ref[:, 2 * model : 2 * model + hidden] = act
     total = dot_last(act, weight_ref[:, start + hidden : start + 2 * hidden])
     total = total + dot_last(mixed, weight_ref[:, qkv_width:start])
     mine_ref[...] = total[:rows]
@@ -322,10 +320,8 @@
     upper_ref,
     lower_ref,
     bias_ref,
-    xhat_ref,
-    scale_ref,
-    packed_ref,
-    pre_ref,
+    low_ref,
+    high_ref,
     vector_ref,
     mine_ref,
     other_ref,
@@ -333,14 +329,14 @@
     d_pre_ref,
     sums_ref,
 ):
-    rows = own_ref.shape[0]
+    rows, model = own_ref.shape
     qkv_width = heads * 3 * HEAD
     start = heads * 4 * HEAD
     wide = cos_ref.shape[1]
-    hidden = pre_ref.shape[1]
+    hidden = high_ref.shape[1] - model - 128
     grad = jnp.concatenate([own_ref[...], far_ref[...]], axis=0)
     d_act = dot(grad, weight_ref[:, start + hidden : start + 2 * hidden])
-    pre = pre_ref[...]
+    pre = high_ref[:, model : model + hidden]
     slope = 0.5 + 0.5 * lax.erf(pre * math.sqrt(0.5))
     slope = slope + pre * (jnp.exp(pre * pre * -0.5) * (1.0 / math.sqrt(2.0 * math.pi)))
     d_pre = (d_act * slope).astype(BF)
@@ -348,7 +344,7 @@
     d_second = dot_last(d_pre, weight_ref[:, start : start + hidden])
     d_mixed = dot(grad, weight_ref[:, qkv_width:start]).astype(BF)
     bias = bias_ref[...]
-    packed = packed_ref[...]
+    packed = low_ref[:, low_ref.shape[1] - wide :]
     parts = []
     for index in range(heads):
         queries, keys, held = head_parts(packed, index)
@@ -367,11 +363,11 @@
     d_packed = turn(d_packed, cos_ref[...], -upper_ref[...], -lower_ref[...]).astype(BF)
     d_packed_ref[...] = d_packed
     d_first = dot_last(d_packed, weight_ref[:, :wide])
-    xhat = xhat_ref[...]
+    xhat = high_ref[:, :model]
     inner = d_first * vector_ref[0:1] + d_second * vector_ref[2:3]
     average = jnp.mean(inner, axis=-1, keepdims=True)
     along = jnp.mean(inner * xhat, axis=-1, keepdims=True)
-    total = (inner - average - xhat * along) * scale_ref[:, 0:1]
+    total = (inner - average - xhat * along) * high_ref[:, model + hidden : model + hidden + 1]
     mine_ref[...] = total[:rows]
     other_ref[...] = total[rows:]
 
@@ -428,7 +424,7 @@
     rest = SMALL - 8 - pieces
     small = jnp.concatenate([sums, stacked, jnp.zeros((rest, tile), F32)], axis=0)
     terms_ref[:, :start] = jnp.concatenate(
-        [dot_first(first, d_packed)[:, :qkv_width], dot_first(grad, mixed)], axis=1
+        [dot_first(first, d_packed)[:, :qkv_width], dot_first(grad, mixed)[:, : heads * HEAD]], axis=1
     ).astype(BF)
     terms_ref[:, start : start + hidden] = dot_first(second, d_pre).astype(BF)
     terms_ref[:, start + hidden : start + 2 * hidden] = dot_first(grad, act).astype(BF)
@@ -487,6 +483,10 @@
     return pl.CostEstimate(flops=int(flops), bytes_accessed=int(moved), transcendentals=0)
 
 
+def mixed_width(heads):
+    return heads * HEAD + -(heads * HEAD) % 128
+
+
 def in_vmem():
     return pl.BlockSpec(memory_space=pltpu.VMEM)
 
@@ -499,8 +499,7 @@
     return pl.pallas_call(
         pack_kernel,
         out_shape=(packet, packet, whole, whole),
-        out_specs=(in_vmem(), in_vmem())
-        + (pl.BlockSpec(memory_space=pl.ANY), pl.BlockSpec(memory_space=pl.ANY)),
+        out_specs=(in_vmem(),) * 4,
         in_specs=[pl.BlockSpec(memory_space=pltpu.SMEM)]
         + [pl.BlockSpec(memory_space=pl.ANY)] * len(arrays),
         scratch_shapes=[pltpu.VMEM(item.shape, item.dtype) for item in arrays]
@@ -543,14 +542,8 @@
     outs = (
         shape(rows, model, F32),
         shape(rows, model, F32),
-        shape(full, model, BF),
-        shape(full, model, BF),
-        shape(full, model, F32),
-        shape(full, 128, F32),
-        shape(full, wide, BF),
-        shape(full, heads * HEAD, BF),
-        shape(full, hidden, F32),
-        shape(full, hidden, BF),
+        shape(full, 2 * model + hidden + mixed_width(heads) + wide, BF),
+        shape(full, model + hidden + 128, F32),
         shape(8, model, F32),
     )
     return pl.pallas_call(
@@ -566,12 +559,13 @@
     rows, model = own.shape
     full = 2 * rows
     wide = layout[0].shape[1]
-    norm1, norm2, xhat, scale, packed, mixed, pre, act, vectors = kept
+    low, high, vectors = kept
+    hidden = high.shape[1] - model - 128
     outs = (
         jax.ShapeDtypeStruct((rows, model), F32),
         jax.ShapeDtypeStruct((rows, model), F32),
         jax.ShapeDtypeStruct((full, wide), BF),
-        jax.ShapeDtypeStruct((full, pre.shape[1]), BF),
+        jax.ShapeDtypeStruct((full, hidden), BF),
         jax.ShapeDtypeStruct((8, model), F32),
     )
     return pl.pallas_call(
@@ -580,19 +574,24 @@
         compiler_params=pltpu.CompilerParams(vmem_limit_bytes=VMEM_LIMIT),
         cost_estimate=cost(5e9, 10e6),
         name="backward",
-    )(own, far, weight, *layout, xhat, scale, packed, pre, vectors)
+    )(own, far, weight, *layout, low, high, vectors)
 
 
 def weight_call(grads, kept, backs, heads, depth):
-    model = kept[0][0].shape[1]
-    hidden = kept[0][7].shape[1]
+    model = grads[0][0].shape[1]
+    hidden = kept[0][1].shape[1] - model - 128
     tile = model // 2
+    mixed = mixed_width(heads)
     width = heads * 4 * HEAD + 2 * hidden + SMALL
     operands, specs = [], []
 
-    def tiled(array):
+    def tiled(array, first=0):
         operands.append(array)
-        specs.append(pl.BlockSpec((array.shape[0], tile), lambda i: (0, i)))
+        specs.append(pl.BlockSpec((array.shape[0], tile), lambda i: (0, first + i)))
+
+    def part(array, start, width):
+        operands.append(array)
+        specs.append(pl.BlockSpec((array.shape[0], width), lambda i: (0, start // width)))
 
     def whole(array):
         operands.append(array)
@@ -600,13 +599,13 @@
 
     for (own, far), keep, back in zip(grads, kept, backs):
         tiled(keep[0])
-        tiled(keep[1])
+        tiled(keep[0], 2)
         tiled(own)
         tiled(far)
         whole(back[2])
         whole(back[3])
-        whole(keep[5])
-        whole(keep[7])
+        part(keep[0], 2 * model + hidden, mixed)
+        part(keep[0], 2 * model, hidden)
         tiled(back[4])
     for back in backs:
         whole(back[4])
@@ -697,16 +696,17 @@
     came_part = swap(sent_part, "pipe")
     chunk = jnp.where(leading, kept_part, came_part)
     gather = RingGather(chunk, first_whole, ahead_steps)
-    gather.advance()
     later = RingGather(
         jnp.where(leading, came_part, kept_part), second_whole, count - 1 - ahead_steps
     )
-    order = []
-    for _ in range(gather.steps - 1):
-        order = gather.advance(*order)
-        if later.step < later.steps - 1:
+    gather.advance()
+    order = later.advance()
+    while gather.step < gather.steps or later.step < later.steps:
+        if gather.step < gather.steps:
+            order = gather.advance(*order)
+        if later.step < later.steps:
             order = later.advance(*order)
-    weights = [gather.result(), None]
+    weights = [gather.result(), later.result()]
 
     lengths = after(lengths, chunk)
     inputs, cotangent = after(inputs, sent_part), after(cotangent, chunk)
@@ -728,9 +728,6 @@
             own, far = current[m]
             found = forward_call(own, far, weights[section], layouts[m], heads, hidden, depth)
             kept_rows.append(found[2:])
-            if section == 0 and m + 1 == micro:
-                later.advance(found[-1])
-                weights[1] = later.result()
             half = half_sum(found[0], found[1])
             base = own.astype(F32) + found[-1][4:5]
             results.append(complete(half, base))
@@ -755,6 +752,8 @@
     backs, results, marks = [], [], ()
     for m in range(micro):
         own, far = grads[m]
+        if marks:
+            own = after(own, marks[-1])
         found = backward_call(own, far, weights[0], layouts[m], stored[0][m], heads)
         backs.append(found)
         results.append(complete(half_sum(found[0], found[1]), own.astype(F32)))

time: 258 us -> 236 us (0.915)
  waiting for transfers between devices: 139 us -> 108 us
  starting transfers between devices: 46.6 us -> 52.5 us
    ppermute x7, waiting for transfers between devices: 27.3 us -> 4.06 us  [advance(): self.back = lax.ppermute(back, 'dp', self.behind)]
    ppermute x7, starting transfers between devices: 3.01 us -> 12.2 us  [advance(): back = lax.ppermute(own, 'dp', self.behind)]
    ppermute x7, waiting for transfers between devices: 41.8 us -> 33.5 us  [advance(): front = lax.ppermute(own, 'dp', self.ahead)]
    ppermute x7, starting transfers between devices: 10.3 us -> 3.21 us  [advance(): front = lax.ppermute(own, 'dp', self.ahead)]
    dynamic_update_slice x14, local copies, waits for them, and re-layouts: 11.1 us -> 14 us  [put(): lax.dynamic_update_slice(self.whole, block, (owner * self.depth, 0))]
    ppermute x7, starting transfers between devices: 3.28 us -> 5.88 us  [advance(): self.back = lax.ppermute(back, 'dp', self.behind)]
  transfers between devices with their start and end apart: 56 -> 56, of which waited for: 28 -> 27; matrix products, arithmetic and copies ran while one was open for 11% -> 13% of each run, Pallas kernels for 11% -> 13%
where the time goes in v3:
time: 236 us; the launch traced here: 235 us
  waiting for transfers between devices  108 us (46%)
  starting transfers between devices  52.5 us (22%)
  Pallas kernels  32.6 us (14%)
  local copies, waits for them, and re-layouts  32.5 us (14%)
  other arithmetic  8.35 us (4%)
    ppermute x7, waiting for transfers between devices, advance(): front = lax.ppermute(own, 'dp', self.ahead)  33.5 us
    ppermute x28, waiting for transfers between devices, swap(): return lax.ppermute(block, axis, [(0, 1), (1, 0)])  32.4 us
    ppermute x7, waiting for transfers between devices, advance(): self.front = lax.ppermute(front, 'dp', self.ahead)  31.3 us
    ppermute x28, starting transfers between devices, swap(): return lax.ppermute(block, axis, [(0, 1), (1, 0)])  21.2 us
    pallas_call x4, Pallas kernels, backward_call(): pl.pallas_call(functools.partial(backward_kernel, heads), out_shape=outs,...  15 us
    dynamic_update_slice x14, local copies, waits for them, and re-layouts, put(): lax.dynamic_update_slice(self.whole, block, (owner * self.depth, 0))  14 us
    ppermute x7, starting transfers between devices, advance(): back = lax.ppermute(own, 'dp', self.behind)  12.2 us
    ppermute x7, starting transfers between devices, advance(): self.front = lax.ppermute(front, 'dp', self.ahead)  10 us
  transfers between devices with their start and end apart: 56, of which 27 were waited for; matrix products, arithmetic and copies ran while one was open for 13% of the time, Pallas kernels for 13%

profile of v3, /device:TPU:0, one launch (start us, length us, event | category | flops | bytes accessed | tf_op | source)
XLA Modules:
  0.0 235.4 jit_solution(250535526939944917)
XLA Ops:
  6.8 1.8 copy-done.4
  8.6 1.8 copy-done.7
  10.4 3.0 %collective-permute-start.1 = (bf16[96,2432]{1,0:T(8,128)(2,1)S(1)}, bf16[96,2432]{1,0:T(8,128)(2,1)S(1)}, u32[]{:S(2)}, u32[]{:S(2)}) collective-permute-start(bf16[96,2432]{1,0:T(8,128)(2,1)S(1)} %get-tuple-element.96), channel_id=1, source_target_pairs={{0,16},{16,0},{1,17},{17,1},{2,18},{18,2},{3,19},{19,3},{4,20},{20... | collective-permute-start | bytes 1400840 | tf_op jit(solution)/shard_map/ppermute | solution.py:157
  14.8 9.3 %collective-permute-done.1 = bf16[96,2432]{1,0:T(8,128)(2,1)S(1)} collective-permute-done((bf16[96,2432]{1,0:T(8,128)(2,1)S(1)}, bf16[96,2432]{1,0:T(8,128)(2,1)S(1)}, u32[]{:S(2)}, u32[]{:S(2)}) %collective-permute-start.1) | collective-permute-done | bytes 466976 | tf_op jit(solution)/shard_map/ppermute | solution.py:157
  24.1 1.4 constant_dynamic-update-slice_fusion.7
  25.6 1.8 collective-permute-start.2
  27.6 1.8 collective-permute-start.6
  30.2 1.4 multiply_sine_fusion.1
  35.7 2.1 concatenate.82.lower_ref
  39.5 1.8 collective-permute-done.3
  41.3 1.6 collective-permute-start.4
  43.3 6.2 %collective-permute-done.6 = bf16[96,2432]{1,0:T(8,128)(2,1)} collective-permute-done((bf16[96,2432]{1,0:T(8,128)(2,1)}, bf16[96,2432]{1,0:T(8,128)(2,1)}, u32[]{:S(2)}, u32[]{:S(2)}) %collective-permute-start.6) | collective-permute-done | bytes 466976 | tf_op jit(solution)/shard_map/ppermute | solution.py:100
  49.5 1.8 collective-permute-done.7
  51.3 1.6 collective-permute-start.10
  53.3 1.9 constant_dynamic-update-slice_fusion.14
  55.2 1.8 constant_dynamic-update-slice_fusion.6
  57.0 1.8 constant_dynamic-update-slice_fusion.13
  58.8 1.8 constant_dynamic-update-slice_fusion.5
  61.2 1.6 collective-permute-start.8
  62.8 6.7 %collective-permute-done.10 = bf16[96,2432]{1,0:T(8,128)(2,1)S(1)} collective-permute-done((bf16[96,2432]{1,0:T(8,128)(2,1)}, bf16[96,2432]{1,0:T(8,128)(2,1)S(1)}, u32[]{:S(2)}, u32[]{:S(2)}) %collective-permute-start.10) | collective-permute-done | bytes 466976 | tf_op jit(solution)/shard_map/ppermute | solution.py:100
  69.4 1.7 collective-permute-start.9
  74.7 4.7 %collective-permute-done.8 = bf16[96,2432]{1,0:T(8,128)(2,1)S(1)} collective-permute-done((bf16[96,2432]{1,0:T(8,128)(2,1)S(1)}, bf16[96,2432]{1,0:T(8,128)(2,1)S(1)}, u32[]{:S(2)}, u32[]{:S(2)}) %collective-permute-start.8) | collective-permute-done | bytes 466976 | tf_op jit(solution)/shard_map/ppermute | solution.py:100
  79.4 1.7 collective-permute-start.20
  81.9 5.7 %collective-permute-done.19 = bf16[96,2432]{1,0:T(8,128)(2,1)S(1)} collective-permute-done((bf16[96,2432]{1,0:T(8,128)(2,1)S(1)}, bf16[96,2432]{1,0:T(8,128)(2,1)S(1)}, u32[]{:S(2)}, u32[]{:S(2)}) %collective-permute-start.19) | collective-permute-done | bytes 466976 | tf_op jit(solution)/shard_map/ppermute | solution.py:100
  87.7 1.4 collective-permute-start.12
  91.3 7.4 %collective-permute-done.12 = bf16[96,2432]{1,0:T(8,128)(2,1)S(1)} collective-permute-done((bf16[96,2432]{1,0:T(8,128)(2,1)S(1)}, bf16[96,2432]{1,0:T(8,128)(2,1)S(1)}, u32[]{:S(2)}, u32[]{:S(2)}) %collective-permute-start.12) | collective-permute-done | bytes 466976 | tf_op jit(solution)/shard_map/ppermute | solution.py:100
  100.6 2.1 copy-done.5
  102.6 2.2 forward.4
  105.0 2.3 forward.5
  107.9 1.6 collective-permute-start.14
  110.7 3.9 %collective-permute-done.14 = bf16[96,768]{1,0:T(8,128)(2,1)S(1)} collective-permute-done((bf16[96,768]{1,0:T(8,128)(2,1)S(1)}, bf16[96,768]{1,0:T(8,128)(2,1)S(1)}, u32[]{:S(2)}, u32[]{:S(2)}) %collective-permute-start.14) | collective-permute-done | bytes 147488 | tf_op jit(solution)/shard_map/ppermute | solution.py:157
  114.7 2.2 collective-permute-done.17
  118.5 2.3 forward.7
  120.9 2.2 forward.6
  123.7 3.7 %backward.4 = (f32[96,768]{1,0:T(8,128)S(1)}, f32[96,768]{1,0:T(8,128)S(1)}, bf16[192,640]{1,0:T(8,128)(2,1)S(1)}, bf16[192,768]{1,0:T(8,128)(2,1)S(1)}, f32[8,768]{1,0:T(8,128)S(1)}) custom-call(bf16[96,768]{1,0:T(8,128)(2,1)S(1)} %get-tuple-element.203.own_ref.refs_2_, bf16[96,768]{1,0:T(8,128)(2,1)S(1)} %collective-permute-done.27.far_ref.refs_3_, ...), custom_call_target="tpu_custom_call" | custom-call | flops 5000000000 | bytes 10000000 | tf_op jit(solution)/shard_map/backward/pallas_call | solution.py:571
  127.6 4.0 %backward.6 = (f32[96,768]{1,0:T(8,128)S(1)}, f32[96,768]{1,0:T(8,128)S(1)}, bf16[192,640]{1,0:T(8,128)(2,1)S(1)}, bf16[192,768]{1,0:T(8,128)(2,1)S(1)}, f32[8,768]{1,0:T(8,128)S(1)}) custom-call(bf16[96,768]{1,0:T(8,128)(2,1)S(1)} %get-tuple-element.204.own_ref.refs_11_, bf16[96,768]{1,0:T(8,128)(2,1)S(1)} %collective-permute-done.33.far_ref.refs_12_, ...), custom_call_target="tpu_custom_call" | custom-call | flops 5000000000 | bytes 10000000 | tf_op jit(solution)/shard_map/backward/pallas_call | solution.py:571
  132.0 1.6 collective-permute-start.26
  134.3 1.6 collective-permute-start.29
  136.4 3.1 %weights.2 = bf16[768,2432]{1,0:T(8,128)(2,1)S(1)} custom-call(bf16[192,3200]{1,0:T(8,128)(2,1)S(1)} %get-tuple-element.125.low_ref.refs_0_.refs_1_.refs_6_.refs_7_, bf16[192,3200]{1,0:T(8,128)(2,1)S(1)} %get-tuple-element.125.low_ref.refs_0_.refs_1_.refs_6_.refs_7_, bf16[96,768]{1,0:T(8,128)(2,1)S(1)} %get-tuple-element.203.own_ref.refs_2_, ...), custom_call_target="tpu_custom_call" | custom-call | flops 8000000000 | bytes 10000000 | tf_op jit(solution)/shard_map/weights/pallas_call | solution.py:612
  140.6 4.5 %collective-permute-done.29 = bf16[96,768]{1,0:T(8,128)(2,1)S(1)} collective-permute-done((bf16[96,768]{1,0:T(8,128)(2,1)S(1)}, bf16[96,768]{1,0:T(8,128)(2,1)S(1)}, u32[]{:S(2)}, u32[]{:S(2)}) %collective-permute-start.29) | collective-permute-done | bytes 147488 | tf_op jit(solution)/shard_map/ppermute | solution.py:157
  145.1 1.5 collective-permute-start.37
  149.0 3.7 %backward.5 = (f32[96,768]{1,0:T(8,128)S(1)}, f32[96,768]{1,0:T(8,128)S(1)}, bf16[192,640]{1,0:T(8,128)(2,1)S(1)}, bf16[192,768]{1,0:T(8,128)(2,1)S(1)}, f32[8,768]{1,0:T(8,128)S(1)}) custom-call(bf16[96,768]{1,0:T(8,128)(2,1)S(1)} %get-tuple-element.201.own_ref.refs_2_, bf16[96,768]{1,0:T(8,128)(2,1)S(1)} %collective-permute-done.30.far_ref.refs_3_, ...), custom_call_target="tpu_custom_call" | custom-call | flops 5000000000 | bytes 10000000 | tf_op jit(solution)/shard_map/backward/pallas_call | solution.py:571
  152.9 3.3 %collective-permute-done.37 = bf16[96,2432]{1,0:T(8,128)(2,1)S(1)} collective-permute-done((bf16[96,2432]{1,0:T(8,128)(2,1)S(1)}, bf16[96,2432]{1,0:T(8,128)(2,1)S(1)}, u32[]{:S(2)}, u32[]{:S(2)}) %collective-permute-start.37) | collective-permute-done | bytes 466976 | tf_op jit(solution)/shard_map/ppermute | solution.py:145
  156.5 1.6 collective-permute-start.44
  158.6 3.7 %backward.7 = (f32[96,768]{1,0:T(8,128)S(1)}, f32[96,768]{1,0:T(8,128)S(1)}, bf16[192,640]{1,0:T(8,128)(2,1)S(1)}, bf16[192,768]{1,0:T(8,128)(2,1)S(1)}, f32[8,768]{1,0:T(8,128)S(1)}) custom-call(bf16[96,768]{1,0:T(8,128)(2,1)S(1)} %get-tuple-element.146.own_ref.refs_11_, bf16[96,768]{1,0:T(8,128)(2,1)S(1)} %collective-permute-done.38.far_ref.refs_12_, ...), custom_call_target="tpu_custom_call" | custom-call | flops 5000000000 | bytes 10000000 | tf_op jit(solution)/shard_map/backward/pallas_call | solution.py:571
  162.3 3.1 %weights.3 = bf16[768,2432]{1,0:T(8,128)(2,1)S(1)} custom-call(bf16[192,3200]{1,0:T(8,128)(2,1)S(1)} %get-tuple-element.129.low_ref.refs_0_.refs_1_.refs_6_.refs_7_, bf16[192,3200]{1,0:T(8,128)(2,1)S(1)} %get-tuple-element.129.low_ref.refs_0_.refs_1_.refs_6_.refs_7_, bf16[96,768]{1,0:T(8,128)(2,1)S(1)} %get-tuple-element.201.own_ref.refs_2_, ...), custom_call_target="tpu_custom_call" | custom-call | flops 8000000000 | bytes 10000000 | tf_op jit(solution)/shard_map/weights/pallas_call | solution.py:612
  166.5 4.2 %collective-permute-done.43 = bf16[96,2432]{1,0:T(8,128)(2,1)S(1)} collective-permute-done((bf16[96,2432]{1,0:T(8,128)(2,1)S(1)}, bf16[96,2432]{1,0:T(8,128)(2,1)S(1)}, u32[]{:S(2)}, u32[]{:S(2)}) %collective-permute-start.43) | collective-permute-done | bytes 466976 | tf_op jit(solution)/shard_map/ppermute | solution.py:139
  170.7 1.7 collective-permute-start.42
  173.0 7.7 %collective-permute-done.41 = bf16[96,2432]{1,0:T(8,128)(2,1)S(1)} collective-permute-done((bf16[96,2432]{1,0:T(8,128)(2,1)S(1)}, bf16[96,2432]{1,0:T(8,128)(2,1)S(1)}, u32[]{:S(2)}, u32[]{:S(2)}) %collective-permute-start.41) | collective-permute-done | bytes 466976 | tf_op jit(solution)/shard_map/ppermute | solution.py:139
  180.7 1.7 collective-permute-start.48
  183.1 7.6 %collective-permute-done.47 = bf16[96,2432]{1,0:T(8,128)(2,1)S(1)} collective-permute-done((bf16[96,2432]{1,0:T(8,128)(2,1)S(1)}, bf16[96,2432]{1,0:T(8,128)(2,1)S(1)}, u32[]{:S(2)}, u32[]{:S(2)}) %collective-permute-start.47) | collective-permute-done | bytes 466976 | tf_op jit(solution)/shard_map/ppermute | solution.py:139
  190.7 1.7 collective-permute-start.46
  192.5 5.5 %collective-permute-done.45 = bf16[96,2432]{1,0:T(8,128)(2,1)S(1)} collective-permute-done((bf16[96,2432]{1,0:T(8,128)(2,1)S(1)}, bf16[96,2432]{1,0:T(8,128)(2,1)S(1)}, u32[]{:S(2)}, u32[]{:S(2)}) %collective-permute-start.45) | collective-permute-done | bytes 466976 | tf_op jit(solution)/shard_map/ppermute | solution.py:139
  198.0 1.5 collective-permute-done.46
  199.9 2.3 collective-permute-start.50
  203.1 1.7 collective-permute-start.32
  204.8 4.7 %collective-permute-done.49 = bf16[96,2432]{1,0:T(8,128)(2,1)S(1)} collective-permute-done((bf16[96,2432]{1,0:T(8,128)(2,1)S(1)}, bf16[96,2432]{1,0:T(8,128)(2,1)S(1)}, u32[]{:S(2)}, u32[]{:S(2)}) %collective-permute-start.49) | collective-permute-done | bytes 466976 | tf_op jit(solution)/shard_map/ppermute | solution.py:139
  210.7 1.6 collective-permute-start.51
  212.5 2.4 %collective-permute-start.40 = (bf16[96,768]{1,0:T(8,128)(2,1)S(1)}, bf16[96,768]{1,0:T(8,128)(2,1)S(1)}, u32[]{:S(2)}, u32[]{:S(2)}) collective-permute-start(bf16[96,768]{1,0:T(8,128)(2,1)S(1)} %add_convert_fusion.11), channel_id=1, source_target_pairs={{0,16},{16,0},{1,17},{17,1},{2,18},{18,2},{3,19},{19,3},{4,20},{20... | collective-permute-start | bytes 442376 | tf_op jit(solution)/shard_map/ppermute | solution.py:157
  214.9 3.8 %collective-permute-done.52 = bf16[96,2432]{1,0:T(8,128)(2,1)S(1)} collective-permute-done((bf16[96,2432]{1,0:T(8,128)(2,1)S(1)}, bf16[96,2432]{1,0:T(8,128)(2,1)S(1)}, u32[]{:S(2)}, u32[]{:S(2)}) %collective-permute-start.52) | collective-permute-done | bytes 466976 | tf_op jit(solution)/shard_map/ppermute | solution.py:139
  220.0 1.9 collective-permute-start.53
  222.0 1.1 collective-permute-start.55
  223.9 9.9 %collective-permute-done.55.came_small_ref = f32[96,128]{1,0:T(8,128)S(1)} collective-permute-done((f32[96,128]{1,0:T(8,128)S(1)}, f32[96,128]{1,0:T(8,128)S(1)}, u32[]{:S(2)}, u32[]{:S(2)}) %collective-permute-start.55) | collective-permute-done | bytes 49184 | tf_op jit(solution)/shard_map/ppermute | solution.py:157
  233.8 1.5 unpack.1
  (173 shorter events, 41.2 us)
Async XLA Ops:
  0.6 29.0 %copy-start.15 = (s32[2,1,3]{2,1,0:T(1,128)S(1)}, s32[2,1,3]{2,1,0:T(1,128)}, u32[]{:S(2)}) copy-start(s32[2,1,3]{2,1,0:T(1,128)} %param.15) | copy-start | bytes 76
  10.4 13.7 %collective-permute-start.1 = (bf16[96,2432]{1,0:T(8,128)(2,1)S(1)}, bf16[96,2432]{1,0:T(8,128)(2,1)S(1)}, u32[]{:S(2)}, u32[]{:S(2)}) collective-permute-start(bf16[96,2432]{1,0:T(8,128)(2,1)S(1)} %get-tuple-element.96), channel_id=1, source_target_pairs={{0,16},{16,0},{1,17},{17,1},{2,18},{18,2},{3,19},{19,3},{4,20},{20... | collective-permute-start | bytes 1400840 | tf_op jit(solution)/shard_map/ppermute | solution.py:157
  14.4 86.1 %collective-permute-start = (bf16[96,768]{1,0:T(8,128)(2,1)S(1)}, bf16[96,768]{1,0:T(8,128)(2,1)S(1)}, u32[]{:S(2)}, u32[]{:S(2)}) collective-permute-start(bf16[96,768]{1,0:T(8,128)(2,1)S(1)} %get-tuple-element.207.own_ref), channel_id=1, source_target_pairs={{0,1},{1,0},{2,3},{3,2},{4,5},{5,4},{6,7},{7,6},{8,9},{9,8},{10,11... | collective-permute-start | bytes 442376 | tf_op jit(solution)/shard_map/ppermute | solution.py:157
  25.6 13.9 %collective-permute-start.2 = (bf16[96,2432]{1,0:T(8,128)(2,1)}, bf16[96,2432]{1,0:T(8,128)(2,1)}, u32[]{:S(2)}, u32[]{:S(2)}) collective-permute-start(bf16[96,2432]{1,0:T(8,128)(2,1)} %get-tuple-element.200), channel_id=1, source_target_pairs={{0,4},{4,8},{8,12},{12,14},{14,10},{10,6},{6,2},{2,0},{1,5},{5,9},... | collective-permute-start | bytes 1400840 | tf_op jit(solution)/shard_map/ppermute | solution.py:100
  27.3 13.9 %collective-permute-start.3 = (bf16[96,2432]{1,0:T(8,128)(2,1)}, bf16[96,2432]{1,0:T(8,128)(2,1)}, u32[]{:S(2)}, u32[]{:S(2)}) collective-permute-start(bf16[96,2432]{1,0:T(8,128)(2,1)} %get-tuple-element.200), channel_id=1, source_target_pairs={{4,0},{8,4},{12,8},{14,12},{10,14},{6,10},{2,6},{0,2},{5,1},{9,5},... | collective-permute-start | bytes 1400840 | tf_op jit(solution)/shard_map/ppermute | solution.py:103
  27.6 21.9 %collective-permute-start.6 = (bf16[96,2432]{1,0:T(8,128)(2,1)}, bf16[96,2432]{1,0:T(8,128)(2,1)}, u32[]{:S(2)}, u32[]{:S(2)}) collective-permute-start(bf16[96,2432]{1,0:T(8,128)(2,1)} %get-tuple-element.182), channel_id=1, source_target_pairs={{0,4},{4,8},{8,12},{12,14},{14,10},{10,6},{6,2},{2,0},{1,5},{5,9},... | collective-permute-start | bytes 1400840 | tf_op jit(solution)/shard_map/ppermute | solution.py:100
  29.4 21.9 %collective-permute-start.7 = (bf16[96,2432]{1,0:T(8,128)(2,1)}, bf16[96,2432]{1,0:T(8,128)(2,1)}, u32[]{:S(2)}, u32[]{:S(2)}) collective-permute-start(bf16[96,2432]{1,0:T(8,128)(2,1)} %get-tuple-element.182), channel_id=1, source_target_pairs={{4,0},{8,4},{12,8},{14,12},{10,14},{6,10},{2,6},{0,2},{5,1},{9,5},... | collective-permute-start | bytes 1400840 | tf_op jit(solution)/shard_map/ppermute | solution.py:103
  31.6 3.3 %copy-start.9 = (f32[192,48]{1,0:T(8,128)}, f32[192,48]{1,0:T(8,128)S(1)}, u32[]{:S(2)}) copy-start(f32[192,48]{1,0:T(8,128)S(1)} %broadcast.139) | copy-start | bytes 110596
  31.6 3.2 %copy-start.10 = (f32[192,64]{1,0:T(8,128)}, f32[192,64]{1,0:T(8,128)S(1)}, u32[]{:S(2)}) copy-start(f32[192,64]{1,0:T(8,128)S(1)} %broadcast.140) | copy-start | bytes 147460
  41.3 19.4 %collective-permute-start.4 = (bf16[96,2432]{1,0:T(8,128)(2,1)}, bf16[96,2432]{1,0:T(8,128)(2,1)S(1)}, u32[]{:S(2)}, u32[]{:S(2)}) collective-permute-start(bf16[96,2432]{1,0:T(8,128)(2,1)} %collective-permute-done.2), channel_id=1, source_target_pairs={{0,4},{4,8},{8,12},{12,14},{14,10},{10,6},{6,2},{2,0},{1,5},{5,9},... | collective-permute-start | bytes 1400840 | tf_op jit(solution)/shard_map/ppermute | solution.py:100
  42.8 18.3 %collective-permute-start.5 = (bf16[96,2432]{1,0:T(8,128)(2,1)}, bf16[96,2432]{1,0:T(8,128)(2,1)S(1)}, u32[]{:S(2)}, u32[]{:S(2)}) collective-permute-start(bf16[96,2432]{1,0:T(8,128)(2,1)} %collective-permute-done.3), channel_id=1, source_target_pairs={{4,0},{8,4},{12,8},{14,12},{10,14},{6,10},{2,6},{0,2},{5,1},{9,5},... | collective-permute-start | bytes 1400840 | tf_op jit(solution)/shard_map/ppermute | solution.py:103
  51.3 18.1 %collective-permute-start.10 = (bf16[96,2432]{1,0:T(8,128)(2,1)}, bf16[96,2432]{1,0:T(8,128)(2,1)S(1)}, u32[]{:S(2)}, u32[]{:S(2)}) collective-permute-start(bf16[96,2432]{1,0:T(8,128)(2,1)} %collective-permute-done.6), channel_id=1, source_target_pairs={{0,4},{4,8},{8,12},{12,14},{14,10},{10,6},{6,2},{2,0},{1,5},{5,9},... | collective-permute-start | bytes 1400840 | tf_op jit(solution)/shard_map/ppermute | solution.py:100
  52.9 18.3 %collective-permute-start.11 = (bf16[96,2432]{1,0:T(8,128)(2,1)}, bf16[96,2432]{1,0:T(8,128)(2,1)S(1)}, u32[]{:S(2)}, u32[]{:S(2)}) collective-permute-start(bf16[96,2432]{1,0:T(8,128)(2,1)} %collective-permute-done.7), channel_id=1, source_target_pairs={{4,0},{8,4},{12,8},{14,12},{10,14},{6,10},{2,6},{0,2},{5,1},{9,5},... | collective-permute-start | bytes 1400840 | tf_op jit(solution)/shard_map/ppermute | solution.py:103
  60.7 44.3 %collective-permute-start.15 = (bf16[96,768]{1,0:T(8,128)(2,1)S(1)}, bf16[96,768]{1,0:T(8,128)(2,1)S(1)}, u32[]{:S(2)}, u32[]{:S(2)}) collective-permute-start(bf16[96,768]{1,0:T(8,128)(2,1)S(1)} %get-tuple-element.208.own_ref), channel_id=1, source_target_pairs={{0,1},{1,0},{2,3},{3,2},{4,5},{5,4},{6,7},{7,6},{8,9},{9,8},{10,11... | collective-permute-start | bytes 442376 | tf_op jit(solution)/shard_map/ppermute | solution.py:157
  61.2 18.2 %collective-permute-start.8 = (bf16[96,2432]{1,0:T(8,128)(2,1)S(1)}, bf16[96,2432]{1,0:T(8,128)(2,1)S(1)}, u32[]{:S(2)}, u32[]{:S(2)}) collective-permute-start(bf16[96,2432]{1,0:T(8,128)(2,1)S(1)} %collective-permute-done.4), channel_id=1, source_target_pairs={{0,4},{4,8},{8,12},{12,14},{14,10},{10,6},{6,2},{2,0},{1,5},{5,9},... | collective-permute-start | bytes 1400840 | tf_op jit(solution)/shard_map/ppermute | solution.py:100
  69.4 20.5 %collective-permute-start.9 = (bf16[96,2432]{1,0:T(8,128)(2,1)S(1)}, bf16[96,2432]{1,0:T(8,128)(2,1)S(1)}, u32[]{:S(2)}, u32[]{:S(2)}) collective-permute-start(bf16[96,2432]{1,0:T(8,128)(2,1)S(1)} %collective-permute-done.5), channel_id=1, source_target_pairs={{4,0},{8,4},{12,8},{14,12},{10,14},{6,10},{2,6},{0,2},{5,1},{9,5},... | collective-permute-start | bytes 1400840 | tf_op jit(solution)/shard_map/ppermute | solution.py:103
  71.1 16.6 %collective-permute-start.19 = (bf16[96,2432]{1,0:T(8,128)(2,1)S(1)}, bf16[96,2432]{1,0:T(8,128)(2,1)S(1)}, u32[]{:S(2)}, u32[]{:S(2)}) collective-permute-start(bf16[96,2432]{1,0:T(8,128)(2,1)S(1)} %collective-permute-done.10), channel_id=1, source_target_pairs={{0,4},{4,8},{8,12},{12,14},{14,10},{10,6},{6,2},{2,0},{1,5},{5,9},... | collective-permute-start | bytes 1400840 | tf_op jit(solution)/shard_map/ppermute | solution.py:100
  79.4 10.5 %collective-permute-start.20 = (bf16[96,2432]{1,0:T(8,128)(2,1)S(1)}, bf16[96,2432]{1,0:T(8,128)(2,1)S(1)}, u32[]{:S(2)}, u32[]{:S(2)}) collective-permute-start(bf16[96,2432]{1,0:T(8,128)(2,1)S(1)} %collective-permute-done.11), channel_id=1, source_target_pairs={{4,0},{8,4},{12,8},{14,12},{10,14},{6,10},{2,6},{0,2},{5,1},{9,5},... | collective-permute-start | bytes 1400840 | tf_op jit(solution)/shard_map/ppermute | solution.py:103
  87.7 11.0 %collective-permute-start.12 = (bf16[96,2432]{1,0:T(8,128)(2,1)S(1)}, bf16[96,2432]{1,0:T(8,128)(2,1)S(1)}, u32[]{:S(2)}, u32[]{:S(2)}) collective-permute-start(bf16[96,2432]{1,0:T(8,128)(2,1)S(1)} %collective-permute-done.8), channel_id=1, source_target_pairs={{0,4},{4,8},{8,12},{12,14},{14,10},{10,6},{6,2},{2,0},{1,5},{5,9},... | collective-permute-start | bytes 1400840 | tf_op jit(solution)/shard_map/ppermute | solution.py:100
  89.9 33.7 %collective-permute-start.27 = (bf16[96,768]{1,0:T(8,128)(2,1)S(1)}, bf16[96,768]{1,0:T(8,128)(2,1)S(1)}, u32[]{:S(2)}, u32[]{:S(2)}) collective-permute-start(bf16[96,768]{1,0:T(8,128)(2,1)S(1)} %get-tuple-element.203.own_ref.refs_2_), channel_id=1, source_target_pairs={{0,1},{1,0},{2,3},{3,2},{4,5},{5,4},{6,7},{7,6},{8,9},{9,8},{10,11... | collective-permute-start | bytes 442376 | tf_op jit(solution)/shard_map/ppermute | solution.py:157
  90.0 37.6 %collective-permute-start.33 = (bf16[96,768]{1,0:T(8,128)(2,1)S(1)}, bf16[96,768]{1,0:T(8,128)(2,1)S(1)}, u32[]{:S(2)}, u32[]{:S(2)}) collective-permute-start(bf16[96,768]{1,0:T(8,128)(2,1)S(1)} %get-tuple-element.204.own_ref.refs_11_), channel_id=1, source_target_pairs={{0,1},{1,0},{2,3},{3,2},{4,5},{5,4},{6,7},{7,6},{8,9},{9,8},{10,11... | collective-permute-start | bytes 442376 | tf_op jit(solution)/shard_map/ppermute | solution.py:157
  98.6 18.5 %collective-permute-start.21 = (bf16[96,2432]{1,0:T(8,128)(2,1)S(1)}, bf16[96,2432]{1,0:T(8,128)(2,1)S(1)}, u32[]{:S(2)}, u32[]{:S(2)}) collective-permute-start(bf16[96,2432]{1,0:T(8,128)(2,1)S(1)} %collective-permute-done.20), channel_id=1, source_target_pairs={{4,0},{8,4},{12,8},{14,12},{10,14},{6,10},{2,6},{0,2},{5,1},{9,5},... | collective-permute-start | bytes 1400840 | tf_op jit(solution)/shard_map/ppermute | solution.py:103
  100.6 2.1 copy-start.5
  102.6 2.3 copy-start.6
  104.9 3.0 %collective-permute-start.13 = (f32[96,768]{1,0:T(8,128)S(1)}, f32[96,768]{1,0:T(8,128)S(1)}, u32[]{:S(2)}, u32[]{:S(2)}) collective-permute-start(f32[96,768]{1,0:T(8,128)S(1)} %get-tuple-element.112), channel_id=1, source_target_pairs={{0,1},{1,0},{2,3},{3,2},{4,5},{5,4},{6,7},{7,6},{8,9},{9,8},{10,11... | collective-permute-start | bytes 884744 | tf_op jit(solution)/shard_map/ppermute | solution.py:157
  105.0 2.8 %copy-start.8 = (bf16[768,2432]{1,0:T(8,128)(2,1)S(1)}, bf16[768,2432]{1,0:T(8,128)(2,1)}, u32[]{:S(2)}) copy-start(bf16[768,2432]{1,0:T(8,128)(2,1)} %constant_dynamic-update-slice_fusion.2) | copy-start | bytes 11206660
  105.0 11.9 %copy-start.13 = (bf16[2,96,768]{2,1,0:T(8,128)(2,1)S(1)}, bf16[2,96,768]{2,1,0:T(8,128)(2,1)}, u32[]{:S(2)}) copy-start(bf16[2,96,768]{2,1,0:T(8,128)(2,1)} %param.14) | copy-start | bytes 884740
  107.3 2.3 collective-permute-start.16
  107.9 6.8 %collective-permute-start.14 = (bf16[96,768]{1,0:T(8,128)(2,1)S(1)}, bf16[96,768]{1,0:T(8,128)(2,1)S(1)}, u32[]{:S(2)}, u32[]{:S(2)}) collective-permute-start(bf16[96,768]{1,0:T(8,128)(2,1)S(1)} %add_convert_fusion.25), channel_id=1, source_target_pairs={{0,16},{16,0},{1,17},{17,1},{2,18},{18,2},{3,19},{19,3},{4,20},{20... | collective-permute-start | bytes 442376 | tf_op jit(solution)/shard_map/ppermute | solution.py:157
  109.6 7.4 %collective-permute-start.17 = (bf16[96,768]{1,0:T(8,128)(2,1)S(1)}, bf16[96,768]{1,0:T(8,128)(2,1)S(1)}, u32[]{:S(2)}, u32[]{:S(2)}) collective-permute-start(bf16[96,768]{1,0:T(8,128)(2,1)S(1)} %add_convert_fusion.23), channel_id=1, source_target_pairs={{0,16},{16,0},{1,17},{17,1},{2,18},{18,2},{3,19},{19,3},{4,20},{20... | collective-permute-start | bytes 442376 | tf_op jit(solution)/shard_map/ppermute | solution.py:157
  117.0 1.4 collective-permute-start.24
  117.2 3.8 %collective-permute-start.18 = (bf16[96,768]{1,0:T(8,128)(2,1)S(1)}, bf16[96,768]{1,0:T(8,128)(2,1)S(1)}, u32[]{:S(2)}, u32[]{:S(2)}) collective-permute-start(bf16[96,768]{1,0:T(8,128)(2,1)S(1)} %get-tuple-element.205.own_ref), channel_id=1, source_target_pairs={{0,1},{1,0},{2,3},{3,2},{4,5},{5,4},{6,7},{7,6},{8,9},{9,8},{10,11... | collective-permute-start | bytes 442376 | tf_op jit(solution)/shard_map/ppermute | solution.py:157
  120.7 11.2 %collective-permute-start.25 = (f32[96,768]{1,0:T(8,128)S(1)}, f32[96,768]{1,0:T(8,128)S(1)}, u32[]{:S(2)}, u32[]{:S(2)}) collective-permute-start(f32[96,768]{1,0:T(8,128)S(1)} %get-tuple-element.123), channel_id=1, source_target_pairs={{0,1},{1,0},{2,3},{3,2},{4,5},{5,4},{6,7},{7,6},{8,9},{9,8},{10,11... | collective-permute-start | bytes 884744 | tf_op jit(solution)/shard_map/ppermute | solution.py:157
  123.2 10.4 %collective-permute-start.22 = (f32[96,768]{1,0:T(8,128)S(1)}, f32[96,768]{1,0:T(8,128)S(1)}, u32[]{:S(2)}, u32[]{:S(2)}) collective-permute-start(f32[96,768]{1,0:T(8,128)S(1)} %get-tuple-element.120), channel_id=1, source_target_pairs={{0,1},{1,0},{2,3},{3,2},{4,5},{5,4},{6,7},{7,6},{8,9},{9,8},{10,11... | collective-permute-start | bytes 884744 | tf_op jit(solution)/shard_map/ppermute | solution.py:157
  127.4 6.9 %collective-permute-start.28 = (f32[96,768]{1,0:T(8,128)S(1)}, f32[96,768]{1,0:T(8,128)S(1)}, u32[]{:S(2)}, u32[]{:S(2)}) collective-permute-start(f32[96,768]{1,0:T(8,128)S(1)} %get-tuple-element.128), channel_id=1, source_target_pairs={{0,1},{1,0},{2,3},{3,2},{4,5},{5,4},{6,7},{7,6},{8,9},{9,8},{10,11... | collective-permute-start | bytes 884744 | tf_op jit(solution)/shard_map/ppermute | solution.py:157
  131.6 4.3 %collective-permute-start.34 = (f32[96,768]{1,0:T(8,128)S(1)}, f32[96,768]{1,0:T(8,128)S(1)}, u32[]{:S(2)}, u32[]{:S(2)}) collective-permute-start(f32[96,768]{1,0:T(8,128)S(1)} %get-tuple-element.136), channel_id=1, source_target_pairs={{0,1},{1,0},{2,3},{3,2},{4,5},{5,4},{6,7},{7,6},{8,9},{9,8},{10,11... | collective-permute-start | bytes 884744 | tf_op jit(solution)/shard_map/ppermute | solution.py:157
  132.0 15.6 %collective-permute-start.26 = (bf16[96,768]{1,0:T(8,128)(2,1)S(1)}, bf16[96,768]{1,0:T(8,128)(2,1)S(1)}, u32[]{:S(2)}, u32[]{:S(2)}) collective-permute-start(bf16[96,768]{1,0:T(8,128)(2,1)S(1)} %add_convert_fusion.19), channel_id=1, source_target_pairs={{0,16},{16,0},{1,17},{17,1},{2,18},{18,2},{3,19},{19,3},{4,20},{20... | collective-permute-start | bytes 442376 | tf_op jit(solution)/shard_map/ppermute | solution.py:157
  133.7 68.5 %collective-permute-start.23 = (bf16[96,768]{1,0:T(8,128)(2,1)S(1)}, bf16[96,768]{1,0:T(8,128)(2,1)S(1)}, u32[]{:S(2)}, u32[]{:S(2)}) collective-permute-start(bf16[96,768]{1,0:T(8,128)(2,1)S(1)} %add_convert_fusion.21), channel_id=1, source_target_pairs={{0,16},{16,0},{1,17},{17,1},{2,18},{18,2},{3,19},{19,3},{4,20},{20... | collective-permute-start | bytes 442376 | tf_op jit(solution)/shard_map/ppermute | solution.py:157
  134.3 10.8 %collective-permute-start.29 = (bf16[96,768]{1,0:T(8,128)(2,1)S(1)}, bf16[96,768]{1,0:T(8,128)(2,1)S(1)}, u32[]{:S(2)}, u32[]{:S(2)}) collective-permute-start(bf16[96,768]{1,0:T(8,128)(2,1)S(1)} %add_convert_fusion.17), channel_id=1, source_target_pairs={{0,16},{16,0},{1,17},{17,1},{2,18},{18,2},{3,19},{19,3},{4,20},{20... | collective-permute-start | bytes 442376 | tf_op jit(solution)/shard_map/ppermute | solution.py:157
  135.9 11.6 %collective-permute-start.35 = (bf16[96,768]{1,0:T(8,128)(2,1)S(1)}, bf16[96,768]{1,0:T(8,128)(2,1)S(1)}, u32[]{:S(2)}, u32[]{:S(2)}) collective-permute-start(bf16[96,768]{1,0:T(8,128)(2,1)S(1)} %add_convert_fusion.13), channel_id=1, source_target_pairs={{0,16},{16,0},{1,17},{17,1},{2,18},{18,2},{3,19},{19,3},{4,20},{20... | collective-permute-start | bytes 442376 | tf_op jit(solution)/shard_map/ppermute | solution.py:157
  136.4 11.0 %copy-start.14 = (bf16[2,96,768]{2,1,0:T(8,128)(2,1)S(1)}, bf16[2,96,768]{2,1,0:T(8,128)(2,1)}, u32[]{:S(2)}) copy-start(bf16[2,96,768]{2,1,0:T(8,128)(2,1)} %param.27) | copy-start | bytes 884740
  139.6 13.3 %collective-permute-start.36 = (bf16[96,2432]{1,0:T(8,128)(2,1)S(1)}, bf16[96,2432]{1,0:T(8,128)(2,1)S(1)}, u32[]{:S(2)}, u32[]{:S(2)}) collective-permute-start(bf16[96,2432]{1,0:T(8,128)(2,1)S(1)} %get-tuple-element.198), channel_id=1, source_target_pairs={{0,4},{4,8},{8,12},{12,14},{14,10},{10,6},{6,2},{2,0},{1,5},{5,9},... | collective-permute-start | bytes 1400840 | tf_op jit(solution)/shard_map/ppermute | solution.py:139
  145.1 11.1 %collective-permute-start.37 = (bf16[96,2432]{1,0:T(8,128)(2,1)S(1)}, bf16[96,2432]{1,0:T(8,128)(2,1)S(1)}, u32[]{:S(2)}, u32[]{:S(2)}) collective-permute-start(bf16[96,2432]{1,0:T(8,128)(2,1)S(1)} %get-tuple-element.197), channel_id=1, source_target_pairs={{4,0},{8,4},{12,8},{14,12},{10,14},{6,10},{2,6},{0,2},{5,1},{9,5},... | collective-permute-start | bytes 1400840 | tf_op jit(solution)/shard_map/ppermute | solution.py:145
  147.6 1.4 collective-permute-start.30
  147.7 10.9 %collective-permute-start.38 = (bf16[96,768]{1,0:T(8,128)(2,1)S(1)}, bf16[96,768]{1,0:T(8,128)(2,1)S(1)}, u32[]{:S(2)}, u32[]{:S(2)}) collective-permute-start(bf16[96,768]{1,0:T(8,128)(2,1)S(1)} %get-tuple-element.146.own_ref.refs_11_), channel_id=1, source_target_pairs={{0,1},{1,0},{2,3},{3,2},{4,5},{5,4},{6,7},{7,6},{8,9},{9,8},{10,11... | collective-permute-start | bytes 442376 | tf_op jit(solution)/shard_map/ppermute | solution.py:157
  152.7 50.3 %collective-permute-start.31 = (f32[96,768]{1,0:T(8,128)S(1)}, f32[96,768]{1,0:T(8,128)S(1)}, u32[]{:S(2)}, u32[]{:S(2)}) collective-permute-start(f32[96,768]{1,0:T(8,128)S(1)} %get-tuple-element.132), channel_id=1, source_target_pairs={{0,1},{1,0},{2,3},{3,2},{4,5},{5,4},{6,7},{7,6},{8,9},{9,8},{10,11... | collective-permute-start | bytes 884744 | tf_op jit(solution)/shard_map/ppermute | solution.py:157
  156.5 15.9 %collective-permute-start.44 = (bf16[96,2432]{1,0:T(8,128)(2,1)S(1)}, bf16[96,2432]{1,0:T(8,128)(2,1)S(1)}, u32[]{:S(2)}, u32[]{:S(2)}) collective-permute-start(bf16[96,2432]{1,0:T(8,128)(2,1)S(1)} %get-tuple-element.196), channel_id=1, source_target_pairs={{4,0},{8,4},{12,8},{14,12},{10,14},{6,10},{2,6},{0,2},{5,1},{9,5},... | collective-permute-start | bytes 1400840 | tf_op jit(solution)/shard_map/ppermute | solution.py:145
  158.1 12.6 %collective-permute-start.43 = (bf16[96,2432]{1,0:T(8,128)(2,1)S(1)}, bf16[96,2432]{1,0:T(8,128)(2,1)S(1)}, u32[]{:S(2)}, u32[]{:S(2)}) collective-permute-start(bf16[96,2432]{1,0:T(8,128)(2,1)S(1)} %get-tuple-element.195), channel_id=1, source_target_pairs={{0,4},{4,8},{8,12},{12,14},{14,10},{10,6},{6,2},{2,0},{1,5},{5,9},... | collective-permute-start | bytes 1400840 | tf_op jit(solution)/shard_map/ppermute | solution.py:139
  165.5 15.2 %collective-permute-start.41 = (bf16[96,2432]{1,0:T(8,128)(2,1)S(1)}, bf16[96,2432]{1,0:T(8,128)(2,1)S(1)}, u32[]{:S(2)}, u32[]{:S(2)}) collective-permute-start(bf16[96,2432]{1,0:T(8,128)(2,1)S(1)} %get-tuple-element.194), channel_id=1, source_target_pairs={{0,4},{4,8},{8,12},{12,14},{14,10},{10,6},{6,2},{2,0},{1,5},{5,9},... | collective-permute-start | bytes 1400840 | tf_op jit(solution)/shard_map/ppermute | solution.py:139
  170.7 11.7 %collective-permute-start.42 = (bf16[96,2432]{1,0:T(8,128)(2,1)S(1)}, bf16[96,2432]{1,0:T(8,128)(2,1)S(1)}, u32[]{:S(2)}, u32[]{:S(2)}) collective-permute-start(bf16[96,2432]{1,0:T(8,128)(2,1)S(1)} %get-tuple-element.193), channel_id=1, source_target_pairs={{4,0},{8,4},{12,8},{14,12},{10,14},{6,10},{2,6},{0,2},{5,1},{9,5},... | collective-permute-start | bytes 1400840 | tf_op jit(solution)/shard_map/ppermute | solution.py:145
  172.7 18.0 %collective-permute-start.47 = (bf16[96,2432]{1,0:T(8,128)(2,1)S(1)}, bf16[96,2432]{1,0:T(8,128)(2,1)S(1)}, u32[]{:S(2)}, u32[]{:S(2)}) collective-permute-start(bf16[96,2432]{1,0:T(8,128)(2,1)S(1)} %get-tuple-element.192), channel_id=1, source_target_pairs={{0,4},{4,8},{8,12},{12,14},{14,10},{10,6},{6,2},{2,0},{1,5},{5,9},... | collective-permute-start | bytes 1400840 | tf_op jit(solution)/shard_map/ppermute | solution.py:139
  180.7 11.7 %collective-permute-start.48 = (bf16[96,2432]{1,0:T(8,128)(2,1)S(1)}, bf16[96,2432]{1,0:T(8,128)(2,1)S(1)}, u32[]{:S(2)}, u32[]{:S(2)}) collective-permute-start(bf16[96,2432]{1,0:T(8,128)(2,1)S(1)} %get-tuple-element.191), channel_id=1, source_target_pairs={{4,0},{8,4},{12,8},{14,12},{10,14},{6,10},{2,6},{0,2},{5,1},{9,5},... | collective-permute-start | bytes 1400840 | tf_op jit(solution)/shard_map/ppermute | solution.py:145
  182.7 15.3 %collective-permute-start.45 = (bf16[96,2432]{1,0:T(8,128)(2,1)S(1)}, bf16[96,2432]{1,0:T(8,128)(2,1)S(1)}, u32[]{:S(2)}, u32[]{:S(2)}) collective-permute-start(bf16[96,2432]{1,0:T(8,128)(2,1)S(1)} %get-tuple-element.190), channel_id=1, source_target_pairs={{0,4},{4,8},{8,12},{12,14},{14,10},{10,6},{6,2},{2,0},{1,5},{5,9},... | collective-permute-start | bytes 1400840 | tf_op jit(solution)/shard_map/ppermute | solution.py:139
  190.7 8.8 %collective-permute-start.46 = (bf16[96,2432]{1,0:T(8,128)(2,1)S(1)}, bf16[96,2432]{1,0:T(8,128)(2,1)S(1)}, u32[]{:S(2)}, u32[]{:S(2)}) collective-permute-start(bf16[96,2432]{1,0:T(8,128)(2,1)S(1)} %get-tuple-element.189), channel_id=1, source_target_pairs={{4,0},{8,4},{12,8},{14,12},{10,14},{6,10},{2,6},{0,2},{5,1},{9,5},... | collective-permute-start | bytes 1400840 | tf_op jit(solution)/shard_map/ppermute | solution.py:145
  199.8 9.7 %collective-permute-start.49 = (bf16[96,2432]{1,0:T(8,128)(2,1)S(1)}, bf16[96,2432]{1,0:T(8,128)(2,1)S(1)}, u32[]{:S(2)}, u32[]{:S(2)}) collective-permute-start(bf16[96,2432]{1,0:T(8,128)(2,1)S(1)} %get-tuple-element.188), channel_id=1, source_target_pairs={{0,4},{4,8},{8,12},{12,14},{14,10},{10,6},{6,2},{2,0},{1,5},{5,9},... | collective-permute-start | bytes 1400840 | tf_op jit(solution)/shard_map/ppermute | solution.py:139
  199.9 10.7 %collective-permute-start.50 = (bf16[96,2432]{1,0:T(8,128)(2,1)S(1)}, bf16[96,2432]{1,0:T(8,128)(2,1)S(1)}, u32[]{:S(2)}, u32[]{:S(2)}) collective-permute-start(bf16[96,2432]{1,0:T(8,128)(2,1)S(1)} %get-tuple-element.187), channel_id=1, source_target_pairs={{4,0},{8,4},{12,8},{14,12},{10,14},{6,10},{2,6},{0,2},{5,1},{9,5},... | collective-permute-start | bytes 1400840 | tf_op jit(solution)/shard_map/ppermute | solution.py:145
  203.0 9.4 %collective-permute-start.39 = (f32[96,768]{1,0:T(8,128)S(1)}, f32[96,768]{1,0:T(8,128)S(1)}, u32[]{:S(2)}, u32[]{:S(2)}) collective-permute-start(f32[96,768]{1,0:T(8,128)S(1)} %get-tuple-element.150), channel_id=1, source_target_pairs={{0,1},{1,0},{2,3},{3,2},{4,5},{5,4},{6,7},{7,6},{8,9},{9,8},{10,11... | collective-permute-start | bytes 884744 | tf_op jit(solution)/shard_map/ppermute | solution.py:157
  203.1 9.3 %collective-permute-start.32 = (bf16[96,768]{1,0:T(8,128)(2,1)S(1)}, bf16[96,768]{1,0:T(8,128)(2,1)S(1)}, u32[]{:S(2)}, u32[]{:S(2)}) collective-permute-start(bf16[96,768]{1,0:T(8,128)(2,1)S(1)} %add_convert_fusion.15), channel_id=1, source_target_pairs={{0,16},{16,0},{1,17},{17,1},{2,18},{18,2},{3,19},{19,3},{4,20},{20... | collective-permute-start | bytes 442376 | tf_op jit(solution)/shard_map/ppermute | solution.py:157
  204.7 13.9 %collective-permute-start.52 = (bf16[96,2432]{1,0:T(8,128)(2,1)S(1)}, bf16[96,2432]{1,0:T(8,128)(2,1)S(1)}, u32[]{:S(2)}, u32[]{:S(2)}) collective-permute-start(bf16[96,2432]{1,0:T(8,128)(2,1)S(1)} %add_convert_fusion.3), channel_id=1, source_target_pairs={{0,4},{4,8},{8,12},{12,14},{14,10},{10,6},{6,2},{2,0},{1,5},{5,9},... | collective-permute-start | bytes 1400840 | tf_op jit(solution)/shard_map/ppermute | solution.py:139
  210.7 8.6 %collective-permute-start.51 = (bf16[96,2432]{1,0:T(8,128)(2,1)S(1)}, bf16[96,2432]{1,0:T(8,128)(2,1)S(1)}, u32[]{:S(2)}, u32[]{:S(2)}) collective-permute-start(bf16[96,2432]{1,0:T(8,128)(2,1)S(1)} %add_convert_fusion), channel_id=1, source_target_pairs={{4,0},{8,4},{12,8},{14,12},{10,14},{6,10},{2,6},{0,2},{5,1},{9,5},... | collective-permute-start | bytes 1400840 | tf_op jit(solution)/shard_map/ppermute | solution.py:145
  212.5 7.4 %collective-permute-start.40 = (bf16[96,768]{1,0:T(8,128)(2,1)S(1)}, bf16[96,768]{1,0:T(8,128)(2,1)S(1)}, u32[]{:S(2)}, u32[]{:S(2)}) collective-permute-start(bf16[96,768]{1,0:T(8,128)(2,1)S(1)} %add_convert_fusion.11), channel_id=1, source_target_pairs={{0,16},{16,0},{1,17},{17,1},{2,18},{18,2},{3,19},{19,3},{4,20},{20... | collective-permute-start | bytes 442376 | tf_op jit(solution)/shard_map/ppermute | solution.py:157
  219.8 2.2 collective-permute-start.54
  220.0 13.8 %collective-permute-start.53 = (bf16[96,2304]{1,0:T(8,128)(2,1)S(1)}, bf16[96,2304]{1,0:T(8,128)(2,1)S(1)}, u32[]{:S(2)}, u32[]{:S(2)}) collective-permute-start(bf16[96,2304]{1,0:T(8,128)(2,1)S(1)} %slice.91), channel_id=1, source_target_pairs={{0,16},{16,0},{1,17},{17,1},{2,18},{18,2},{3,19},{19,3},{4,20},{20... | collective-permute-start | bytes 1327112 | tf_op jit(solution)/shard_map/ppermute | solution.py:157
  222.0 11.8 %collective-permute-start.55 = (f32[96,128]{1,0:T(8,128)S(1)}, f32[96,128]{1,0:T(8,128)S(1)}, u32[]{:S(2)}, u32[]{:S(2)}) collective-permute-start(f32[96,128]{1,0:T(8,128)S(1)} %get-tuple-element.209), channel_id=1, source_target_pairs={{0,16},{16,0},{1,17},{17,1},{2,18},{18,2},{3,19},{19,3},{4,20},{20... | collective-permute-start | bytes 147464 | tf_op jit(solution)/shard_map/ppermute | solution.py:157
  (8 other events, 10.6 us)

commit v4 on v3

--- a/solution.py
+++ b/solution.py
@@ -71,6 +71,20 @@
         return values
     tied = list(lax.optimization_barrier((*present, *earlier))[: len(present)])
     return [None if item is None else tied.pop(0) for item in values]
+
+
+def blank_kernel(like_ref, whole_ref):
+    whole_ref[:16, :] = jnp.zeros((16, whole_ref.shape[1]), whole_ref.dtype)
+
+
+def blank_call(like, count):
+    return pl.pallas_call(
+        blank_kernel,
+        out_shape=jax.ShapeDtypeStruct((count * like.shape[0], like.shape[1]), like.dtype),
+        compiler_params=pltpu.CompilerParams(vmem_limit_bytes=VMEM_LIMIT),
+        cost_estimate=cost(0, 1e5),
+        name="blank",
+    )(like)
 
 
 class RingGather:
@@ -192,7 +206,7 @@
 
 def pack_kernel(pipe_ref, *refs):
     sources, (kept_ref, sent_ref) = refs[:6], refs[6:8]
-    held, marks = refs[10:16], refs[16]
+    held, marks = refs[8:14], refs[14]
     copies = [
         pltpu.make_async_copy(source, target, marks.at[i])
         for i, (source, target) in enumerate(zip(sources, held))
@@ -491,15 +505,13 @@
     return pl.BlockSpec(memory_space=pltpu.VMEM)
 
 
-def pack_call(pipe, arrays, count):
+def pack_call(pipe, arrays):
     qkv, out, fc = arrays[:3]
     width = (qkv.shape[1] + out.shape[1]) // 2 + fc.shape[1] + SMALL
     packet = jax.ShapeDtypeStruct((qkv.shape[0], width), BF)
-    whole = jax.ShapeDtypeStruct((count * qkv.shape[0], width), BF)
     return pl.pallas_call(
         pack_kernel,
-        out_shape=(packet, packet, whole, whole),
-        out_specs=(in_vmem(),) * 4,
+        out_shape=(packet, packet),
         in_specs=[pl.BlockSpec(memory_space=pltpu.SMEM)]
         + [pl.BlockSpec(memory_space=pl.ANY)] * len(arrays),
         scratch_shapes=[pltpu.VMEM(item.shape, item.dtype) for item in arrays]
@@ -681,7 +693,7 @@
     pipe_word = pipe.astype(jnp.int32).reshape(1)
     vectors = jnp.concatenate([ln1_gain, ln1_shift, ln2_gain, ln2_shift, branch_bias], axis=0)
     vectors = jnp.pad(vectors.astype(F32), ((0, 3), (0, 0)))
-    kept_part, sent_part, first_whole, second_whole = pack_call(
+    kept_part, sent_part = pack_call(
         pipe_word,
         (
             qkv_weight[0],
@@ -691,8 +703,8 @@
             vectors,
             jnp.concatenate([qkv_bias, fc_bias], axis=1).astype(F32),
         ),
-        count,
-    )
+    )
+    first_whole, second_whole = blank_call(sent_part, count), blank_call(kept_part, count)
     came_part = swap(sent_part, "pipe")
     chunk = jnp.where(leading, kept_part, came_part)
     gather = RingGather(chunk, first_whole, ahead_steps)

time: 236 us -> 232 us (0.983)
  waiting for transfers between devices: 108 us -> 105 us
    ppermute x28, waiting for transfers between devices: 32.4 us -> 28.9 us  [swap(): return lax.ppermute(block, axis, [(0, 1), (1, 0)])]
where the time goes in v4:
time: 232 us
  waiting for transfers between devices  105 us (45%)
  starting transfers between devices  52 us (22%)
  Pallas kernels  32.6 us (14%)
  local copies, waits for them, and re-layouts  32.5 us (14%)
  other arithmetic  8.34 us (4%)
    ppermute x7, waiting for transfers between devices, advance(): front = lax.ppermute(own, 'dp', self.ahead)  33.4 us
    ppermute x7, waiting for transfers between devices, advance(): self.front = lax.ppermute(front, 'dp', self.ahead)  31.3 us
    ppermute x28, waiting for transfers between devices, swap(): return lax.ppermute(block, axis, [(0, 1), (1, 0)])  28.9 us
    ppermute x28, starting transfers between devices, swap(): return lax.ppermute(block, axis, [(0, 1), (1, 0)])  21.3 us
    pallas_call x4, Pallas kernels, backward_call(): pl.pallas_call(functools.partial(backward_kernel, heads), out_shape=outs,...  15 us
    dynamic_update_slice x14, local copies, waits for them, and re-layouts, put(): lax.dynamic_update_slice(self.whole, block, (owner * self.depth, 0))  14 us
    ppermute x7, starting transfers between devices, advance(): back = lax.ppermute(own, 'dp', self.behind)  11.3 us
    ppermute x7, starting transfers between devices, advance(): self.front = lax.ppermute(front, 'dp', self.ahead)  10 us
  transfers between devices with their start and end apart: 56, of which 27 were waited for; matrix products, arithmetic and copies ran while one was open for 13% of the time, Pallas kernels for 13%

profile of v4, /device:TPU:0, one launch (start us, length us, event | category | flops | bytes accessed | tf_op | source)
XLA Modules:
  0.0 231.7 jit_solution(760871505302161869)
XLA Ops:
  6.7 3.1 %collective-permute-start.1 = (bf16[96,2432]{1,0:T(8,128)(2,1)S(1)}, bf16[96,2432]{1,0:T(8,128)(2,1)S(1)}, u32[]{:S(2)}, u32[]{:S(2)}) collective-permute-start(bf16[96,2432]{1,0:T(8,128)(2,1)S(1)} %get-tuple-element.94.like_ref), channel_id=1, source_target_pairs={{0,16},{16,0},{1,17},{17,1},{2,18},{18,2},{3,19},{19,3},{4,20},{20... | collective-permute-start | bytes 1400840 | tf_op jit(solution)/shard_map/ppermute | solution.py:171
  10.9 1.8 copy-done
  12.8 1.8 copy-done.3
  14.6 5.9 %collective-permute-done.1 = bf16[96,2432]{1,0:T(8,128)(2,1)S(1)} collective-permute-done((bf16[96,2432]{1,0:T(8,128)(2,1)S(1)}, bf16[96,2432]{1,0:T(8,128)(2,1)S(1)}, u32[]{:S(2)}, u32[]{:S(2)}) %collective-permute-start.1) | collective-permute-done | bytes 466976 | tf_op jit(solution)/shard_map/ppermute | solution.py:171
  20.5 1.4 constant_dynamic-update-slice_fusion.7
  22.0 1.8 collective-permute-start.2
  24.0 1.8 collective-permute-start.6
  26.6 1.4 multiply_sine_fusion.1
  32.1 2.1 concatenate.82.lower_ref
  35.9 1.8 collective-permute-done.3
  37.7 1.6 collective-permute-start.4
  39.7 6.2 %collective-permute-done.6 = bf16[96,2432]{1,0:T(8,128)(2,1)} collective-permute-done((bf16[96,2432]{1,0:T(8,128)(2,1)}, bf16[96,2432]{1,0:T(8,128)(2,1)}, u32[]{:S(2)}, u32[]{:S(2)}) %collective-permute-start.6) | collective-permute-done | bytes 466976 | tf_op jit(solution)/shard_map/ppermute | solution.py:114
  45.9 1.8 collective-permute-done.7
  47.7 1.6 collective-permute-start.10
  49.7 1.9 constant_dynamic-update-slice_fusion.14
  51.6 1.8 constant_dynamic-update-slice_fusion.6
  53.4 1.8 constant_dynamic-update-slice_fusion.13
  55.2 1.8 constant_dynamic-update-slice_fusion.5
  57.6 1.6 collective-permute-start.8
  59.2 6.7 %collective-permute-done.10 = bf16[96,2432]{1,0:T(8,128)(2,1)S(1)} collective-permute-done((bf16[96,2432]{1,0:T(8,128)(2,1)}, bf16[96,2432]{1,0:T(8,128)(2,1)S(1)}, u32[]{:S(2)}, u32[]{:S(2)}) %collective-permute-start.10) | collective-permute-done | bytes 466976 | tf_op jit(solution)/shard_map/ppermute | solution.py:114
  65.8 1.7 collective-permute-start.9
  71.1 4.7 %collective-permute-done.8 = bf16[96,2432]{1,0:T(8,128)(2,1)S(1)} collective-permute-done((bf16[96,2432]{1,0:T(8,128)(2,1)S(1)}, bf16[96,2432]{1,0:T(8,128)(2,1)S(1)}, u32[]{:S(2)}, u32[]{:S(2)}) %collective-permute-start.8) | collective-permute-done | bytes 466976 | tf_op jit(solution)/shard_map/ppermute | solution.py:114
  75.8 1.7 collective-permute-start.20
  78.3 5.7 %collective-permute-done.19 = bf16[96,2432]{1,0:T(8,128)(2,1)S(1)} collective-permute-done((bf16[96,2432]{1,0:T(8,128)(2,1)S(1)}, bf16[96,2432]{1,0:T(8,128)(2,1)S(1)}, u32[]{:S(2)}, u32[]{:S(2)}) %collective-permute-start.19) | collective-permute-done | bytes 466976 | tf_op jit(solution)/shard_map/ppermute | solution.py:114
  84.1 1.4 collective-permute-start.12
  87.7 7.4 %collective-permute-done.12 = bf16[96,2432]{1,0:T(8,128)(2,1)S(1)} collective-permute-done((bf16[96,2432]{1,0:T(8,128)(2,1)S(1)}, bf16[96,2432]{1,0:T(8,128)(2,1)S(1)}, u32[]{:S(2)}, u32[]{:S(2)}) %collective-permute-start.12) | collective-permute-done | bytes 466976 | tf_op jit(solution)/shard_map/ppermute | solution.py:114
  97.0 2.1 copy-done.1
  99.0 2.2 forward.4
  101.4 2.3 forward.5
  104.3 1.6 collective-permute-start.14
  107.1 3.9 %collective-permute-done.14 = bf16[96,768]{1,0:T(8,128)(2,1)S(1)} collective-permute-done((bf16[96,768]{1,0:T(8,128)(2,1)S(1)}, bf16[96,768]{1,0:T(8,128)(2,1)S(1)}, u32[]{:S(2)}, u32[]{:S(2)}) %collective-permute-start.14) | collective-permute-done | bytes 147488 | tf_op jit(solution)/shard_map/ppermute | solution.py:171
  111.0 2.2 collective-permute-done.17
  114.9 2.3 forward.7
  117.3 2.2 forward.6
  120.0 3.7 %backward.4 = (f32[96,768]{1,0:T(8,128)S(1)}, f32[96,768]{1,0:T(8,128)S(1)}, bf16[192,640]{1,0:T(8,128)(2,1)S(1)}, bf16[192,768]{1,0:T(8,128)(2,1)S(1)}, f32[8,768]{1,0:T(8,128)S(1)}) custom-call(bf16[96,768]{1,0:T(8,128)(2,1)S(1)} %get-tuple-element.199.own_ref.refs_2_, bf16[96,768]{1,0:T(8,128)(2,1)S(1)} %collective-permute-done.27.far_ref.refs_3_, ...), custom_call_target="tpu_custom_call" | custom-call | flops 5000000000 | bytes 10000000 | tf_op jit(solution)/shard_map/backward/pallas_call | solution.py:583
  124.0 3.9 %backward.6 = (f32[96,768]{1,0:T(8,128)S(1)}, f32[96,768]{1,0:T(8,128)S(1)}, bf16[192,640]{1,0:T(8,128)(2,1)S(1)}, bf16[192,768]{1,0:T(8,128)(2,1)S(1)}, f32[8,768]{1,0:T(8,128)S(1)}) custom-call(bf16[96,768]{1,0:T(8,128)(2,1)S(1)} %get-tuple-element.200.own_ref.refs_11_, bf16[96,768]{1,0:T(8,128)(2,1)S(1)} %collective-permute-done.33.far_ref.refs_12_, ...), custom_call_target="tpu_custom_call" | custom-call | flops 5000000000 | bytes 10000000 | tf_op jit(solution)/shard_map/backward/pallas_call | solution.py:583
  128.4 1.6 collective-permute-start.26
  130.6 1.6 collective-permute-start.29
  132.8 3.1 %weights.2 = bf16[768,2432]{1,0:T(8,128)(2,1)S(1)} custom-call(bf16[192,3200]{1,0:T(8,128)(2,1)S(1)} %get-tuple-element.121.low_ref.refs_0_.refs_1_.refs_6_.refs_7_, bf16[192,3200]{1,0:T(8,128)(2,1)S(1)} %get-tuple-element.121.low_ref.refs_0_.refs_1_.refs_6_.refs_7_, bf16[96,768]{1,0:T(8,128)(2,1)S(1)} %get-tuple-element.199.own_ref.refs_2_, ...), custom_call_target="tpu_custom_call" | custom-call | flops 8000000000 | bytes 10000000 | tf_op jit(solution)/shard_map/weights/pallas_call | solution.py:624
  137.0 4.5 %collective-permute-done.29 = bf16[96,768]{1,0:T(8,128)(2,1)S(1)} collective-permute-done((bf16[96,768]{1,0:T(8,128)(2,1)S(1)}, bf16[96,768]{1,0:T(8,128)(2,1)S(1)}, u32[]{:S(2)}, u32[]{:S(2)}) %collective-permute-start.29) | collective-permute-done | bytes 147488 | tf_op jit(solution)/shard_map/ppermute | solution.py:171
  141.5 1.5 collective-permute-start.37
  145.4 3.7 %backward.5 = (f32[96,768]{1,0:T(8,128)S(1)}, f32[96,768]{1,0:T(8,128)S(1)}, bf16[192,640]{1,0:T(8,128)(2,1)S(1)}, bf16[192,768]{1,0:T(8,128)(2,1)S(1)}, f32[8,768]{1,0:T(8,128)S(1)}) custom-call(bf16[96,768]{1,0:T(8,128)(2,1)S(1)} %get-tuple-element.197.own_ref.refs_2_, bf16[96,768]{1,0:T(8,128)(2,1)S(1)} %collective-permute-done.30.far_ref.refs_3_, ...), custom_call_target="tpu_custom_call" | custom-call | flops 5000000000 | bytes 10000000 | tf_op jit(solution)/shard_map/backward/pallas_call | solution.py:583
  149.3 3.3 %collective-permute-done.37 = bf16[96,2432]{1,0:T(8,128)(2,1)S(1)} collective-permute-done((bf16[96,2432]{1,0:T(8,128)(2,1)S(1)}, bf16[96,2432]{1,0:T(8,128)(2,1)S(1)}, u32[]{:S(2)}, u32[]{:S(2)}) %collective-permute-start.37) | collective-permute-done | bytes 466976 | tf_op jit(solution)/shard_map/ppermute | solution.py:159
  152.9 1.6 collective-permute-start.44
  155.0 3.7 %backward.7 = (f32[96,768]{1,0:T(8,128)S(1)}, f32[96,768]{1,0:T(8,128)S(1)}, bf16[192,640]{1,0:T(8,128)(2,1)S(1)}, bf16[192,768]{1,0:T(8,128)(2,1)S(1)}, f32[8,768]{1,0:T(8,128)S(1)}) custom-call(bf16[96,768]{1,0:T(8,128)(2,1)S(1)} %get-tuple-element.142.own_ref.refs_11_, bf16[96,768]{1,0:T(8,128)(2,1)S(1)} %collective-permute-done.38.far_ref.refs_12_, ...), custom_call_target="tpu_custom_call" | custom-call | flops 5000000000 | bytes 10000000 | tf_op jit(solution)/shard_map/backward/pallas_call | solution.py:583
  158.6 3.1 %weights.3 = bf16[768,2432]{1,0:T(8,128)(2,1)S(1)} custom-call(bf16[192,3200]{1,0:T(8,128)(2,1)S(1)} %get-tuple-element.125.low_ref.refs_0_.refs_1_.refs_6_.refs_7_, bf16[192,3200]{1,0:T(8,128)(2,1)S(1)} %get-tuple-element.125.low_ref.refs_0_.refs_1_.refs_6_.refs_7_, bf16[96,768]{1,0:T(8,128)(2,1)S(1)} %get-tuple-element.197.own_ref.refs_2_, ...), custom_call_target="tpu_custom_call" | custom-call | flops 8000000000 | bytes 10000000 | tf_op jit(solution)/shard_map/weights/pallas_call | solution.py:624
  162.8 4.3 %collective-permute-done.43 = bf16[96,2432]{1,0:T(8,128)(2,1)S(1)} collective-permute-done((bf16[96,2432]{1,0:T(8,128)(2,1)S(1)}, bf16[96,2432]{1,0:T(8,128)(2,1)S(1)}, u32[]{:S(2)}, u32[]{:S(2)}) %collective-permute-start.43) | collective-permute-done | bytes 466976 | tf_op jit(solution)/shard_map/ppermute | solution.py:153
  167.1 1.6 collective-permute-start.42
  169.4 7.7 %collective-permute-done.41 = bf16[96,2432]{1,0:T(8,128)(2,1)S(1)} collective-permute-done((bf16[96,2432]{1,0:T(8,128)(2,1)S(1)}, bf16[96,2432]{1,0:T(8,128)(2,1)S(1)}, u32[]{:S(2)}, u32[]{:S(2)}) %collective-permute-start.41) | collective-permute-done | bytes 466976 | tf_op jit(solution)/shard_map/ppermute | solution.py:153
  177.1 1.6 collective-permute-start.48
  179.5 7.6 %collective-permute-done.47 = bf16[96,2432]{1,0:T(8,128)(2,1)S(1)} collective-permute-done((bf16[96,2432]{1,0:T(8,128)(2,1)S(1)}, bf16[96,2432]{1,0:T(8,128)(2,1)S(1)}, u32[]{:S(2)}, u32[]{:S(2)}) %collective-permute-start.47) | collective-permute-done | bytes 466976 | tf_op jit(solution)/shard_map/ppermute | solution.py:153
  187.1 1.6 collective-permute-start.46
  188.8 5.6 %collective-permute-done.45 = bf16[96,2432]{1,0:T(8,128)(2,1)S(1)} collective-permute-done((bf16[96,2432]{1,0:T(8,128)(2,1)S(1)}, bf16[96,2432]{1,0:T(8,128)(2,1)S(1)}, u32[]{:S(2)}, u32[]{:S(2)}) %collective-permute-start.45) | collective-permute-done | bytes 466976 | tf_op jit(solution)/shard_map/ppermute | solution.py:153
  194.4 1.6 collective-permute-done.46
  196.4 2.1 collective-permute-start.50
  199.3 1.8 collective-permute-start.32
  201.2 4.5 %collective-permute-done.49 = bf16[96,2432]{1,0:T(8,128)(2,1)S(1)} collective-permute-done((bf16[96,2432]{1,0:T(8,128)(2,1)S(1)}, bf16[96,2432]{1,0:T(8,128)(2,1)S(1)}, u32[]{:S(2)}, u32[]{:S(2)}) %collective-permute-start.49) | collective-permute-done | bytes 466976 | tf_op jit(solution)/shard_map/ppermute | solution.py:153
  205.7 1.4 collective-permute-done.50
  207.2 1.4 collective-permute-start.51
  208.7 2.4 %collective-permute-start.40 = (bf16[96,768]{1,0:T(8,128)(2,1)S(1)}, bf16[96,768]{1,0:T(8,128)(2,1)S(1)}, u32[]{:S(2)}, u32[]{:S(2)}) collective-permute-start(bf16[96,768]{1,0:T(8,128)(2,1)S(1)} %add_convert_fusion.11), channel_id=1, source_target_pairs={{0,16},{16,0},{1,17},{17,1},{2,18},{18,2},{3,19},{19,3},{4,20},{20... | collective-permute-start | bytes 442376 | tf_op jit(solution)/shard_map/ppermute | solution.py:171
  211.2 3.7 %collective-permute-done.52 = bf16[96,2432]{1,0:T(8,128)(2,1)S(1)} collective-permute-done((bf16[96,2432]{1,0:T(8,128)(2,1)S(1)}, bf16[96,2432]{1,0:T(8,128)(2,1)S(1)}, u32[]{:S(2)}, u32[]{:S(2)}) %collective-permute-start.52) | collective-permute-done | bytes 466976 | tf_op jit(solution)/shard_map/ppermute | solution.py:153
  216.5 1.8 collective-permute-start.53
  220.3 9.9 %collective-permute-done.55.came_small_ref = f32[96,128]{1,0:T(8,128)S(1)} collective-permute-done((f32[96,128]{1,0:T(8,128)S(1)}, f32[96,128]{1,0:T(8,128)S(1)}, u32[]{:S(2)}, u32[]{:S(2)}) %collective-permute-start.55) | collective-permute-done | bytes 49184 | tf_op jit(solution)/shard_map/ppermute | solution.py:171
  230.2 1.5 unpack.1
  (175 shorter events, 41.8 us)
Async XLA Ops:
  6.7 13.8 %collective-permute-start.1 = (bf16[96,2432]{1,0:T(8,128)(2,1)S(1)}, bf16[96,2432]{1,0:T(8,128)(2,1)S(1)}, u32[]{:S(2)}, u32[]{:S(2)}) collective-permute-start(bf16[96,2432]{1,0:T(8,128)(2,1)S(1)} %get-tuple-element.94.like_ref), channel_id=1, source_target_pairs={{0,16},{16,0},{1,17},{17,1},{2,18},{18,2},{3,19},{19,3},{4,20},{20... | collective-permute-start | bytes 1400840 | tf_op jit(solution)/shard_map/ppermute | solution.py:171
  10.8 86.1 %collective-permute-start = (bf16[96,768]{1,0:T(8,128)(2,1)S(1)}, bf16[96,768]{1,0:T(8,128)(2,1)S(1)}, u32[]{:S(2)}, u32[]{:S(2)}) collective-permute-start(bf16[96,768]{1,0:T(8,128)(2,1)S(1)} %get-tuple-element.203.own_ref), channel_id=1, source_target_pairs={{0,1},{1,0},{2,3},{3,2},{4,5},{5,4},{6,7},{7,6},{8,9},{9,8},{10,11... | collective-permute-start | bytes 442376 | tf_op jit(solution)/shard_map/ppermute | solution.py:171
  12.7 13.3 %copy-start.15 = (s32[2,1,3]{2,1,0:T(1,128)S(1)}, s32[2,1,3]{2,1,0:T(1,128)}, u32[]{:S(2)}) copy-start(s32[2,1,3]{2,1,0:T(1,128)} %param.15) | copy-start | bytes 76
  22.0 13.9 %collective-permute-start.2 = (bf16[96,2432]{1,0:T(8,128)(2,1)}, bf16[96,2432]{1,0:T(8,128)(2,1)}, u32[]{:S(2)}, u32[]{:S(2)}) collective-permute-start(bf16[96,2432]{1,0:T(8,128)(2,1)} %get-tuple-element.196), channel_id=1, source_target_pairs={{0,4},{4,8},{8,12},{12,14},{14,10},{10,6},{6,2},{2,0},{1,5},{5,9},... | collective-permute-start | bytes 1400840 | tf_op jit(solution)/shard_map/ppermute | solution.py:114
  23.7 13.9 %collective-permute-start.3 = (bf16[96,2432]{1,0:T(8,128)(2,1)}, bf16[96,2432]{1,0:T(8,128)(2,1)}, u32[]{:S(2)}, u32[]{:S(2)}) collective-permute-start(bf16[96,2432]{1,0:T(8,128)(2,1)} %get-tuple-element.196), channel_id=1, source_target_pairs={{4,0},{8,4},{12,8},{14,12},{10,14},{6,10},{2,6},{0,2},{5,1},{9,5},... | collective-permute-start | bytes 1400840 | tf_op jit(solution)/shard_map/ppermute | solution.py:117
  24.0 21.9 %collective-permute-start.6 = (bf16[96,2432]{1,0:T(8,128)(2,1)}, bf16[96,2432]{1,0:T(8,128)(2,1)}, u32[]{:S(2)}, u32[]{:S(2)}) collective-permute-start(bf16[96,2432]{1,0:T(8,128)(2,1)} %get-tuple-element.178), channel_id=1, source_target_pairs={{0,4},{4,8},{8,12},{12,14},{14,10},{10,6},{6,2},{2,0},{1,5},{5,9},... | collective-permute-start | bytes 1400840 | tf_op jit(solution)/shard_map/ppermute | solution.py:114
  25.7 21.9 %collective-permute-start.7 = (bf16[96,2432]{1,0:T(8,128)(2,1)}, bf16[96,2432]{1,0:T(8,128)(2,1)}, u32[]{:S(2)}, u32[]{:S(2)}) collective-permute-start(bf16[96,2432]{1,0:T(8,128)(2,1)} %get-tuple-element.178), channel_id=1, source_target_pairs={{4,0},{8,4},{12,8},{14,12},{10,14},{6,10},{2,6},{0,2},{5,1},{9,5},... | collective-permute-start | bytes 1400840 | tf_op jit(solution)/shard_map/ppermute | solution.py:117
  28.0 3.3 %copy-start.9 = (f32[192,48]{1,0:T(8,128)}, f32[192,48]{1,0:T(8,128)S(1)}, u32[]{:S(2)}) copy-start(f32[192,48]{1,0:T(8,128)S(1)} %broadcast.139) | copy-start | bytes 110596
  28.0 3.2 %copy-start.10 = (f32[192,64]{1,0:T(8,128)}, f32[192,64]{1,0:T(8,128)S(1)}, u32[]{:S(2)}) copy-start(f32[192,64]{1,0:T(8,128)S(1)} %broadcast.140) | copy-start | bytes 147460
  37.7 19.4 %collective-permute-start.4 = (bf16[96,2432]{1,0:T(8,128)(2,1)}, bf16[96,2432]{1,0:T(8,128)(2,1)S(1)}, u32[]{:S(2)}, u32[]{:S(2)}) collective-permute-start(bf16[96,2432]{1,0:T(8,128)(2,1)} %collective-permute-done.2), channel_id=1, source_target_pairs={{0,4},{4,8},{8,12},{12,14},{14,10},{10,6},{6,2},{2,0},{1,5},{5,9},... | collective-permute-start | bytes 1400840 | tf_op jit(solution)/shard_map/ppermute | solution.py:114
  39.2 18.3 %collective-permute-start.5 = (bf16[96,2432]{1,0:T(8,128)(2,1)}, bf16[96,2432]{1,0:T(8,128)(2,1)S(1)}, u32[]{:S(2)}, u32[]{:S(2)}) collective-permute-start(bf16[96,2432]{1,0:T(8,128)(2,1)} %collective-permute-done.3), channel_id=1, source_target_pairs={{4,0},{8,4},{12,8},{14,12},{10,14},{6,10},{2,6},{0,2},{5,1},{9,5},... | collective-permute-start | bytes 1400840 | tf_op jit(solution)/shard_map/ppermute | solution.py:117
  47.7 18.1 %collective-permute-start.10 = (bf16[96,2432]{1,0:T(8,128)(2,1)}, bf16[96,2432]{1,0:T(8,128)(2,1)S(1)}, u32[]{:S(2)}, u32[]{:S(2)}) collective-permute-start(bf16[96,2432]{1,0:T(8,128)(2,1)} %collective-permute-done.6), channel_id=1, source_target_pairs={{0,4},{4,8},{8,12},{12,14},{14,10},{10,6},{6,2},{2,0},{1,5},{5,9},... | collective-permute-start | bytes 1400840 | tf_op jit(solution)/shard_map/ppermute | solution.py:114
  49.3 18.3 %collective-permute-start.11 = (bf16[96,2432]{1,0:T(8,128)(2,1)}, bf16[96,2432]{1,0:T(8,128)(2,1)S(1)}, u32[]{:S(2)}, u32[]{:S(2)}) collective-permute-start(bf16[96,2432]{1,0:T(8,128)(2,1)} %collective-permute-done.7), channel_id=1, source_target_pairs={{4,0},{8,4},{12,8},{14,12},{10,14},{6,10},{2,6},{0,2},{5,1},{9,5},... | collective-permute-start | bytes 1400840 | tf_op jit(solution)/shard_map/ppermute | solution.py:117
  57.1 44.3 %collective-permute-start.15 = (bf16[96,768]{1,0:T(8,128)(2,1)S(1)}, bf16[96,768]{1,0:T(8,128)(2,1)S(1)}, u32[]{:S(2)}, u32[]{:S(2)}) collective-permute-start(bf16[96,768]{1,0:T(8,128)(2,1)S(1)} %get-tuple-element.204.own_ref), channel_id=1, source_target_pairs={{0,1},{1,0},{2,3},{3,2},{4,5},{5,4},{6,7},{7,6},{8,9},{9,8},{10,11... | collective-permute-start | bytes 442376 | tf_op jit(solution)/shard_map/ppermute | solution.py:171
  57.6 18.2 %collective-permute-start.8 = (bf16[96,2432]{1,0:T(8,128)(2,1)S(1)}, bf16[96,2432]{1,0:T(8,128)(2,1)S(1)}, u32[]{:S(2)}, u32[]{:S(2)}) collective-permute-start(bf16[96,2432]{1,0:T(8,128)(2,1)S(1)} %collective-permute-done.4), channel_id=1, source_target_pairs={{0,4},{4,8},{8,12},{12,14},{14,10},{10,6},{6,2},{2,0},{1,5},{5,9},... | collective-permute-start | bytes 1400840 | tf_op jit(solution)/shard_map/ppermute | solution.py:114
  65.8 20.5 %collective-permute-start.9 = (bf16[96,2432]{1,0:T(8,128)(2,1)S(1)}, bf16[96,2432]{1,0:T(8,128)(2,1)S(1)}, u32[]{:S(2)}, u32[]{:S(2)}) collective-permute-start(bf16[96,2432]{1,0:T(8,128)(2,1)S(1)} %collective-permute-done.5), channel_id=1, source_target_pairs={{4,0},{8,4},{12,8},{14,12},{10,14},{6,10},{2,6},{0,2},{5,1},{9,5},... | collective-permute-start | bytes 1400840 | tf_op jit(solution)/shard_map/ppermute | solution.py:117
  67.5 16.6 %collective-permute-start.19 = (bf16[96,2432]{1,0:T(8,128)(2,1)S(1)}, bf16[96,2432]{1,0:T(8,128)(2,1)S(1)}, u32[]{:S(2)}, u32[]{:S(2)}) collective-permute-start(bf16[96,2432]{1,0:T(8,128)(2,1)S(1)} %collective-permute-done.10), channel_id=1, source_target_pairs={{0,4},{4,8},{8,12},{12,14},{14,10},{10,6},{6,2},{2,0},{1,5},{5,9},... | collective-permute-start | bytes 1400840 | tf_op jit(solution)/shard_map/ppermute | solution.py:114
  75.8 10.5 %collective-permute-start.20 = (bf16[96,2432]{1,0:T(8,128)(2,1)S(1)}, bf16[96,2432]{1,0:T(8,128)(2,1)S(1)}, u32[]{:S(2)}, u32[]{:S(2)}) collective-permute-start(bf16[96,2432]{1,0:T(8,128)(2,1)S(1)} %collective-permute-done.11), channel_id=1, source_target_pairs={{4,0},{8,4},{12,8},{14,12},{10,14},{6,10},{2,6},{0,2},{5,1},{9,5},... | collective-permute-start | bytes 1400840 | tf_op jit(solution)/shard_map/ppermute | solution.py:117
  84.1 11.0 %collective-permute-start.12 = (bf16[96,2432]{1,0:T(8,128)(2,1)S(1)}, bf16[96,2432]{1,0:T(8,128)(2,1)S(1)}, u32[]{:S(2)}, u32[]{:S(2)}) collective-permute-start(bf16[96,2432]{1,0:T(8,128)(2,1)S(1)} %collective-permute-done.8), channel_id=1, source_target_pairs={{0,4},{4,8},{8,12},{12,14},{14,10},{10,6},{6,2},{2,0},{1,5},{5,9},... | collective-permute-start | bytes 1400840 | tf_op jit(solution)/shard_map/ppermute | solution.py:114
  86.3 33.7 %collective-permute-start.27 = (bf16[96,768]{1,0:T(8,128)(2,1)S(1)}, bf16[96,768]{1,0:T(8,128)(2,1)S(1)}, u32[]{:S(2)}, u32[]{:S(2)}) collective-permute-start(bf16[96,768]{1,0:T(8,128)(2,1)S(1)} %get-tuple-element.199.own_ref.refs_2_), channel_id=1, source_target_pairs={{0,1},{1,0},{2,3},{3,2},{4,5},{5,4},{6,7},{7,6},{8,9},{9,8},{10,11... | collective-permute-start | bytes 442376 | tf_op jit(solution)/shard_map/ppermute | solution.py:171
  86.4 37.6 %collective-permute-start.33 = (bf16[96,768]{1,0:T(8,128)(2,1)S(1)}, bf16[96,768]{1,0:T(8,128)(2,1)S(1)}, u32[]{:S(2)}, u32[]{:S(2)}) collective-permute-start(bf16[96,768]{1,0:T(8,128)(2,1)S(1)} %get-tuple-element.200.own_ref.refs_11_), channel_id=1, source_target_pairs={{0,1},{1,0},{2,3},{3,2},{4,5},{5,4},{6,7},{7,6},{8,9},{9,8},{10,11... | collective-permute-start | bytes 442376 | tf_op jit(solution)/shard_map/ppermute | solution.py:171
  95.0 18.5 %collective-permute-start.21 = (bf16[96,2432]{1,0:T(8,128)(2,1)S(1)}, bf16[96,2432]{1,0:T(8,128)(2,1)S(1)}, u32[]{:S(2)}, u32[]{:S(2)}) collective-permute-start(bf16[96,2432]{1,0:T(8,128)(2,1)S(1)} %collective-permute-done.20), channel_id=1, source_target_pairs={{4,0},{8,4},{12,8},{14,12},{10,14},{6,10},{2,6},{0,2},{5,1},{9,5},... | collective-permute-start | bytes 1400840 | tf_op jit(solution)/shard_map/ppermute | solution.py:117
  97.0 2.1 copy-start.1
  101.3 2.9 %collective-permute-start.13 = (f32[96,768]{1,0:T(8,128)S(1)}, f32[96,768]{1,0:T(8,128)S(1)}, u32[]{:S(2)}, u32[]{:S(2)}) collective-permute-start(f32[96,768]{1,0:T(8,128)S(1)} %get-tuple-element.109), channel_id=1, source_target_pairs={{0,1},{1,0},{2,3},{3,2},{4,5},{5,4},{6,7},{7,6},{8,9},{9,8},{10,11... | collective-permute-start | bytes 884744 | tf_op jit(solution)/shard_map/ppermute | solution.py:171
  101.4 2.8 %copy-start.4 = (bf16[768,2432]{1,0:T(8,128)(2,1)S(1)}, bf16[768,2432]{1,0:T(8,128)(2,1)}, u32[]{:S(2)}) copy-start(bf16[768,2432]{1,0:T(8,128)(2,1)} %constant_dynamic-update-slice_fusion.2) | copy-start | bytes 11206660
  101.4 11.9 %copy-start.13 = (bf16[2,96,768]{2,1,0:T(8,128)(2,1)S(1)}, bf16[2,96,768]{2,1,0:T(8,128)(2,1)}, u32[]{:S(2)}) copy-start(bf16[2,96,768]{2,1,0:T(8,128)(2,1)} %param.14) | copy-start | bytes 884740
  103.6 2.3 collective-permute-start.16
  104.3 6.8 %collective-permute-start.14 = (bf16[96,768]{1,0:T(8,128)(2,1)S(1)}, bf16[96,768]{1,0:T(8,128)(2,1)S(1)}, u32[]{:S(2)}, u32[]{:S(2)}) collective-permute-start(bf16[96,768]{1,0:T(8,128)(2,1)S(1)} %add_convert_fusion.25), channel_id=1, source_target_pairs={{0,16},{16,0},{1,17},{17,1},{2,18},{18,2},{3,19},{19,3},{4,20},{20... | collective-permute-start | bytes 442376 | tf_op jit(solution)/shard_map/ppermute | solution.py:171
  105.9 7.3 %collective-permute-start.17 = (bf16[96,768]{1,0:T(8,128)(2,1)S(1)}, bf16[96,768]{1,0:T(8,128)(2,1)S(1)}, u32[]{:S(2)}, u32[]{:S(2)}) collective-permute-start(bf16[96,768]{1,0:T(8,128)(2,1)S(1)} %add_convert_fusion.23), channel_id=1, source_target_pairs={{0,16},{16,0},{1,17},{17,1},{2,18},{18,2},{3,19},{19,3},{4,20},{20... | collective-permute-start | bytes 442376 | tf_op jit(solution)/shard_map/ppermute | solution.py:171
  113.4 1.4 collective-permute-start.24
  113.6 3.8 %collective-permute-start.18 = (bf16[96,768]{1,0:T(8,128)(2,1)S(1)}, bf16[96,768]{1,0:T(8,128)(2,1)S(1)}, u32[]{:S(2)}, u32[]{:S(2)}) collective-permute-start(bf16[96,768]{1,0:T(8,128)(2,1)S(1)} %get-tuple-element.201.own_ref), channel_id=1, source_target_pairs={{0,1},{1,0},{2,3},{3,2},{4,5},{5,4},{6,7},{7,6},{8,9},{9,8},{10,11... | collective-permute-start | bytes 442376 | tf_op jit(solution)/shard_map/ppermute | solution.py:171
  117.1 11.3 %collective-permute-start.25 = (f32[96,768]{1,0:T(8,128)S(1)}, f32[96,768]{1,0:T(8,128)S(1)}, u32[]{:S(2)}, u32[]{:S(2)}) collective-permute-start(f32[96,768]{1,0:T(8,128)S(1)} %get-tuple-element.119), channel_id=1, source_target_pairs={{0,1},{1,0},{2,3},{3,2},{4,5},{5,4},{6,7},{7,6},{8,9},{9,8},{10,11... | collective-permute-start | bytes 884744 | tf_op jit(solution)/shard_map/ppermute | solution.py:171
  119.6 10.5 %collective-permute-start.22 = (f32[96,768]{1,0:T(8,128)S(1)}, f32[96,768]{1,0:T(8,128)S(1)}, u32[]{:S(2)}, u32[]{:S(2)}) collective-permute-start(f32[96,768]{1,0:T(8,128)S(1)} %get-tuple-element.116), channel_id=1, source_target_pairs={{0,1},{1,0},{2,3},{3,2},{4,5},{5,4},{6,7},{7,6},{8,9},{9,8},{10,11... | collective-permute-start | bytes 884744 | tf_op jit(solution)/shard_map/ppermute | solution.py:171
  123.8 6.9 %collective-permute-start.28 = (f32[96,768]{1,0:T(8,128)S(1)}, f32[96,768]{1,0:T(8,128)S(1)}, u32[]{:S(2)}, u32[]{:S(2)}) collective-permute-start(f32[96,768]{1,0:T(8,128)S(1)} %get-tuple-element.124), channel_id=1, source_target_pairs={{0,1},{1,0},{2,3},{3,2},{4,5},{5,4},{6,7},{7,6},{8,9},{9,8},{10,11... | collective-permute-start | bytes 884744 | tf_op jit(solution)/shard_map/ppermute | solution.py:171
  127.9 4.3 %collective-permute-start.34 = (f32[96,768]{1,0:T(8,128)S(1)}, f32[96,768]{1,0:T(8,128)S(1)}, u32[]{:S(2)}, u32[]{:S(2)}) collective-permute-start(f32[96,768]{1,0:T(8,128)S(1)} %get-tuple-element.132), channel_id=1, source_target_pairs={{0,1},{1,0},{2,3},{3,2},{4,5},{5,4},{6,7},{7,6},{8,9},{9,8},{10,11... | collective-permute-start | bytes 884744 | tf_op jit(solution)/shard_map/ppermute | solution.py:171
  128.4 15.6 %collective-permute-start.26 = (bf16[96,768]{1,0:T(8,128)(2,1)S(1)}, bf16[96,768]{1,0:T(8,128)(2,1)S(1)}, u32[]{:S(2)}, u32[]{:S(2)}) collective-permute-start(bf16[96,768]{1,0:T(8,128)(2,1)S(1)} %add_convert_fusion.19), channel_id=1, source_target_pairs={{0,16},{16,0},{1,17},{17,1},{2,18},{18,2},{3,19},{19,3},{4,20},{20... | collective-permute-start | bytes 442376 | tf_op jit(solution)/shard_map/ppermute | solution.py:171
  130.1 68.4 %collective-permute-start.23 = (bf16[96,768]{1,0:T(8,128)(2,1)S(1)}, bf16[96,768]{1,0:T(8,128)(2,1)S(1)}, u32[]{:S(2)}, u32[]{:S(2)}) collective-permute-start(bf16[96,768]{1,0:T(8,128)(2,1)S(1)} %add_convert_fusion.21), channel_id=1, source_target_pairs={{0,16},{16,0},{1,17},{17,1},{2,18},{18,2},{3,19},{19,3},{4,20},{20... | collective-permute-start | bytes 442376 | tf_op jit(solution)/shard_map/ppermute | solution.py:171
  130.6 10.8 %collective-permute-start.29 = (bf16[96,768]{1,0:T(8,128)(2,1)S(1)}, bf16[96,768]{1,0:T(8,128)(2,1)S(1)}, u32[]{:S(2)}, u32[]{:S(2)}) collective-permute-start(bf16[96,768]{1,0:T(8,128)(2,1)S(1)} %add_convert_fusion.17), channel_id=1, source_target_pairs={{0,16},{16,0},{1,17},{17,1},{2,18},{18,2},{3,19},{19,3},{4,20},{20... | collective-permute-start | bytes 442376 | tf_op jit(solution)/shard_map/ppermute | solution.py:171
  132.3 11.5 %collective-permute-start.35 = (bf16[96,768]{1,0:T(8,128)(2,1)S(1)}, bf16[96,768]{1,0:T(8,128)(2,1)S(1)}, u32[]{:S(2)}, u32[]{:S(2)}) collective-permute-start(bf16[96,768]{1,0:T(8,128)(2,1)S(1)} %add_convert_fusion.13), channel_id=1, source_target_pairs={{0,16},{16,0},{1,17},{17,1},{2,18},{18,2},{3,19},{19,3},{4,20},{20... | collective-permute-start | bytes 442376 | tf_op jit(solution)/shard_map/ppermute | solution.py:171
  132.8 11.0 %copy-start.14 = (bf16[2,96,768]{2,1,0:T(8,128)(2,1)S(1)}, bf16[2,96,768]{2,1,0:T(8,128)(2,1)}, u32[]{:S(2)}) copy-start(bf16[2,96,768]{2,1,0:T(8,128)(2,1)} %param.27) | copy-start | bytes 884740
  132.8 12.6 %copy-start.2 = (bf16[768,2432]{1,0:T(8,128)(2,1)S(1)}, bf16[768,2432]{1,0:T(8,128)(2,1)}, u32[]{:S(2)}) copy-start(bf16[768,2432]{1,0:T(8,128)(2,1)} %constant_dynamic-update-slice_fusion.8.weight_ref) | copy-start | bytes 11206660
  136.0 13.3 %collective-permute-start.36 = (bf16[96,2432]{1,0:T(8,128)(2,1)S(1)}, bf16[96,2432]{1,0:T(8,128)(2,1)S(1)}, u32[]{:S(2)}, u32[]{:S(2)}) collective-permute-start(bf16[96,2432]{1,0:T(8,128)(2,1)S(1)} %get-tuple-element.194), channel_id=1, source_target_pairs={{0,4},{4,8},{8,12},{12,14},{14,10},{10,6},{6,2},{2,0},{1,5},{5,9},... | collective-permute-start | bytes 1400840 | tf_op jit(solution)/shard_map/ppermute | solution.py:153
  141.5 11.1 %collective-permute-start.37 = (bf16[96,2432]{1,0:T(8,128)(2,1)S(1)}, bf16[96,2432]{1,0:T(8,128)(2,1)S(1)}, u32[]{:S(2)}, u32[]{:S(2)}) collective-permute-start(bf16[96,2432]{1,0:T(8,128)(2,1)S(1)} %get-tuple-element.193), channel_id=1, source_target_pairs={{4,0},{8,4},{12,8},{14,12},{10,14},{6,10},{2,6},{0,2},{5,1},{9,5},... | collective-permute-start | bytes 1400840 | tf_op jit(solution)/shard_map/ppermute | solution.py:159
  144.0 1.4 collective-permute-start.30
  144.1 10.9 %collective-permute-start.38 = (bf16[96,768]{1,0:T(8,128)(2,1)S(1)}, bf16[96,768]{1,0:T(8,128)(2,1)S(1)}, u32[]{:S(2)}, u32[]{:S(2)}) collective-permute-start(bf16[96,768]{1,0:T(8,128)(2,1)S(1)} %get-tuple-element.142.own_ref.refs_11_), channel_id=1, source_target_pairs={{0,1},{1,0},{2,3},{3,2},{4,5},{5,4},{6,7},{7,6},{8,9},{9,8},{10,11... | collective-permute-start | bytes 442376 | tf_op jit(solution)/shard_map/ppermute | solution.py:171
  149.1 50.2 %collective-permute-start.31 = (f32[96,768]{1,0:T(8,128)S(1)}, f32[96,768]{1,0:T(8,128)S(1)}, u32[]{:S(2)}, u32[]{:S(2)}) collective-permute-start(f32[96,768]{1,0:T(8,128)S(1)} %get-tuple-element.128), channel_id=1, source_target_pairs={{0,1},{1,0},{2,3},{3,2},{4,5},{5,4},{6,7},{7,6},{8,9},{9,8},{10,11... | collective-permute-start | bytes 884744 | tf_op jit(solution)/shard_map/ppermute | solution.py:171
  152.9 15.8 %collective-permute-start.44 = (bf16[96,2432]{1,0:T(8,128)(2,1)S(1)}, bf16[96,2432]{1,0:T(8,128)(2,1)S(1)}, u32[]{:S(2)}, u32[]{:S(2)}) collective-permute-start(bf16[96,2432]{1,0:T(8,128)(2,1)S(1)} %get-tuple-element.192), channel_id=1, source_target_pairs={{4,0},{8,4},{12,8},{14,12},{10,14},{6,10},{2,6},{0,2},{5,1},{9,5},... | collective-permute-start | bytes 1400840 | tf_op jit(solution)/shard_map/ppermute | solution.py:159
  154.5 12.7 %collective-permute-start.43 = (bf16[96,2432]{1,0:T(8,128)(2,1)S(1)}, bf16[96,2432]{1,0:T(8,128)(2,1)S(1)}, u32[]{:S(2)}, u32[]{:S(2)}) collective-permute-start(bf16[96,2432]{1,0:T(8,128)(2,1)S(1)} %get-tuple-element.191), channel_id=1, source_target_pairs={{0,4},{4,8},{8,12},{12,14},{14,10},{10,6},{6,2},{2,0},{1,5},{5,9},... | collective-permute-start | bytes 1400840 | tf_op jit(solution)/shard_map/ppermute | solution.py:153
  161.9 15.2 %collective-permute-start.41 = (bf16[96,2432]{1,0:T(8,128)(2,1)S(1)}, bf16[96,2432]{1,0:T(8,128)(2,1)S(1)}, u32[]{:S(2)}, u32[]{:S(2)}) collective-permute-start(bf16[96,2432]{1,0:T(8,128)(2,1)S(1)} %get-tuple-element.190), channel_id=1, source_target_pairs={{0,4},{4,8},{8,12},{12,14},{14,10},{10,6},{6,2},{2,0},{1,5},{5,9},... | collective-permute-start | bytes 1400840 | tf_op jit(solution)/shard_map/ppermute | solution.py:153
  167.1 11.6 %collective-permute-start.42 = (bf16[96,2432]{1,0:T(8,128)(2,1)S(1)}, bf16[96,2432]{1,0:T(8,128)(2,1)S(1)}, u32[]{:S(2)}, u32[]{:S(2)}) collective-permute-start(bf16[96,2432]{1,0:T(8,128)(2,1)S(1)} %get-tuple-element.189), channel_id=1, source_target_pairs={{4,0},{8,4},{12,8},{14,12},{10,14},{6,10},{2,6},{0,2},{5,1},{9,5},... | collective-permute-start | bytes 1400840 | tf_op jit(solution)/shard_map/ppermute | solution.py:159
  169.0 18.2 %collective-permute-start.47 = (bf16[96,2432]{1,0:T(8,128)(2,1)S(1)}, bf16[96,2432]{1,0:T(8,128)(2,1)S(1)}, u32[]{:S(2)}, u32[]{:S(2)}) collective-permute-start(bf16[96,2432]{1,0:T(8,128)(2,1)S(1)} %get-tuple-element.188), channel_id=1, source_target_pairs={{0,4},{4,8},{8,12},{12,14},{14,10},{10,6},{6,2},{2,0},{1,5},{5,9},... | collective-permute-start | bytes 1400840 | tf_op jit(solution)/shard_map/ppermute | solution.py:153
  177.1 11.6 %collective-permute-start.48 = (bf16[96,2432]{1,0:T(8,128)(2,1)S(1)}, bf16[96,2432]{1,0:T(8,128)(2,1)S(1)}, u32[]{:S(2)}, u32[]{:S(2)}) collective-permute-start(bf16[96,2432]{1,0:T(8,128)(2,1)S(1)} %get-tuple-element.187), channel_id=1, source_target_pairs={{4,0},{8,4},{12,8},{14,12},{10,14},{6,10},{2,6},{0,2},{5,1},{9,5},... | collective-permute-start | bytes 1400840 | tf_op jit(solution)/shard_map/ppermute | solution.py:159
  179.0 15.4 %collective-permute-start.45 = (bf16[96,2432]{1,0:T(8,128)(2,1)S(1)}, bf16[96,2432]{1,0:T(8,128)(2,1)S(1)}, u32[]{:S(2)}, u32[]{:S(2)}) collective-permute-start(bf16[96,2432]{1,0:T(8,128)(2,1)S(1)} %get-tuple-element.186), channel_id=1, source_target_pairs={{0,4},{4,8},{8,12},{12,14},{14,10},{10,6},{6,2},{2,0},{1,5},{5,9},... | collective-permute-start | bytes 1400840 | tf_op jit(solution)/shard_map/ppermute | solution.py:153
  187.1 8.9 %collective-permute-start.46 = (bf16[96,2432]{1,0:T(8,128)(2,1)S(1)}, bf16[96,2432]{1,0:T(8,128)(2,1)S(1)}, u32[]{:S(2)}, u32[]{:S(2)}) collective-permute-start(bf16[96,2432]{1,0:T(8,128)(2,1)S(1)} %get-tuple-element.185), channel_id=1, source_target_pairs={{4,0},{8,4},{12,8},{14,12},{10,14},{6,10},{2,6},{0,2},{5,1},{9,5},... | collective-permute-start | bytes 1400840 | tf_op jit(solution)/shard_map/ppermute | solution.py:159
  196.3 9.4 %collective-permute-start.49 = (bf16[96,2432]{1,0:T(8,128)(2,1)S(1)}, bf16[96,2432]{1,0:T(8,128)(2,1)S(1)}, u32[]{:S(2)}, u32[]{:S(2)}) collective-permute-start(bf16[96,2432]{1,0:T(8,128)(2,1)S(1)} %get-tuple-element.184), channel_id=1, source_target_pairs={{0,4},{4,8},{8,12},{12,14},{14,10},{10,6},{6,2},{2,0},{1,5},{5,9},... | collective-permute-start | bytes 1400840 | tf_op jit(solution)/shard_map/ppermute | solution.py:153
  196.4 10.7 %collective-permute-start.50 = (bf16[96,2432]{1,0:T(8,128)(2,1)S(1)}, bf16[96,2432]{1,0:T(8,128)(2,1)S(1)}, u32[]{:S(2)}, u32[]{:S(2)}) collective-permute-start(bf16[96,2432]{1,0:T(8,128)(2,1)S(1)} %get-tuple-element.183), channel_id=1, source_target_pairs={{4,0},{8,4},{12,8},{14,12},{10,14},{6,10},{2,6},{0,2},{5,1},{9,5},... | collective-permute-start | bytes 1400840 | tf_op jit(solution)/shard_map/ppermute | solution.py:159
  199.3 9.4 %collective-permute-start.39 = (f32[96,768]{1,0:T(8,128)S(1)}, f32[96,768]{1,0:T(8,128)S(1)}, u32[]{:S(2)}, u32[]{:S(2)}) collective-permute-start(f32[96,768]{1,0:T(8,128)S(1)} %get-tuple-element.146), channel_id=1, source_target_pairs={{0,1},{1,0},{2,3},{3,2},{4,5},{5,4},{6,7},{7,6},{8,9},{9,8},{10,11... | collective-permute-start | bytes 884744 | tf_op jit(solution)/shard_map/ppermute | solution.py:171
  199.3 9.3 %collective-permute-start.32 = (bf16[96,768]{1,0:T(8,128)(2,1)S(1)}, bf16[96,768]{1,0:T(8,128)(2,1)S(1)}, u32[]{:S(2)}, u32[]{:S(2)}) collective-permute-start(bf16[96,768]{1,0:T(8,128)(2,1)S(1)} %add_convert_fusion.15), channel_id=1, source_target_pairs={{0,16},{16,0},{1,17},{17,1},{2,18},{18,2},{3,19},{19,3},{4,20},{20... | collective-permute-start | bytes 442376 | tf_op jit(solution)/shard_map/ppermute | solution.py:171
  201.1 13.8 %collective-permute-start.52 = (bf16[96,2432]{1,0:T(8,128)(2,1)S(1)}, bf16[96,2432]{1,0:T(8,128)(2,1)S(1)}, u32[]{:S(2)}, u32[]{:S(2)}) collective-permute-start(bf16[96,2432]{1,0:T(8,128)(2,1)S(1)} %add_convert_fusion.3), channel_id=1, source_target_pairs={{0,4},{4,8},{8,12},{12,14},{14,10},{10,6},{6,2},{2,0},{1,5},{5,9},... | collective-permute-start | bytes 1400840 | tf_op jit(solution)/shard_map/ppermute | solution.py:153
  207.2 8.6 %collective-permute-start.51 = (bf16[96,2432]{1,0:T(8,128)(2,1)S(1)}, bf16[96,2432]{1,0:T(8,128)(2,1)S(1)}, u32[]{:S(2)}, u32[]{:S(2)}) collective-permute-start(bf16[96,2432]{1,0:T(8,128)(2,1)S(1)} %add_convert_fusion), channel_id=1, source_target_pairs={{4,0},{8,4},{12,8},{14,12},{10,14},{6,10},{2,6},{0,2},{5,1},{9,5},... | collective-permute-start | bytes 1400840 | tf_op jit(solution)/shard_map/ppermute | solution.py:159
  208.7 7.6 %collective-permute-start.40 = (bf16[96,768]{1,0:T(8,128)(2,1)S(1)}, bf16[96,768]{1,0:T(8,128)(2,1)S(1)}, u32[]{:S(2)}, u32[]{:S(2)}) collective-permute-start(bf16[96,768]{1,0:T(8,128)(2,1)S(1)} %add_convert_fusion.11), channel_id=1, source_target_pairs={{0,16},{16,0},{1,17},{17,1},{2,18},{18,2},{3,19},{19,3},{4,20},{20... | collective-permute-start | bytes 442376 | tf_op jit(solution)/shard_map/ppermute | solution.py:171
  216.3 2.1 collective-permute-start.54
  216.5 13.7 %collective-permute-start.53 = (bf16[96,2304]{1,0:T(8,128)(2,1)S(1)}, bf16[96,2304]{1,0:T(8,128)(2,1)S(1)}, u32[]{:S(2)}, u32[]{:S(2)}) collective-permute-start(bf16[96,2304]{1,0:T(8,128)(2,1)S(1)} %slice.91), channel_id=1, source_target_pairs={{0,16},{16,0},{1,17},{17,1},{2,18},{18,2},{3,19},{19,3},{4,20},{20... | collective-permute-start | bytes 1327112 | tf_op jit(solution)/shard_map/ppermute | solution.py:171
  218.4 11.8 %collective-permute-start.55 = (f32[96,128]{1,0:T(8,128)S(1)}, f32[96,128]{1,0:T(8,128)S(1)}, u32[]{:S(2)}, u32[]{:S(2)}) collective-permute-start(f32[96,128]{1,0:T(8,128)S(1)} %get-tuple-element.205), channel_id=1, source_target_pairs={{0,16},{16,0},{1,17},{17,1},{2,18},{18,2},{3,19},{19,3},{4,20},{20... | collective-permute-start | bytes 147464 | tf_op jit(solution)/shard_map/ppermute | solution.py:171
  (8 other events, 10.6 us)

commit v5 on v4

--- a/solution.py
+++ b/solution.py
@@ -205,8 +205,8 @@
 
 
 def pack_kernel(pipe_ref, *refs):
-    sources, (kept_ref, sent_ref) = refs[:6], refs[6:8]
-    held, marks = refs[8:14], refs[14]
+    sources, (kept_ref, sent_ref) = refs[:5], refs[5:7]
+    held, marks = refs[7:12], refs[12]
     copies = [
         pltpu.make_async_copy(source, target, marks.at[i])
         for i, (source, target) in enumerate(zip(sources, held))
@@ -217,8 +217,10 @@
         copy.wait()
     qkv_ref, out_ref, fc_ref, proj_ref = held[:4]
     depth = qkv_ref.shape[0]
-    rows = [held[4][...]]
-    long_bias = held[5][...]
+    line = held[4][...]
+    rows = [line[:, i * depth : (i + 1) * depth] for i in range(5)]
+    rows.append(jnp.zeros((3, depth), F32))
+    long_bias = line[:, 5 * depth :]
     qkv_width, out_width = qkv_ref.shape[1] // 2, out_ref.shape[1] // 2
     hidden = fc_ref.shape[1] // 2
     start = qkv_width + out_width
@@ -691,8 +693,9 @@
     ahead_steps = count // 2
 
     pipe_word = pipe.astype(jnp.int32).reshape(1)
-    vectors = jnp.concatenate([ln1_gain, ln1_shift, ln2_gain, ln2_shift, branch_bias], axis=0)
-    vectors = jnp.pad(vectors.astype(F32), ((0, 3), (0, 0)))
+    line = jnp.concatenate(
+        [ln1_gain, ln1_shift, ln2_gain, ln2_shift, branch_bias, qkv_bias, fc_bias], axis=1
+    ).astype(F32)
     kept_part, sent_part = pack_call(
         pipe_word,
         (
@@ -700,8 +703,7 @@
             jnp.transpose(out_weight[0]),
             fc_weight[0],
             jnp.transpose(proj_weight[0]),
-            vectors,
-            jnp.concatenate([qkv_bias, fc_bias], axis=1).astype(F32),
+            line,
         ),
     )
     first_whole, second_whole = blank_call(sent_part, count), blank_call(kept_part, count)

time: 232 us -> 232 us (level)
  no operation moved by 1% of the time
where the time goes in v5:
time: 232 us; the launch traced here: 231 us
  waiting for transfers between devices  105 us (45%)
  starting transfers between devices  51.9 us (22%)
  local copies, waits for them, and re-layouts  32.7 us (14%)
  Pallas kernels  32.6 us (14%)
  other arithmetic  7.63 us (3%)
    ppermute x7, waiting for transfers between devices, advance(): front = lax.ppermute(own, 'dp', self.ahead)  33.9 us
    ppermute x7, waiting for transfers between devices, advance(): self.front = lax.ppermute(front, 'dp', self.ahead)  31.1 us
    ppermute x28, waiting for transfers between devices, swap(): return lax.ppermute(block, axis, [(0, 1), (1, 0)])  29.1 us
    ppermute x28, starting transfers between devices, swap(): return lax.ppermute(block, axis, [(0, 1), (1, 0)])  20.7 us
    pallas_call x4, Pallas kernels, backward_call(): pl.pallas_call(functools.partial(backward_kernel, heads), out_shape=outs,...  15 us
    dynamic_update_slice x14, local copies, waits for them, and re-layouts, put(): lax.dynamic_update_slice(self.whole, block, (owner * self.depth, 0))  14 us
    ppermute x7, starting transfers between devices, advance(): back = lax.ppermute(own, 'dp', self.behind)  12 us
    ppermute x7, starting transfers between devices, advance(): self.front = lax.ppermute(front, 'dp', self.ahead)  10.1 us
  transfers between devices with their start and end apart: 56, of which 27 were waited for; matrix products, arithmetic and copies ran while one was open for 13% of the time, Pallas kernels for 13%

profile of v5, /device:TPU:0, one launch (start us, length us, event | category | flops | bytes accessed | tf_op | source)
XLA Modules:
  0.0 231.1 jit_solution(1408851673176275466)
XLA Ops:
  6.2 3.0 %collective-permute-start.1 = (bf16[96,2432]{1,0:T(8,128)(2,1)S(1)}, bf16[96,2432]{1,0:T(8,128)(2,1)S(1)}, u32[]{:S(2)}, u32[]{:S(2)}) collective-permute-start(bf16[96,2432]{1,0:T(8,128)(2,1)S(1)} %get-tuple-element.94.like_ref), channel_id=1, source_target_pairs={{0,16},{16,0},{1,17},{17,1},{2,18},{18,2},{3,19},{19,3},{4,20},{20... | collective-permute-start | bytes 1400840 | tf_op jit(solution)/shard_map/ppermute | solution.py:171
  10.3 1.8 copy-done
  12.2 1.8 copy-done.3
  14.0 5.9 %collective-permute-done.1 = bf16[96,2432]{1,0:T(8,128)(2,1)S(1)} collective-permute-done((bf16[96,2432]{1,0:T(8,128)(2,1)S(1)}, bf16[96,2432]{1,0:T(8,128)(2,1)S(1)}, u32[]{:S(2)}, u32[]{:S(2)}) %collective-permute-start.1) | collective-permute-done | bytes 466976 | tf_op jit(solution)/shard_map/ppermute | solution.py:171
  19.9 1.4 constant_dynamic-update-slice_fusion.7
  21.3 1.8 collective-permute-start.2
  23.4 1.8 collective-permute-start.6
  26.0 1.4 multiply_sine_fusion.1
  31.5 2.1 concatenate.78.lower_ref
  35.3 1.8 collective-permute-done.3
  37.1 1.6 collective-permute-start.4
  39.1 6.2 %collective-permute-done.6 = bf16[96,2432]{1,0:T(8,128)(2,1)} collective-permute-done((bf16[96,2432]{1,0:T(8,128)(2,1)}, bf16[96,2432]{1,0:T(8,128)(2,1)}, u32[]{:S(2)}, u32[]{:S(2)}) %collective-permute-start.6) | collective-permute-done | bytes 466976 | tf_op jit(solution)/shard_map/ppermute | solution.py:114
  45.3 1.8 collective-permute-done.7
  47.1 1.6 collective-permute-start.10
  49.1 1.9 constant_dynamic-update-slice_fusion.14
  51.0 1.8 constant_dynamic-update-slice_fusion.6
  52.8 1.8 constant_dynamic-update-slice_fusion.13
  54.6 1.8 constant_dynamic-update-slice_fusion.5
  57.0 1.6 collective-permute-start.8
  58.6 6.6 %collective-permute-done.10 = bf16[96,2432]{1,0:T(8,128)(2,1)S(1)} collective-permute-done((bf16[96,2432]{1,0:T(8,128)(2,1)}, bf16[96,2432]{1,0:T(8,128)(2,1)S(1)}, u32[]{:S(2)}, u32[]{:S(2)}) %collective-permute-start.10) | collective-permute-done | bytes 466976 | tf_op jit(solution)/shard_map/ppermute | solution.py:114
  65.2 1.7 collective-permute-start.9
  70.5 4.7 %collective-permute-done.8 = bf16[96,2432]{1,0:T(8,128)(2,1)S(1)} collective-permute-done((bf16[96,2432]{1,0:T(8,128)(2,1)S(1)}, bf16[96,2432]{1,0:T(8,128)(2,1)S(1)}, u32[]{:S(2)}, u32[]{:S(2)}) %collective-permute-start.8) | collective-permute-done | bytes 466976 | tf_op jit(solution)/shard_map/ppermute | solution.py:114
  75.2 1.7 collective-permute-start.20
  77.8 5.7 %collective-permute-done.19 = bf16[96,2432]{1,0:T(8,128)(2,1)S(1)} collective-permute-done((bf16[96,2432]{1,0:T(8,128)(2,1)S(1)}, bf16[96,2432]{1,0:T(8,128)(2,1)S(1)}, u32[]{:S(2)}, u32[]{:S(2)}) %collective-permute-start.19) | collective-permute-done | bytes 466976 | tf_op jit(solution)/shard_map/ppermute | solution.py:114
  83.5 1.5 collective-permute-start.12
  87.1 7.3 %collective-permute-done.12 = bf16[96,2432]{1,0:T(8,128)(2,1)S(1)} collective-permute-done((bf16[96,2432]{1,0:T(8,128)(2,1)S(1)}, bf16[96,2432]{1,0:T(8,128)(2,1)S(1)}, u32[]{:S(2)}, u32[]{:S(2)}) %collective-permute-start.12) | collective-permute-done | bytes 466976 | tf_op jit(solution)/shard_map/ppermute | solution.py:114
  96.4 2.1 copy-done.1
  98.4 2.2 forward.4
  100.8 2.3 forward.5
  103.7 1.6 collective-permute-start.14
  106.5 4.0 %collective-permute-done.14 = bf16[96,768]{1,0:T(8,128)(2,1)S(1)} collective-permute-done((bf16[96,768]{1,0:T(8,128)(2,1)S(1)}, bf16[96,768]{1,0:T(8,128)(2,1)S(1)}, u32[]{:S(2)}, u32[]{:S(2)}) %collective-permute-start.14) | collective-permute-done | bytes 147488 | tf_op jit(solution)/shard_map/ppermute | solution.py:171
  110.5 2.2 collective-permute-done.17
  114.3 2.3 forward.7
  116.8 2.2 forward.6
  119.5 3.7 %backward.4 = (f32[96,768]{1,0:T(8,128)S(1)}, f32[96,768]{1,0:T(8,128)S(1)}, bf16[192,640]{1,0:T(8,128)(2,1)S(1)}, bf16[192,768]{1,0:T(8,128)(2,1)S(1)}, f32[8,768]{1,0:T(8,128)S(1)}) custom-call(bf16[96,768]{1,0:T(8,128)(2,1)S(1)} %get-tuple-element.199.own_ref.refs_2_, bf16[96,768]{1,0:T(8,128)(2,1)S(1)} %collective-permute-done.27.far_ref.refs_3_, ...), custom_call_target="tpu_custom_call" | custom-call | flops 5000000000 | bytes 10000000 | tf_op jit(solution)/shard_map/backward/pallas_call | solution.py:585
  123.4 3.9 %backward.6 = (f32[96,768]{1,0:T(8,128)S(1)}, f32[96,768]{1,0:T(8,128)S(1)}, bf16[192,640]{1,0:T(8,128)(2,1)S(1)}, bf16[192,768]{1,0:T(8,128)(2,1)S(1)}, f32[8,768]{1,0:T(8,128)S(1)}) custom-call(bf16[96,768]{1,0:T(8,128)(2,1)S(1)} %get-tuple-element.200.own_ref.refs_11_, bf16[96,768]{1,0:T(8,128)(2,1)S(1)} %collective-permute-done.33.far_ref.refs_12_, ...), custom_call_target="tpu_custom_call" | custom-call | flops 5000000000 | bytes 10000000 | tf_op jit(solution)/shard_map/backward/pallas_call | solution.py:585
  127.8 1.6 collective-permute-start.26
  130.1 1.6 collective-permute-start.29
  132.3 3.1 %weights.2 = bf16[768,2432]{1,0:T(8,128)(2,1)S(1)} custom-call(bf16[192,3200]{1,0:T(8,128)(2,1)S(1)} %get-tuple-element.121.low_ref.refs_0_.refs_1_.refs_6_.refs_7_, bf16[192,3200]{1,0:T(8,128)(2,1)S(1)} %get-tuple-element.121.low_ref.refs_0_.refs_1_.refs_6_.refs_7_, bf16[96,768]{1,0:T(8,128)(2,1)S(1)} %get-tuple-element.199.own_ref.refs_2_, ...), custom_call_target="tpu_custom_call" | custom-call | flops 8000000000 | bytes 10000000 | tf_op jit(solution)/shard_map/weights/pallas_call | solution.py:626
  136.4 4.5 %collective-permute-done.29 = bf16[96,768]{1,0:T(8,128)(2,1)S(1)} collective-permute-done((bf16[96,768]{1,0:T(8,128)(2,1)S(1)}, bf16[96,768]{1,0:T(8,128)(2,1)S(1)}, u32[]{:S(2)}, u32[]{:S(2)}) %collective-permute-start.29) | collective-permute-done | bytes 147488 | tf_op jit(solution)/shard_map/ppermute | solution.py:171
  140.9 1.5 collective-permute-start.37
  144.8 3.7 %backward.5 = (f32[96,768]{1,0:T(8,128)S(1)}, f32[96,768]{1,0:T(8,128)S(1)}, bf16[192,640]{1,0:T(8,128)(2,1)S(1)}, bf16[192,768]{1,0:T(8,128)(2,1)S(1)}, f32[8,768]{1,0:T(8,128)S(1)}) custom-call(bf16[96,768]{1,0:T(8,128)(2,1)S(1)} %get-tuple-element.197.own_ref.refs_2_, bf16[96,768]{1,0:T(8,128)(2,1)S(1)} %collective-permute-done.30.far_ref.refs_3_, ...), custom_call_target="tpu_custom_call" | custom-call | flops 5000000000 | bytes 10000000 | tf_op jit(solution)/shard_map/backward/pallas_call | solution.py:585
  148.8 3.3 %collective-permute-done.37 = bf16[96,2432]{1,0:T(8,128)(2,1)S(1)} collective-permute-done((bf16[96,2432]{1,0:T(8,128)(2,1)S(1)}, bf16[96,2432]{1,0:T(8,128)(2,1)S(1)}, u32[]{:S(2)}, u32[]{:S(2)}) %collective-permute-start.37) | collective-permute-done | bytes 466976 | tf_op jit(solution)/shard_map/ppermute | solution.py:159
  152.3 1.6 collective-permute-start.44
  154.4 3.7 %backward.7 = (f32[96,768]{1,0:T(8,128)S(1)}, f32[96,768]{1,0:T(8,128)S(1)}, bf16[192,640]{1,0:T(8,128)(2,1)S(1)}, bf16[192,768]{1,0:T(8,128)(2,1)S(1)}, f32[8,768]{1,0:T(8,128)S(1)}) custom-call(bf16[96,768]{1,0:T(8,128)(2,1)S(1)} %get-tuple-element.142.own_ref.refs_11_, bf16[96,768]{1,0:T(8,128)(2,1)S(1)} %collective-permute-done.38.far_ref.refs_12_, ...), custom_call_target="tpu_custom_call" | custom-call | flops 5000000000 | bytes 10000000 | tf_op jit(solution)/shard_map/backward/pallas_call | solution.py:585
  158.1 3.1 %weights.3 = bf16[768,2432]{1,0:T(8,128)(2,1)S(1)} custom-call(bf16[192,3200]{1,0:T(8,128)(2,1)S(1)} %get-tuple-element.125.low_ref.refs_0_.refs_1_.refs_6_.refs_7_, bf16[192,3200]{1,0:T(8,128)(2,1)S(1)} %get-tuple-element.125.low_ref.refs_0_.refs_1_.refs_6_.refs_7_, bf16[96,768]{1,0:T(8,128)(2,1)S(1)} %get-tuple-element.197.own_ref.refs_2_, ...), custom_call_target="tpu_custom_call" | custom-call | flops 8000000000 | bytes 10000000 | tf_op jit(solution)/shard_map/weights/pallas_call | solution.py:626
  162.2 4.3 %collective-permute-done.43 = bf16[96,2432]{1,0:T(8,128)(2,1)S(1)} collective-permute-done((bf16[96,2432]{1,0:T(8,128)(2,1)S(1)}, bf16[96,2432]{1,0:T(8,128)(2,1)S(1)}, u32[]{:S(2)}, u32[]{:S(2)}) %collective-permute-start.43) | collective-permute-done | bytes 466976 | tf_op jit(solution)/shard_map/ppermute | solution.py:153
  166.5 1.7 collective-permute-start.42
  168.8 7.7 %collective-permute-done.41 = bf16[96,2432]{1,0:T(8,128)(2,1)S(1)} collective-permute-done((bf16[96,2432]{1,0:T(8,128)(2,1)S(1)}, bf16[96,2432]{1,0:T(8,128)(2,1)S(1)}, u32[]{:S(2)}, u32[]{:S(2)}) %collective-permute-start.41) | collective-permute-done | bytes 466976 | tf_op jit(solution)/shard_map/ppermute | solution.py:153
  176.5 1.7 collective-permute-start.48
  178.9 7.6 %collective-permute-done.47 = bf16[96,2432]{1,0:T(8,128)(2,1)S(1)} collective-permute-done((bf16[96,2432]{1,0:T(8,128)(2,1)S(1)}, bf16[96,2432]{1,0:T(8,128)(2,1)S(1)}, u32[]{:S(2)}, u32[]{:S(2)}) %collective-permute-start.47) | collective-permute-done | bytes 466976 | tf_op jit(solution)/shard_map/ppermute | solution.py:153
  186.5 1.7 collective-permute-start.46
  188.4 5.5 %collective-permute-done.45 = bf16[96,2432]{1,0:T(8,128)(2,1)S(1)} collective-permute-done((bf16[96,2432]{1,0:T(8,128)(2,1)S(1)}, bf16[96,2432]{1,0:T(8,128)(2,1)S(1)}, u32[]{:S(2)}, u32[]{:S(2)}) %collective-permute-start.45) | collective-permute-done | bytes 466976 | tf_op jit(solution)/shard_map/ppermute | solution.py:153
  193.8 1.6 collective-permute-done.46
  195.8 2.2 collective-permute-start.50
  198.9 1.6 collective-permute-start.32
  200.5 4.9 %collective-permute-done.49 = bf16[96,2432]{1,0:T(8,128)(2,1)S(1)} collective-permute-done((bf16[96,2432]{1,0:T(8,128)(2,1)S(1)}, bf16[96,2432]{1,0:T(8,128)(2,1)S(1)}, u32[]{:S(2)}, u32[]{:S(2)}) %collective-permute-start.49) | collective-permute-done | bytes 466976 | tf_op jit(solution)/shard_map/ppermute | solution.py:153
  206.6 1.6 collective-permute-start.51
  208.4 2.2 collective-permute-start.40
  210.6 3.9 %collective-permute-done.52 = bf16[96,2432]{1,0:T(8,128)(2,1)S(1)} collective-permute-done((bf16[96,2432]{1,0:T(8,128)(2,1)S(1)}, bf16[96,2432]{1,0:T(8,128)(2,1)S(1)}, u32[]{:S(2)}, u32[]{:S(2)}) %collective-permute-start.52) | collective-permute-done | bytes 466976 | tf_op jit(solution)/shard_map/ppermute | solution.py:153
  215.9 1.8 collective-permute-start.53
  217.7 1.1 collective-permute-start.55
  219.7 9.9 %collective-permute-done.55.came_small_ref = f32[96,128]{1,0:T(8,128)S(1)} collective-permute-done((f32[96,128]{1,0:T(8,128)S(1)}, f32[96,128]{1,0:T(8,128)S(1)}, u32[]{:S(2)}, u32[]{:S(2)}) %collective-permute-start.55) | collective-permute-done | bytes 49184 | tf_op jit(solution)/shard_map/ppermute | solution.py:171
  229.6 1.5 unpack.1
  (174 shorter events, 40.6 us)
Async XLA Ops:
  6.2 13.7 %collective-permute-start.1 = (bf16[96,2432]{1,0:T(8,128)(2,1)S(1)}, bf16[96,2432]{1,0:T(8,128)(2,1)S(1)}, u32[]{:S(2)}, u32[]{:S(2)}) collective-permute-start(bf16[96,2432]{1,0:T(8,128)(2,1)S(1)} %get-tuple-element.94.like_ref), channel_id=1, source_target_pairs={{0,16},{16,0},{1,17},{17,1},{2,18},{18,2},{3,19},{19,3},{4,20},{20... | collective-permute-start | bytes 1400840 | tf_op jit(solution)/shard_map/ppermute | solution.py:171
  10.2 86.2 %collective-permute-start = (bf16[96,768]{1,0:T(8,128)(2,1)S(1)}, bf16[96,768]{1,0:T(8,128)(2,1)S(1)}, u32[]{:S(2)}, u32[]{:S(2)}) collective-permute-start(bf16[96,768]{1,0:T(8,128)(2,1)S(1)} %get-tuple-element.203.own_ref), channel_id=1, source_target_pairs={{0,1},{1,0},{2,3},{3,2},{4,5},{5,4},{6,7},{7,6},{8,9},{9,8},{10,11... | collective-permute-start | bytes 442376 | tf_op jit(solution)/shard_map/ppermute | solution.py:171
  12.1 13.3 %copy-start.15 = (s32[2,1,3]{2,1,0:T(1,128)S(1)}, s32[2,1,3]{2,1,0:T(1,128)}, u32[]{:S(2)}) copy-start(s32[2,1,3]{2,1,0:T(1,128)} %param.15) | copy-start | bytes 76
  21.3 13.9 %collective-permute-start.2 = (bf16[96,2432]{1,0:T(8,128)(2,1)}, bf16[96,2432]{1,0:T(8,128)(2,1)}, u32[]{:S(2)}, u32[]{:S(2)}) collective-permute-start(bf16[96,2432]{1,0:T(8,128)(2,1)} %get-tuple-element.196), channel_id=1, source_target_pairs={{0,4},{4,8},{8,12},{12,14},{14,10},{10,6},{6,2},{2,0},{1,5},{5,9},... | collective-permute-start | bytes 1400840 | tf_op jit(solution)/shard_map/ppermute | solution.py:114
  23.1 13.9 %collective-permute-start.3 = (bf16[96,2432]{1,0:T(8,128)(2,1)}, bf16[96,2432]{1,0:T(8,128)(2,1)}, u32[]{:S(2)}, u32[]{:S(2)}) collective-permute-start(bf16[96,2432]{1,0:T(8,128)(2,1)} %get-tuple-element.196), channel_id=1, source_target_pairs={{4,0},{8,4},{12,8},{14,12},{10,14},{6,10},{2,6},{0,2},{5,1},{9,5},... | collective-permute-start | bytes 1400840 | tf_op jit(solution)/shard_map/ppermute | solution.py:117
  23.4 21.9 %collective-permute-start.6 = (bf16[96,2432]{1,0:T(8,128)(2,1)}, bf16[96,2432]{1,0:T(8,128)(2,1)}, u32[]{:S(2)}, u32[]{:S(2)}) collective-permute-start(bf16[96,2432]{1,0:T(8,128)(2,1)} %get-tuple-element.178), channel_id=1, source_target_pairs={{0,4},{4,8},{8,12},{12,14},{14,10},{10,6},{6,2},{2,0},{1,5},{5,9},... | collective-permute-start | bytes 1400840 | tf_op jit(solution)/shard_map/ppermute | solution.py:114
  25.2 21.9 %collective-permute-start.7 = (bf16[96,2432]{1,0:T(8,128)(2,1)}, bf16[96,2432]{1,0:T(8,128)(2,1)}, u32[]{:S(2)}, u32[]{:S(2)}) collective-permute-start(bf16[96,2432]{1,0:T(8,128)(2,1)} %get-tuple-element.178), channel_id=1, source_target_pairs={{4,0},{8,4},{12,8},{14,12},{10,14},{6,10},{2,6},{0,2},{5,1},{9,5},... | collective-permute-start | bytes 1400840 | tf_op jit(solution)/shard_map/ppermute | solution.py:117
  27.4 3.3 %copy-start.9 = (f32[192,48]{1,0:T(8,128)}, f32[192,48]{1,0:T(8,128)S(1)}, u32[]{:S(2)}) copy-start(f32[192,48]{1,0:T(8,128)S(1)} %broadcast.137) | copy-start | bytes 110596
  27.4 3.2 %copy-start.10 = (f32[192,64]{1,0:T(8,128)}, f32[192,64]{1,0:T(8,128)S(1)}, u32[]{:S(2)}) copy-start(f32[192,64]{1,0:T(8,128)S(1)} %broadcast.138) | copy-start | bytes 147460
  37.1 19.4 %collective-permute-start.4 = (bf16[96,2432]{1,0:T(8,128)(2,1)}, bf16[96,2432]{1,0:T(8,128)(2,1)S(1)}, u32[]{:S(2)}, u32[]{:S(2)}) collective-permute-start(bf16[96,2432]{1,0:T(8,128)(2,1)} %collective-permute-done.2), channel_id=1, source_target_pairs={{0,4},{4,8},{8,12},{12,14},{14,10},{10,6},{6,2},{2,0},{1,5},{5,9},... | collective-permute-start | bytes 1400840 | tf_op jit(solution)/shard_map/ppermute | solution.py:114
  38.7 18.3 %collective-permute-start.5 = (bf16[96,2432]{1,0:T(8,128)(2,1)}, bf16[96,2432]{1,0:T(8,128)(2,1)S(1)}, u32[]{:S(2)}, u32[]{:S(2)}) collective-permute-start(bf16[96,2432]{1,0:T(8,128)(2,1)} %collective-permute-done.3), channel_id=1, source_target_pairs={{4,0},{8,4},{12,8},{14,12},{10,14},{6,10},{2,6},{0,2},{5,1},{9,5},... | collective-permute-start | bytes 1400840 | tf_op jit(solution)/shard_map/ppermute | solution.py:117
  47.1 18.1 %collective-permute-start.10 = (bf16[96,2432]{1,0:T(8,128)(2,1)}, bf16[96,2432]{1,0:T(8,128)(2,1)S(1)}, u32[]{:S(2)}, u32[]{:S(2)}) collective-permute-start(bf16[96,2432]{1,0:T(8,128)(2,1)} %collective-permute-done.6), channel_id=1, source_target_pairs={{0,4},{4,8},{8,12},{12,14},{14,10},{10,6},{6,2},{2,0},{1,5},{5,9},... | collective-permute-start | bytes 1400840 | tf_op jit(solution)/shard_map/ppermute | solution.py:114
  48.7 18.3 %collective-permute-start.11 = (bf16[96,2432]{1,0:T(8,128)(2,1)}, bf16[96,2432]{1,0:T(8,128)(2,1)S(1)}, u32[]{:S(2)}, u32[]{:S(2)}) collective-permute-start(bf16[96,2432]{1,0:T(8,128)(2,1)} %collective-permute-done.7), channel_id=1, source_target_pairs={{4,0},{8,4},{12,8},{14,12},{10,14},{6,10},{2,6},{0,2},{5,1},{9,5},... | collective-permute-start | bytes 1400840 | tf_op jit(solution)/shard_map/ppermute | solution.py:117
  56.5 44.3 %collective-permute-start.15 = (bf16[96,768]{1,0:T(8,128)(2,1)S(1)}, bf16[96,768]{1,0:T(8,128)(2,1)S(1)}, u32[]{:S(2)}, u32[]{:S(2)}) collective-permute-start(bf16[96,768]{1,0:T(8,128)(2,1)S(1)} %get-tuple-element.204.own_ref), channel_id=1, source_target_pairs={{0,1},{1,0},{2,3},{3,2},{4,5},{5,4},{6,7},{7,6},{8,9},{9,8},{10,11... | collective-permute-start | bytes 442376 | tf_op jit(solution)/shard_map/ppermute | solution.py:171
  57.0 18.2 %collective-permute-start.8 = (bf16[96,2432]{1,0:T(8,128)(2,1)S(1)}, bf16[96,2432]{1,0:T(8,128)(2,1)S(1)}, u32[]{:S(2)}, u32[]{:S(2)}) collective-permute-start(bf16[96,2432]{1,0:T(8,128)(2,1)S(1)} %collective-permute-done.4), channel_id=1, source_target_pairs={{0,4},{4,8},{8,12},{12,14},{14,10},{10,6},{6,2},{2,0},{1,5},{5,9},... | collective-permute-start | bytes 1400840 | tf_op jit(solution)/shard_map/ppermute | solution.py:114
  65.2 20.6 %collective-permute-start.9 = (bf16[96,2432]{1,0:T(8,128)(2,1)S(1)}, bf16[96,2432]{1,0:T(8,128)(2,1)S(1)}, u32[]{:S(2)}, u32[]{:S(2)}) collective-permute-start(bf16[96,2432]{1,0:T(8,128)(2,1)S(1)} %collective-permute-done.5), channel_id=1, source_target_pairs={{4,0},{8,4},{12,8},{14,12},{10,14},{6,10},{2,6},{0,2},{5,1},{9,5},... | collective-permute-start | bytes 1400840 | tf_op jit(solution)/shard_map/ppermute | solution.py:117
  66.9 16.5 %collective-permute-start.19 = (bf16[96,2432]{1,0:T(8,128)(2,1)S(1)}, bf16[96,2432]{1,0:T(8,128)(2,1)S(1)}, u32[]{:S(2)}, u32[]{:S(2)}) collective-permute-start(bf16[96,2432]{1,0:T(8,128)(2,1)S(1)} %collective-permute-done.10), channel_id=1, source_target_pairs={{0,4},{4,8},{8,12},{12,14},{14,10},{10,6},{6,2},{2,0},{1,5},{5,9},... | collective-permute-start | bytes 1400840 | tf_op jit(solution)/shard_map/ppermute | solution.py:114
  75.2 10.6 %collective-permute-start.20 = (bf16[96,2432]{1,0:T(8,128)(2,1)S(1)}, bf16[96,2432]{1,0:T(8,128)(2,1)S(1)}, u32[]{:S(2)}, u32[]{:S(2)}) collective-permute-start(bf16[96,2432]{1,0:T(8,128)(2,1)S(1)} %collective-permute-done.11), channel_id=1, source_target_pairs={{4,0},{8,4},{12,8},{14,12},{10,14},{6,10},{2,6},{0,2},{5,1},{9,5},... | collective-permute-start | bytes 1400840 | tf_op jit(solution)/shard_map/ppermute | solution.py:117
  83.5 11.0 %collective-permute-start.12 = (bf16[96,2432]{1,0:T(8,128)(2,1)S(1)}, bf16[96,2432]{1,0:T(8,128)(2,1)S(1)}, u32[]{:S(2)}, u32[]{:S(2)}) collective-permute-start(bf16[96,2432]{1,0:T(8,128)(2,1)S(1)} %collective-permute-done.8), channel_id=1, source_target_pairs={{0,4},{4,8},{8,12},{12,14},{14,10},{10,6},{6,2},{2,0},{1,5},{5,9},... | collective-permute-start | bytes 1400840 | tf_op jit(solution)/shard_map/ppermute | solution.py:114
  85.8 33.7 %collective-permute-start.27 = (bf16[96,768]{1,0:T(8,128)(2,1)S(1)}, bf16[96,768]{1,0:T(8,128)(2,1)S(1)}, u32[]{:S(2)}, u32[]{:S(2)}) collective-permute-start(bf16[96,768]{1,0:T(8,128)(2,1)S(1)} %get-tuple-element.199.own_ref.refs_2_), channel_id=1, source_target_pairs={{0,1},{1,0},{2,3},{3,2},{4,5},{5,4},{6,7},{7,6},{8,9},{9,8},{10,11... | collective-permute-start | bytes 442376 | tf_op jit(solution)/shard_map/ppermute | solution.py:171
  85.8 37.6 %collective-permute-start.33 = (bf16[96,768]{1,0:T(8,128)(2,1)S(1)}, bf16[96,768]{1,0:T(8,128)(2,1)S(1)}, u32[]{:S(2)}, u32[]{:S(2)}) collective-permute-start(bf16[96,768]{1,0:T(8,128)(2,1)S(1)} %get-tuple-element.200.own_ref.refs_11_), channel_id=1, source_target_pairs={{0,1},{1,0},{2,3},{3,2},{4,5},{5,4},{6,7},{7,6},{8,9},{9,8},{10,11... | collective-permute-start | bytes 442376 | tf_op jit(solution)/shard_map/ppermute | solution.py:171
  94.4 18.5 %collective-permute-start.21 = (bf16[96,2432]{1,0:T(8,128)(2,1)S(1)}, bf16[96,2432]{1,0:T(8,128)(2,1)S(1)}, u32[]{:S(2)}, u32[]{:S(2)}) collective-permute-start(bf16[96,2432]{1,0:T(8,128)(2,1)S(1)} %collective-permute-done.20), channel_id=1, source_target_pairs={{4,0},{8,4},{12,8},{14,12},{10,14},{6,10},{2,6},{0,2},{5,1},{9,5},... | collective-permute-start | bytes 1400840 | tf_op jit(solution)/shard_map/ppermute | solution.py:117
  96.4 2.1 copy-start.1
  100.7 3.0 %collective-permute-start.13 = (f32[96,768]{1,0:T(8,128)S(1)}, f32[96,768]{1,0:T(8,128)S(1)}, u32[]{:S(2)}, u32[]{:S(2)}) collective-permute-start(f32[96,768]{1,0:T(8,128)S(1)} %get-tuple-element.109), channel_id=1, source_target_pairs={{0,1},{1,0},{2,3},{3,2},{4,5},{5,4},{6,7},{7,6},{8,9},{9,8},{10,11... | collective-permute-start | bytes 884744 | tf_op jit(solution)/shard_map/ppermute | solution.py:171
  100.8 2.8 %copy-start.4 = (bf16[768,2432]{1,0:T(8,128)(2,1)S(1)}, bf16[768,2432]{1,0:T(8,128)(2,1)}, u32[]{:S(2)}) copy-start(bf16[768,2432]{1,0:T(8,128)(2,1)} %constant_dynamic-update-slice_fusion.2) | copy-start | bytes 11206660
  100.8 11.9 %copy-start.13 = (bf16[2,96,768]{2,1,0:T(8,128)(2,1)S(1)}, bf16[2,96,768]{2,1,0:T(8,128)(2,1)}, u32[]{:S(2)}) copy-start(bf16[2,96,768]{2,1,0:T(8,128)(2,1)} %param.14) | copy-start | bytes 884740
  103.1 2.2 collective-permute-start.16
  103.7 6.8 %collective-permute-start.14 = (bf16[96,768]{1,0:T(8,128)(2,1)S(1)}, bf16[96,768]{1,0:T(8,128)(2,1)S(1)}, u32[]{:S(2)}, u32[]{:S(2)}) collective-permute-start(bf16[96,768]{1,0:T(8,128)(2,1)S(1)} %add_convert_fusion.25), channel_id=1, source_target_pairs={{0,16},{16,0},{1,17},{17,1},{2,18},{18,2},{3,19},{19,3},{4,20},{20... | collective-permute-start | bytes 442376 | tf_op jit(solution)/shard_map/ppermute | solution.py:171
  105.3 7.4 %collective-permute-start.17 = (bf16[96,768]{1,0:T(8,128)(2,1)S(1)}, bf16[96,768]{1,0:T(8,128)(2,1)S(1)}, u32[]{:S(2)}, u32[]{:S(2)}) collective-permute-start(bf16[96,768]{1,0:T(8,128)(2,1)S(1)} %add_convert_fusion.23), channel_id=1, source_target_pairs={{0,16},{16,0},{1,17},{17,1},{2,18},{18,2},{3,19},{19,3},{4,20},{20... | collective-permute-start | bytes 442376 | tf_op jit(solution)/shard_map/ppermute | solution.py:171
  112.8 1.4 collective-permute-start.24
  113.0 3.8 %collective-permute-start.18 = (bf16[96,768]{1,0:T(8,128)(2,1)S(1)}, bf16[96,768]{1,0:T(8,128)(2,1)S(1)}, u32[]{:S(2)}, u32[]{:S(2)}) collective-permute-start(bf16[96,768]{1,0:T(8,128)(2,1)S(1)} %get-tuple-element.201.own_ref), channel_id=1, source_target_pairs={{0,1},{1,0},{2,3},{3,2},{4,5},{5,4},{6,7},{7,6},{8,9},{9,8},{10,11... | collective-permute-start | bytes 442376 | tf_op jit(solution)/shard_map/ppermute | solution.py:171
  116.5 11.3 %collective-permute-start.25 = (f32[96,768]{1,0:T(8,128)S(1)}, f32[96,768]{1,0:T(8,128)S(1)}, u32[]{:S(2)}, u32[]{:S(2)}) collective-permute-start(f32[96,768]{1,0:T(8,128)S(1)} %get-tuple-element.119), channel_id=1, source_target_pairs={{0,1},{1,0},{2,3},{3,2},{4,5},{5,4},{6,7},{7,6},{8,9},{9,8},{10,11... | collective-permute-start | bytes 884744 | tf_op jit(solution)/shard_map/ppermute | solution.py:171
  119.0 10.4 %collective-permute-start.22 = (f32[96,768]{1,0:T(8,128)S(1)}, f32[96,768]{1,0:T(8,128)S(1)}, u32[]{:S(2)}, u32[]{:S(2)}) collective-permute-start(f32[96,768]{1,0:T(8,128)S(1)} %get-tuple-element.116), channel_id=1, source_target_pairs={{0,1},{1,0},{2,3},{3,2},{4,5},{5,4},{6,7},{7,6},{8,9},{9,8},{10,11... | collective-permute-start | bytes 884744 | tf_op jit(solution)/shard_map/ppermute | solution.py:171
  123.2 6.9 %collective-permute-start.28 = (f32[96,768]{1,0:T(8,128)S(1)}, f32[96,768]{1,0:T(8,128)S(1)}, u32[]{:S(2)}, u32[]{:S(2)}) collective-permute-start(f32[96,768]{1,0:T(8,128)S(1)} %get-tuple-element.124), channel_id=1, source_target_pairs={{0,1},{1,0},{2,3},{3,2},{4,5},{5,4},{6,7},{7,6},{8,9},{9,8},{10,11... | collective-permute-start | bytes 884744 | tf_op jit(solution)/shard_map/ppermute | solution.py:171
  127.4 4.3 %collective-permute-start.34 = (f32[96,768]{1,0:T(8,128)S(1)}, f32[96,768]{1,0:T(8,128)S(1)}, u32[]{:S(2)}, u32[]{:S(2)}) collective-permute-start(f32[96,768]{1,0:T(8,128)S(1)} %get-tuple-element.132), channel_id=1, source_target_pairs={{0,1},{1,0},{2,3},{3,2},{4,5},{5,4},{6,7},{7,6},{8,9},{9,8},{10,11... | collective-permute-start | bytes 884744 | tf_op jit(solution)/shard_map/ppermute | solution.py:171
  127.8 15.6 %collective-permute-start.26 = (bf16[96,768]{1,0:T(8,128)(2,1)S(1)}, bf16[96,768]{1,0:T(8,128)(2,1)S(1)}, u32[]{:S(2)}, u32[]{:S(2)}) collective-permute-start(bf16[96,768]{1,0:T(8,128)(2,1)S(1)} %add_convert_fusion.19), channel_id=1, source_target_pairs={{0,16},{16,0},{1,17},{17,1},{2,18},{18,2},{3,19},{19,3},{4,20},{20... | collective-permute-start | bytes 442376 | tf_op jit(solution)/shard_map/ppermute | solution.py:171
  129.5 68.5 %collective-permute-start.23 = (bf16[96,768]{1,0:T(8,128)(2,1)S(1)}, bf16[96,768]{1,0:T(8,128)(2,1)S(1)}, u32[]{:S(2)}, u32[]{:S(2)}) collective-permute-start(bf16[96,768]{1,0:T(8,128)(2,1)S(1)} %add_convert_fusion.21), channel_id=1, source_target_pairs={{0,16},{16,0},{1,17},{17,1},{2,18},{18,2},{3,19},{19,3},{4,20},{20... | collective-permute-start | bytes 442376 | tf_op jit(solution)/shard_map/ppermute | solution.py:171
  130.1 10.8 %collective-permute-start.29 = (bf16[96,768]{1,0:T(8,128)(2,1)S(1)}, bf16[96,768]{1,0:T(8,128)(2,1)S(1)}, u32[]{:S(2)}, u32[]{:S(2)}) collective-permute-start(bf16[96,768]{1,0:T(8,128)(2,1)S(1)} %add_convert_fusion.17), channel_id=1, source_target_pairs={{0,16},{16,0},{1,17},{17,1},{2,18},{18,2},{3,19},{19,3},{4,20},{20... | collective-permute-start | bytes 442376 | tf_op jit(solution)/shard_map/ppermute | solution.py:171
  131.7 11.6 %collective-permute-start.35 = (bf16[96,768]{1,0:T(8,128)(2,1)S(1)}, bf16[96,768]{1,0:T(8,128)(2,1)S(1)}, u32[]{:S(2)}, u32[]{:S(2)}) collective-permute-start(bf16[96,768]{1,0:T(8,128)(2,1)S(1)} %add_convert_fusion.13), channel_id=1, source_target_pairs={{0,16},{16,0},{1,17},{17,1},{2,18},{18,2},{3,19},{19,3},{4,20},{20... | collective-permute-start | bytes 442376 | tf_op jit(solution)/shard_map/ppermute | solution.py:171
  132.3 11.0 %copy-start.14 = (bf16[2,96,768]{2,1,0:T(8,128)(2,1)S(1)}, bf16[2,96,768]{2,1,0:T(8,128)(2,1)}, u32[]{:S(2)}) copy-start(bf16[2,96,768]{2,1,0:T(8,128)(2,1)} %param.27) | copy-start | bytes 884740
  132.3 12.6 %copy-start.2 = (bf16[768,2432]{1,0:T(8,128)(2,1)S(1)}, bf16[768,2432]{1,0:T(8,128)(2,1)}, u32[]{:S(2)}) copy-start(bf16[768,2432]{1,0:T(8,128)(2,1)} %constant_dynamic-update-slice_fusion.8.weight_ref) | copy-start | bytes 11206660
  135.4 13.3 %collective-permute-start.36 = (bf16[96,2432]{1,0:T(8,128)(2,1)S(1)}, bf16[96,2432]{1,0:T(8,128)(2,1)S(1)}, u32[]{:S(2)}, u32[]{:S(2)}) collective-permute-start(bf16[96,2432]{1,0:T(8,128)(2,1)S(1)} %get-tuple-element.194), channel_id=1, source_target_pairs={{0,4},{4,8},{8,12},{12,14},{14,10},{10,6},{6,2},{2,0},{1,5},{5,9},... | collective-permute-start | bytes 1400840 | tf_op jit(solution)/shard_map/ppermute | solution.py:153
  140.9 11.1 %collective-permute-start.37 = (bf16[96,2432]{1,0:T(8,128)(2,1)S(1)}, bf16[96,2432]{1,0:T(8,128)(2,1)S(1)}, u32[]{:S(2)}, u32[]{:S(2)}) collective-permute-start(bf16[96,2432]{1,0:T(8,128)(2,1)S(1)} %get-tuple-element.193), channel_id=1, source_target_pairs={{4,0},{8,4},{12,8},{14,12},{10,14},{6,10},{2,6},{0,2},{5,1},{9,5},... | collective-permute-start | bytes 1400840 | tf_op jit(solution)/shard_map/ppermute | solution.py:159
  143.4 1.4 collective-permute-start.30
  143.5 10.9 %collective-permute-start.38 = (bf16[96,768]{1,0:T(8,128)(2,1)S(1)}, bf16[96,768]{1,0:T(8,128)(2,1)S(1)}, u32[]{:S(2)}, u32[]{:S(2)}) collective-permute-start(bf16[96,768]{1,0:T(8,128)(2,1)S(1)} %get-tuple-element.142.own_ref.refs_11_), channel_id=1, source_target_pairs={{0,1},{1,0},{2,3},{3,2},{4,5},{5,4},{6,7},{7,6},{8,9},{9,8},{10,11... | collective-permute-start | bytes 442376 | tf_op jit(solution)/shard_map/ppermute | solution.py:171
  148.6 50.3 %collective-permute-start.31 = (f32[96,768]{1,0:T(8,128)S(1)}, f32[96,768]{1,0:T(8,128)S(1)}, u32[]{:S(2)}, u32[]{:S(2)}) collective-permute-start(f32[96,768]{1,0:T(8,128)S(1)} %get-tuple-element.128), channel_id=1, source_target_pairs={{0,1},{1,0},{2,3},{3,2},{4,5},{5,4},{6,7},{7,6},{8,9},{9,8},{10,11... | collective-permute-start | bytes 884744 | tf_op jit(solution)/shard_map/ppermute | solution.py:171
  152.3 15.9 %collective-permute-start.44 = (bf16[96,2432]{1,0:T(8,128)(2,1)S(1)}, bf16[96,2432]{1,0:T(8,128)(2,1)S(1)}, u32[]{:S(2)}, u32[]{:S(2)}) collective-permute-start(bf16[96,2432]{1,0:T(8,128)(2,1)S(1)} %get-tuple-element.192), channel_id=1, source_target_pairs={{4,0},{8,4},{12,8},{14,12},{10,14},{6,10},{2,6},{0,2},{5,1},{9,5},... | collective-permute-start | bytes 1400840 | tf_op jit(solution)/shard_map/ppermute | solution.py:159
  153.9 12.6 %collective-permute-start.43 = (bf16[96,2432]{1,0:T(8,128)(2,1)S(1)}, bf16[96,2432]{1,0:T(8,128)(2,1)S(1)}, u32[]{:S(2)}, u32[]{:S(2)}) collective-permute-start(bf16[96,2432]{1,0:T(8,128)(2,1)S(1)} %get-tuple-element.191), channel_id=1, source_target_pairs={{0,4},{4,8},{8,12},{12,14},{14,10},{10,6},{6,2},{2,0},{1,5},{5,9},... | collective-permute-start | bytes 1400840 | tf_op jit(solution)/shard_map/ppermute | solution.py:153
  161.3 15.2 %collective-permute-start.41 = (bf16[96,2432]{1,0:T(8,128)(2,1)S(1)}, bf16[96,2432]{1,0:T(8,128)(2,1)S(1)}, u32[]{:S(2)}, u32[]{:S(2)}) collective-permute-start(bf16[96,2432]{1,0:T(8,128)(2,1)S(1)} %get-tuple-element.190), channel_id=1, source_target_pairs={{0,4},{4,8},{8,12},{12,14},{14,10},{10,6},{6,2},{2,0},{1,5},{5,9},... | collective-permute-start | bytes 1400840 | tf_op jit(solution)/shard_map/ppermute | solution.py:153
  166.5 11.7 %collective-permute-start.42 = (bf16[96,2432]{1,0:T(8,128)(2,1)S(1)}, bf16[96,2432]{1,0:T(8,128)(2,1)S(1)}, u32[]{:S(2)}, u32[]{:S(2)}) collective-permute-start(bf16[96,2432]{1,0:T(8,128)(2,1)S(1)} %get-tuple-element.189), channel_id=1, source_target_pairs={{4,0},{8,4},{12,8},{14,12},{10,14},{6,10},{2,6},{0,2},{5,1},{9,5},... | collective-permute-start | bytes 1400840 | tf_op jit(solution)/shard_map/ppermute | solution.py:159
  168.5 18.0 %collective-permute-start.47 = (bf16[96,2432]{1,0:T(8,128)(2,1)S(1)}, bf16[96,2432]{1,0:T(8,128)(2,1)S(1)}, u32[]{:S(2)}, u32[]{:S(2)}) collective-permute-start(bf16[96,2432]{1,0:T(8,128)(2,1)S(1)} %get-tuple-element.188), channel_id=1, source_target_pairs={{0,4},{4,8},{8,12},{12,14},{14,10},{10,6},{6,2},{2,0},{1,5},{5,9},... | collective-permute-start | bytes 1400840 | tf_op jit(solution)/shard_map/ppermute | solution.py:153
  176.5 11.7 %collective-permute-start.48 = (bf16[96,2432]{1,0:T(8,128)(2,1)S(1)}, bf16[96,2432]{1,0:T(8,128)(2,1)S(1)}, u32[]{:S(2)}, u32[]{:S(2)}) collective-permute-start(bf16[96,2432]{1,0:T(8,128)(2,1)S(1)} %get-tuple-element.187), channel_id=1, source_target_pairs={{4,0},{8,4},{12,8},{14,12},{10,14},{6,10},{2,6},{0,2},{5,1},{9,5},... | collective-permute-start | bytes 1400840 | tf_op jit(solution)/shard_map/ppermute | solution.py:159
  178.5 15.3 %collective-permute-start.45 = (bf16[96,2432]{1,0:T(8,128)(2,1)S(1)}, bf16[96,2432]{1,0:T(8,128)(2,1)S(1)}, u32[]{:S(2)}, u32[]{:S(2)}) collective-permute-start(bf16[96,2432]{1,0:T(8,128)(2,1)S(1)} %get-tuple-element.186), channel_id=1, source_target_pairs={{0,4},{4,8},{8,12},{12,14},{14,10},{10,6},{6,2},{2,0},{1,5},{5,9},... | collective-permute-start | bytes 1400840 | tf_op jit(solution)/shard_map/ppermute | solution.py:153
  186.5 8.9 %collective-permute-start.46 = (bf16[96,2432]{1,0:T(8,128)(2,1)S(1)}, bf16[96,2432]{1,0:T(8,128)(2,1)S(1)}, u32[]{:S(2)}, u32[]{:S(2)}) collective-permute-start(bf16[96,2432]{1,0:T(8,128)(2,1)S(1)} %get-tuple-element.185), channel_id=1, source_target_pairs={{4,0},{8,4},{12,8},{14,12},{10,14},{6,10},{2,6},{0,2},{5,1},{9,5},... | collective-permute-start | bytes 1400840 | tf_op jit(solution)/shard_map/ppermute | solution.py:159
  195.7 9.7 %collective-permute-start.49 = (bf16[96,2432]{1,0:T(8,128)(2,1)S(1)}, bf16[96,2432]{1,0:T(8,128)(2,1)S(1)}, u32[]{:S(2)}, u32[]{:S(2)}) collective-permute-start(bf16[96,2432]{1,0:T(8,128)(2,1)S(1)} %get-tuple-element.184), channel_id=1, source_target_pairs={{0,4},{4,8},{8,12},{12,14},{14,10},{10,6},{6,2},{2,0},{1,5},{5,9},... | collective-permute-start | bytes 1400840 | tf_op jit(solution)/shard_map/ppermute | solution.py:153
  195.8 10.7 %collective-permute-start.50 = (bf16[96,2432]{1,0:T(8,128)(2,1)S(1)}, bf16[96,2432]{1,0:T(8,128)(2,1)S(1)}, u32[]{:S(2)}, u32[]{:S(2)}) collective-permute-start(bf16[96,2432]{1,0:T(8,128)(2,1)S(1)} %get-tuple-element.183), channel_id=1, source_target_pairs={{4,0},{8,4},{12,8},{14,12},{10,14},{6,10},{2,6},{0,2},{5,1},{9,5},... | collective-permute-start | bytes 1400840 | tf_op jit(solution)/shard_map/ppermute | solution.py:159
  198.9 9.5 %collective-permute-start.39 = (f32[96,768]{1,0:T(8,128)S(1)}, f32[96,768]{1,0:T(8,128)S(1)}, u32[]{:S(2)}, u32[]{:S(2)}) collective-permute-start(f32[96,768]{1,0:T(8,128)S(1)} %get-tuple-element.146), channel_id=1, source_target_pairs={{0,1},{1,0},{2,3},{3,2},{4,5},{5,4},{6,7},{7,6},{8,9},{9,8},{10,11... | collective-permute-start | bytes 884744 | tf_op jit(solution)/shard_map/ppermute | solution.py:171
  198.9 9.4 %collective-permute-start.32 = (bf16[96,768]{1,0:T(8,128)(2,1)S(1)}, bf16[96,768]{1,0:T(8,128)(2,1)S(1)}, u32[]{:S(2)}, u32[]{:S(2)}) collective-permute-start(bf16[96,768]{1,0:T(8,128)(2,1)S(1)} %add_convert_fusion.15), channel_id=1, source_target_pairs={{0,16},{16,0},{1,17},{17,1},{2,18},{18,2},{3,19},{19,3},{4,20},{20... | collective-permute-start | bytes 442376 | tf_op jit(solution)/shard_map/ppermute | solution.py:171
  200.5 14.0 %collective-permute-start.52 = (bf16[96,2432]{1,0:T(8,128)(2,1)S(1)}, bf16[96,2432]{1,0:T(8,128)(2,1)S(1)}, u32[]{:S(2)}, u32[]{:S(2)}) collective-permute-start(bf16[96,2432]{1,0:T(8,128)(2,1)S(1)} %add_convert_fusion.3), channel_id=1, source_target_pairs={{0,4},{4,8},{8,12},{12,14},{14,10},{10,6},{6,2},{2,0},{1,5},{5,9},... | collective-permute-start | bytes 1400840 | tf_op jit(solution)/shard_map/ppermute | solution.py:153
  206.6 8.6 %collective-permute-start.51 = (bf16[96,2432]{1,0:T(8,128)(2,1)S(1)}, bf16[96,2432]{1,0:T(8,128)(2,1)S(1)}, u32[]{:S(2)}, u32[]{:S(2)}) collective-permute-start(bf16[96,2432]{1,0:T(8,128)(2,1)S(1)} %add_convert_fusion), channel_id=1, source_target_pairs={{4,0},{8,4},{12,8},{14,12},{10,14},{6,10},{2,6},{0,2},{5,1},{9,5},... | collective-permute-start | bytes 1400840 | tf_op jit(solution)/shard_map/ppermute | solution.py:159
  208.4 7.4 %collective-permute-start.40 = (bf16[96,768]{1,0:T(8,128)(2,1)S(1)}, bf16[96,768]{1,0:T(8,128)(2,1)S(1)}, u32[]{:S(2)}, u32[]{:S(2)}) collective-permute-start(bf16[96,768]{1,0:T(8,128)(2,1)S(1)} %add_convert_fusion.11), channel_id=1, source_target_pairs={{0,16},{16,0},{1,17},{17,1},{2,18},{18,2},{3,19},{19,3},{4,20},{20... | collective-permute-start | bytes 442376 | tf_op jit(solution)/shard_map/ppermute | solution.py:171
  215.7 2.0 collective-permute-start.54
  215.9 13.7 %collective-permute-start.53 = (bf16[96,2304]{1,0:T(8,128)(2,1)S(1)}, bf16[96,2304]{1,0:T(8,128)(2,1)S(1)}, u32[]{:S(2)}, u32[]{:S(2)}) collective-permute-start(bf16[96,2304]{1,0:T(8,128)(2,1)S(1)} %slice.91), channel_id=1, source_target_pairs={{0,16},{16,0},{1,17},{17,1},{2,18},{18,2},{3,19},{19,3},{4,20},{20... | collective-permute-start | bytes 1327112 | tf_op jit(solution)/shard_map/ppermute | solution.py:171
  217.7 11.9 %collective-permute-start.55 = (f32[96,128]{1,0:T(8,128)S(1)}, f32[96,128]{1,0:T(8,128)S(1)}, u32[]{:S(2)}, u32[]{:S(2)}) collective-permute-start(f32[96,128]{1,0:T(8,128)S(1)} %get-tuple-element.205), channel_id=1, source_target_pairs={{0,16},{16,0},{1,17},{17,1},{2,18},{18,2},{3,19},{19,3},{4,20},{20... | collective-permute-start | bytes 147464 | tf_op jit(solution)/shard_map/ppermute | solution.py:171
  (8 other events, 10.6 us)
